TPU v7x, 32 devices: a whole 2x2x4 slice. The times are simulated.
32 devices in a mesh: seq: 8 (over z, x), wa: 4 (over y, core).
Axes of the slice: x: 2, y: 2, z: 4, core: 2. Of those that a mesh axis runs over, the one named last changes fastest.
Arguments:
- inputs: bfloat16 [2, 4096, 768], P(None, 'seq', 'wa'), may hold values from -6 to 6
- targets: bfloat16 [2, 4096, 768], P(None, 'seq'), may hold values from -6 to 6
- lengths: int32 [2], replicated, may hold values from 2048 to 4096, as said below
- positions: int32 [2, 4096], P(None, 'seq'), may hold values from 0 to 8190, as said below
- ema_decay: float32 [768, 16], P('wa'), may hold values from 0 to 1
- ema_feed: float32 [768, 16], P('wa'), may hold values from -4 to 4
- ema_read: float32 [768, 16], P('wa'), may hold values from -1.5 to 1.5
- ema_skip: float32 [768], P('wa'), may hold values from -3 to 3
- zeta_proj: bfloat16 [768, 128], replicated, may hold values from -0.21875 to 0.21875
- zeta_bias: float32 [128], replicated, may hold values from -3 to 3
- query_gain: float32 [128], replicated, may hold values from 1.5 to 4
- query_shift: float32 [128], replicated, may hold values from -3 to 3
- key_gain: float32 [128], replicated, may hold values from 1.5 to 4
- rel_bias: float32 [255], replicated, may hold values from -4 to 4
- reset_proj: bfloat16 [768, 1536], P(None, 'wa'), may hold values from -0.21875 to 0.21875
- reset_bias: float32 [1536], P('wa'), may hold values from -3 to 3
- value_proj: bfloat16 [768, 1536], P(None, 'wa'), may hold values from -0.21875 to 0.21875
- value_bias: float32 [1536], P('wa'), may hold values from -3 to 3
- update_proj: bfloat16 [768, 768], P('wa'), may hold values from -0.21875 to 0.21875
- update_bias: float32 [768], replicated, may hold values from -3 to 3
- mixer_proj: bfloat16 [768, 768], P('wa'), may hold values from -0.21875 to 0.21875
- output_proj: bfloat16 [1536, 768], P('wa'), may hold values from -0.4375 to 0.4375
- output_bias: float32 [768], replicated, may hold values from -3 to 3
- first_gain: float32 [768], replicated, may hold values from 0.25 to 1.75
- first_shift: float32 [768], replicated, may hold values from -3 to 3
- up_proj: bfloat16 [768, 1536], P(None, 'wa'), may hold values from -0.21875 to 0.21875
- up_bias: bfloat16 [1536], P('wa'), may hold values from -3 to 3
- down_proj: bfloat16 [1536, 768], P('wa'), may hold values from -0.15625 to 0.15625
- down_bias: float32 [768], replicated, may hold values from -3 to 3
- second_gain: float32 [768], replicated, may hold values from 0.25 to 1.75
- second_shift: float32 [768], replicated, may hold values from -3 to 3
Outputs:
- block_out: bfloat16 [2, 4096, 768], P(None, 'seq', 'wa')
- input_grad: float32 [2, 4096, 768], P(None, 'seq', 'wa')
- teacher_loss: float32 [], replicated
- decay_grad: float32 [768, 16], P('wa')
- feed_grad: float32 [768, 16], P('wa')
- read_grad: float32 [768, 16], P('wa')
- skip_grad: float32 [768], P('wa')
- zeta_grad: float32 [768, 128], replicated
- zbias_grad: float32 [128], replicated
- qgain_grad: float32 [128], replicated
- qshift_grad: float32 [128], replicated
- kgain_grad: float32 [128], replicated
- rel_grad: float32 [255], replicated
- reset_grad: float32 [768, 1536], P(None, 'wa')
- rbias_grad: float32 [1536], P('wa')
- value_grad: float32 [768, 1536], P(None, 'wa')
- vbias_grad: float32 [1536], P('wa')
- update_grad: float32 [768, 768], P('wa')
- ubias_grad: float32 [768], replicated
- mixer_grad: float32 [768, 768], P('wa')
- output_grad: float32 [1536, 768], P('wa')
- obias_grad: float32 [768], replicated
- gainone_grad: float32 [768], replicated
- shiftone_grad: float32 [768], replicated
- up_grad: float32 [768, 1536], P(None, 'wa')
- upbias_grad: float32 [1536], P('wa')
- down_grad: float32 [1536, 768], P('wa')
- downbias_grad: float32 [768], replicated
- gaintwo_grad: float32 [768], replicated
- shifttwo_grad: float32 [768], replicated
Inputs may be any that keep to these rules, and one draw needn't show every extreme that they name: `lengths`: one sequence is complete. `positions`: within each sequence the ids start at 0 and rise by 1 or 2 from one token to the next; in one sequence every rise is 2.
All inputs are finite; a program needn't handle non-finite values.
Results may differ from a plain program's by a relative error of at most 0.0181.
The roundings to bfloat16 on the way count: a program that leaves them out, or rounds other values in their place, can miss the bound.
Values may be sent and summed in bfloat16 or wider, within the bound.
No kernel may reach another device: no remote copies, remote signals or barrier semaphores. Data moves between devices by JAX's collectives and lax.ppermute only.
A program may use at most 192 MiB of HBM per device.

v0:
```python
import jax
import jax.numpy as jnp
from jax import lax
from jax.sharding import PartitionSpec as P

Z = 128
GROUP = 128


EPSILON = 1e-05
HIGHEST = lax.Precision.HIGHEST


def carried_in(x, axis, combine, identity, reverse):
    peers, position = (lax.axis_size(axis), lax.axis_index(axis))
    everything = jax.tree.map(lambda part: lax.all_gather(part, axis), x)
    start = jax.tree.map(
        lambda part, zero: jnp.broadcast_to(jnp.asarray(zero, part.dtype), part.shape), x, identity
    )

    def hop(k, before):
        at = peers - 1 - k if reverse else k
        reached = at > position if reverse else at < position
        new = combine(before, jax.tree.map(lambda part: part[at], everything))
        return jax.tree.map(lambda a, b: jnp.where(reached, a, b), new, before)

    return lax.fori_loop(0, peers, hop, start)


def silu_slope(pre_act):
    gate_val = jax.nn.sigmoid(pre_act)
    return gate_val * (1.0 + pre_act * (1.0 - gate_val))


def compose(earlier, latter):
    return (earlier[0] * latter[0], latter[0] * earlier[1] + latter[1])


def project(left_side, weight):
    return jnp.dot(left_side, weight, preferred_element_type=jnp.float32)


def project_back(left_side, weight):
    return lax.dot_general(
        left_side, weight, (((1,), (1,)), ((), ())), preferred_element_type=jnp.float32
    )


def contract_rows(left_side, right_side):
    return lax.dot_general(
        left_side, right_side, (((0,), (0,)), ((), ())), preferred_element_type=jnp.float32
    )


def layer_norm(values, scales, offsets):
    center = values - jnp.mean(values, axis=-1, keepdims=True)
    inv_scale = lax.rsqrt(jnp.mean(center * center, axis=-1, keepdims=True) + EPSILON)
    normed = center * inv_scale
    return (normed * scales + offsets, normed, inv_scale)


def norm_back(grad_out, normed, inv_scale, scales):
    scaled = grad_out * scales
    mean_one = jnp.mean(scaled, axis=-1, keepdims=True)
    mean_two = jnp.mean(scaled * normed, axis=-1, keepdims=True)
    return inv_scale * (scaled - mean_one - normed * mean_two)


def doubling(drive, decay_flat, backward):
    row_count = drive.shape[1]
    running = drive
    span = 1
    while span < row_count:
        factor = decay_flat**span
        padding = jnp.zeros((drive.shape[0], span, drive.shape[2]), jnp.float32)
        if backward:
            moved = jnp.concatenate([running[:, span:], padding], axis=1)
        else:
            moved = jnp.concatenate([padding, running[:, :-span]], axis=1)
        running = running + factor * moved
        span = span * 2
    return running


def per_device(
    inputs,
    targets,
    lengths,
    positions,
    ema_decay,
    ema_feed,
    ema_read,
    ema_skip,
    zeta_proj,
    zeta_bias,
    query_gain,
    query_shift,
    key_gain,
    rel_bias,
    reset_proj,
    reset_bias,
    value_proj,
    value_bias,
    update_proj,
    update_bias,
    mixer_proj,
    output_proj,
    output_bias,
    first_gain,
    first_shift,
    up_proj,
    up_bias,
    down_proj,
    down_bias,
    second_gain,
    second_shift,
):
    seq_count, seq_rows, local_width = inputs.shape
    tok_rows = seq_count * seq_rows
    model_width = targets.shape[2]
    comp_count = ema_decay.shape[1]
    flat_width = local_width * comp_count
    seq_devices = lax.axis_size("seq")
    wa_devices = lax.axis_size("wa")
    seq_place = lax.axis_index("seq")
    wa_place = lax.axis_index("wa")
    total_tokens = tok_rows * seq_devices
    bucket_count = rel_bias.shape[0]
    score_scale = Z ** (-0.5)
    offsets = seq_place * seq_rows + lax.iota(jnp.int32, seq_rows)
    row_weight = (offsets[None, :] < lengths[:, None]).astype(jnp.float32).reshape(tok_rows)
    true_count = jnp.sum(lengths).astype(jnp.float32)
    at_start = (seq_place == 0).astype(jnp.float32)
    at_end = (seq_place == seq_devices - 1).astype(jnp.float32)

    def spread(field):
        return jnp.broadcast_to(field[:, :, :, None], field.shape + (comp_count,)).reshape(
            seq_count, seq_rows, flat_width
        )

    def fold(field):
        return jnp.sum(field.reshape(seq_count, seq_rows, local_width, comp_count), axis=-1)

    inputs_three = inputs.astype(jnp.float32)
    inputs_f = inputs_three.reshape(tok_rows, local_width)
    inputs_rows = inputs.reshape(tok_rows, local_width)
    decay_flat = ema_decay.reshape(flat_width)
    feed_flat = ema_feed.reshape(flat_width)
    read_flat = ema_read.reshape(flat_width)
    log_decay = jnp.log(decay_flat)
    row_steps = lax.iota(jnp.float32, seq_rows)
    powers = jnp.exp((row_steps + 1.0)[:, None] * log_decay)
    back_powers = jnp.exp((seq_rows - row_steps)[:, None] * log_decay)
    block_power = jnp.broadcast_to(powers[-1], (seq_count, flat_width))
    inputs_spread = spread(inputs_three)
    partial_state = doubling(inputs_spread * feed_flat, decay_flat, False)
    identity = (
        jnp.ones((seq_count, flat_width), jnp.float32),
        jnp.zeros((seq_count, flat_width), jnp.float32),
    )
    prefix = carried_in(
        (block_power * (1.0 - at_start), partial_state[:, -1]), "seq", compose, identity, False
    )
    state_in = prefix[1] * (1.0 - at_start)
    states = powers[None] * state_in[:, None] + partial_state
    ema_three = fold(states * read_flat) + ema_skip * inputs_three
    ema_val = ema_three.reshape(tok_rows, local_width)
    mixed_bf = jax.nn.silu(ema_val).astype(jnp.bfloat16)
    mixed_all, inputs_all = (
        lax.all_gather(mixed_bf, "wa", axis=1, tiled=True),
        lax.all_gather(inputs_rows, "wa", axis=1, tiled=True),
    )
    zeta_pre = project(mixed_all, zeta_proj) + zeta_bias
    zeta_act = jax.nn.silu(zeta_pre)
    queries_bf = (zeta_act * query_gain + query_shift).astype(jnp.bfloat16)
    keys_bf = (zeta_act * key_gain).astype(jnp.bfloat16)
    reset_pre = project(mixed_all, reset_proj) + reset_bias
    reset_gate = jax.nn.silu(reset_pre)
    value_pre = project(inputs_all, value_proj) + value_bias
    values_bf = jax.nn.silu(value_pre).astype(jnp.bfloat16)
    n_groups = tok_rows // GROUP
    query_blocks = queries_bf.reshape(n_groups, GROUP, -1)
    key_blocks = keys_bf.reshape(n_groups, GROUP, -1)
    value_blocks = values_bf.reshape(n_groups, GROUP, -1)
    pos_blocks = positions.reshape(n_groups, GROUP)
    distance = jnp.clip(pos_blocks[:, :, None] - pos_blocks[:, None, :], 0, bucket_count - 1)
    causal = lax.iota(jnp.int32, GROUP)[:, None] >= lax.iota(jnp.int32, GROUP)[None, :]
    bucket_ids = lax.iota(jnp.int32, bucket_count)

    def pick_bias(block_dist):
        hits = (block_dist[:, :, None] == bucket_ids).astype(jnp.float32)
        return jnp.einsum("qkb,b->qk", hits, rel_bias, precision=HIGHEST)

    bias_table = lax.map(pick_bias, distance)

    def score_blocks():
        raw_scores = (
            jnp.einsum("cqz,ckz->cqk", query_blocks, key_blocks, preferred_element_type=jnp.float32)
            * score_scale
            + bias_table
        )
        return jnp.where(causal, raw_scores, -jnp.inf)

    scores = score_blocks()
    top_score = jnp.max(scores, axis=-1, keepdims=True)
    shifted = jnp.exp(scores - top_score)
    totals = jnp.sum(shifted, axis=-1, keepdims=True)
    log_norm = top_score + jnp.log(totals)
    probs_bf = (shifted / totals).astype(jnp.bfloat16)
    attended = jnp.einsum(
        "cqk,ckv->cqv", probs_bf, value_blocks, preferred_element_type=jnp.float32
    ).reshape(tok_rows, -1)
    gated_bf = (reset_gate * attended).astype(jnp.bfloat16)
    mixer_part = project(mixed_bf, mixer_proj) + project(gated_bf, output_proj)
    update_part = project(mixed_bf, update_proj)
    mixer_sum, update_sum = lax.psum((mixer_part, update_part), "wa")
    out_pre = mixer_sum + output_bias
    update_gate = jax.nn.sigmoid(update_sum + update_bias)
    out_act = jax.nn.silu(out_pre)
    inputs_wide = inputs_all.astype(jnp.float32)
    block_mid = update_gate * out_act + (1.0 - update_gate) * inputs_wide
    first_out, first_normed, first_inv = layer_norm(block_mid, first_gain, first_shift)
    first_bf = first_out.astype(jnp.bfloat16)
    part_rows = tok_rows // wa_devices
    up_whole, down_whole, bias_whole = (
        lax.all_gather(up_proj, "wa", axis=1, tiled=True),
        lax.all_gather(down_proj, "wa", axis=0, tiled=True),
        lax.all_gather(up_bias, "wa", axis=0, tiled=True),
    )
    first_rows = lax.dynamic_slice_in_dim(first_bf, wa_place * part_rows, part_rows, 0)
    up_pre = project(first_rows, up_whole) + bias_whole.astype(jnp.float32)
    up_act = jax.nn.silu(up_pre).astype(jnp.bfloat16)
    ffn_sum = lax.all_gather(project(up_act, down_whole), "wa", axis=0, tiled=True)
    second_in = first_out + ffn_sum + down_bias
    second_out, second_normed, second_inv = layer_norm(second_in, second_gain, second_shift)
    misfit = second_out - targets.astype(jnp.float32).reshape(tok_rows, model_width)
    loss_part = jnp.sum(row_weight * jnp.sum(misfit * misfit, axis=1)) / (
        2.0 * model_width * true_count
    )
    grad_out = misfit * (row_weight * (total_tokens / true_count))[:, None]
    gaintwo_grad = jnp.sum(grad_out * second_normed, axis=0)
    shifttwo_grad = jnp.sum(grad_out, axis=0)
    second_grad = norm_back(grad_out, second_normed, second_inv, second_gain)
    ffn_grad = second_grad.astype(jnp.bfloat16)
    downbias_grad = jnp.sum(ffn_grad.astype(jnp.float32), axis=0)
    grad_rows = lax.dynamic_slice_in_dim(ffn_grad, wa_place * part_rows, part_rows, 0)
    down_full = contract_rows(up_act, grad_rows)
    upre_grad = (project_back(grad_rows, down_whole) * silu_slope(up_pre)).astype(jnp.bfloat16)
    up_full = contract_rows(first_rows, upre_grad)
    upbias_full = jnp.sum(upre_grad.astype(jnp.float32), axis=0)
    up_grad, down_grad, upbias_grad = (
        lax.psum_scatter(
            up_full.astype(jnp.bfloat16), "wa", scatter_dimension=1, tiled=True
        ).astype(jnp.float32),
        lax.psum_scatter(
            down_full.astype(jnp.bfloat16), "wa", scatter_dimension=0, tiled=True
        ).astype(jnp.float32),
        lax.psum_scatter(
            upbias_full.astype(jnp.bfloat16), "wa", scatter_dimension=0, tiled=True
        ).astype(jnp.float32),
    )
    first_part = lax.all_gather(project_back(upre_grad, up_whole), "wa", axis=0, tiled=True)
    first_grad = second_grad + first_part
    gainone_grad = jnp.sum(first_grad * first_normed, axis=0)
    shiftone_grad = jnp.sum(first_grad, axis=0)
    mid_grad = norm_back(first_grad, first_normed, first_inv, first_gain)
    opre_grad = (mid_grad * update_gate * silu_slope(out_pre)).astype(jnp.bfloat16)
    upre_gate = (mid_grad * (out_act - inputs_wide) * update_gate * (1.0 - update_gate)).astype(
        jnp.bfloat16
    )
    direct = mid_grad * (1.0 - update_gate)
    obias_grad = jnp.sum(opre_grad.astype(jnp.float32), axis=0)
    ubias_grad = jnp.sum(upre_gate.astype(jnp.float32), axis=0)
    mixer_grad = contract_rows(mixed_bf, opre_grad)
    update_grad = contract_rows(mixed_bf, upre_gate)
    output_grad = contract_rows(gated_bf, opre_grad)
    gated_grad = project_back(opre_grad, output_proj)
    mixed_local = project_back(opre_grad, mixer_proj) + project_back(upre_gate, update_proj)
    ract_grad = gated_grad * attended
    attn_grad = (gated_grad * reset_gate).astype(jnp.bfloat16)
    attn_blocks = attn_grad.reshape(n_groups, GROUP, -1)
    prob_part = jnp.einsum(
        "cqv,ckv->cqk", attn_blocks, value_blocks, preferred_element_type=jnp.float32
    )
    prob_grad = lax.psum(prob_part, "wa")
    probs_again = jnp.exp(score_blocks() - log_norm)
    row_dot = jnp.sum(probs_again * prob_grad, axis=-1, keepdims=True)
    sgrad_bf = (probs_again * (prob_grad - row_dot)).astype(jnp.bfloat16)
    vals_grad = jnp.einsum(
        "cqk,cqv->ckv", probs_bf, attn_blocks, preferred_element_type=jnp.float32
    ).reshape(tok_rows, -1)
    query_grad = (
        jnp.einsum(
            "cqk,ckz->cqz", sgrad_bf, key_blocks, preferred_element_type=jnp.float32
        ).reshape(tok_rows, -1)
        * score_scale
    )
    key_grad = (
        jnp.einsum(
            "cqk,cqz->ckz", sgrad_bf, query_blocks, preferred_element_type=jnp.float32
        ).reshape(tok_rows, -1)
        * score_scale
    )

    def bucket_sums(pair):
        block_dist, block_grad = pair
        hits = (block_dist[:, :, None] == bucket_ids).astype(jnp.float32)
        return jnp.einsum("qkb,qk->b", hits, block_grad.astype(jnp.float32), precision=HIGHEST)

    rel_grad = jnp.sum(lax.map(bucket_sums, (distance, sgrad_bf)), axis=0)
    qgain_grad = jnp.sum(query_grad * zeta_act, axis=0)
    qshift_grad = jnp.sum(query_grad, axis=0)
    kgain_grad = jnp.sum(key_grad * zeta_act, axis=0)
    zpre_grad = ((query_grad * query_gain + key_grad * key_gain) * silu_slope(zeta_pre)).astype(
        jnp.bfloat16
    )
    rpre_grad = (ract_grad * silu_slope(reset_pre)).astype(jnp.bfloat16)
    vpre_grad = (vals_grad * silu_slope(value_pre)).astype(jnp.bfloat16)
    zbias_grad = jnp.sum(zpre_grad.astype(jnp.float32), axis=0)
    rbias_grad = jnp.sum(rpre_grad.astype(jnp.float32), axis=0)
    vbias_grad = jnp.sum(vpre_grad.astype(jnp.float32), axis=0)
    zeta_grad = contract_rows(mixed_all, zpre_grad)
    reset_grad = contract_rows(mixed_all, rpre_grad)
    value_grad = contract_rows(inputs_all, vpre_grad)
    mixed_rest, inputs_value = (
        lax.psum_scatter(
            project_back(rpre_grad, reset_proj).astype(jnp.bfloat16),
            "wa",
            scatter_dimension=1,
            tiled=True,
        ).astype(jnp.float32),
        lax.psum_scatter(
            project_back(vpre_grad, value_proj).astype(jnp.bfloat16),
            "wa",
            scatter_dimension=1,
            tiled=True,
        ).astype(jnp.float32),
    )
    zeta_rows = lax.dynamic_slice_in_dim(zeta_proj, wa_place * local_width, local_width, 0)
    mixed_grad = mixed_local + mixed_rest + project_back(zpre_grad, zeta_rows)
    ema_grad = mixed_grad * silu_slope(ema_val)
    ema_three_grad = ema_grad.reshape(seq_count, seq_rows, local_width)
    back_partial = doubling(spread(ema_three_grad) * read_flat, decay_flat, True)
    suffix = carried_in(
        (block_power * (1.0 - at_end), back_partial[:, 0]), "seq", compose, identity, True
    )
    grad_in = suffix[1] * (1.0 - at_end)
    state_grads = back_powers[None] * grad_in[:, None] + back_partial
    prev_states = jnp.concatenate([state_in[:, None], states[:, :-1]], axis=1)
    decay_grad = jnp.sum(state_grads * prev_states, axis=(0, 1)).reshape(local_width, comp_count)
    feed_grad = jnp.sum(state_grads * inputs_spread, axis=(0, 1)).reshape(local_width, comp_count)
    read_grad = jnp.sum(states * spread(ema_three_grad), axis=(0, 1)).reshape(
        local_width, comp_count
    )
    skip_grad = jnp.sum(ema_grad * inputs_f, axis=0)
    direct_cols = lax.dynamic_slice_in_dim(direct, wa_place * local_width, local_width, 1)
    rest_three = (inputs_value + direct_cols).reshape(seq_count, seq_rows, local_width)
    input_grad = fold(state_grads * feed_flat) + ema_skip * ema_three_grad + rest_three
    summed = lax.psum(
        (
            decay_grad,
            feed_grad,
            read_grad,
            skip_grad,
            zeta_grad,
            zbias_grad,
            qgain_grad,
            qshift_grad,
            kgain_grad,
            rel_grad,
            reset_grad,
            rbias_grad,
            value_grad,
            vbias_grad,
            update_grad,
            ubias_grad,
            mixer_grad,
            output_grad,
            obias_grad,
            gainone_grad,
            shiftone_grad,
            up_grad,
            upbias_grad,
            down_grad,
            downbias_grad,
            gaintwo_grad,
            shifttwo_grad,
            loss_part,
        ),
        "seq",
    )
    block_cols = lax.dynamic_slice_in_dim(second_out, wa_place * local_width, local_width, 1)
    block_cols = block_cols.reshape(seq_count, seq_rows, local_width).astype(jnp.bfloat16)
    return (
        block_cols,
        input_grad,
        summed[27],
        summed[0],
        summed[1],
        summed[2],
        summed[3],
        summed[4],
        summed[5],
        summed[6],
        summed[7],
        summed[8],
        summed[9],
        summed[10],
        summed[11],
        summed[12],
        summed[13],
        summed[14],
        summed[15],
        summed[16],
        summed[17],
        summed[18],
        summed[19],
        summed[20],
        summed[21],
        summed[22],
        summed[23],
        summed[24],
        summed[25],
        summed[26],
    )


def solution(mesh):
    return jax.shard_map(
        per_device,
        mesh=mesh,
        in_specs=(
            P(None, "seq", "wa"),
            P(None, "seq", None),
            P(),
            P(None, "seq"),
            P("wa", None),
            P("wa", None),
            P("wa", None),
            P("wa"),
            P(),
            P(),
            P(),
            P(),
            P(),
            P(),
            P(None, "wa"),
            P("wa"),
            P(None, "wa"),
            P("wa"),
            P("wa", None),
            P(),
            P("wa", None),
            P("wa", None),
            P(),
            P(),
            P(),
            P(None, "wa"),
            P("wa"),
            P("wa", None),
            P(),
            P(),
            P(),
        ),
        out_specs=(
            P(None, "seq", "wa"),
            P(None, "seq", "wa"),
            P(),
            P("wa", None),
            P("wa", None),
            P("wa", None),
            P("wa"),
            P(),
            P(),
            P(),
            P(),
            P(),
            P(),
            P(None, "wa"),
            P("wa"),
            P(None, "wa"),
            P("wa"),
            P("wa", None),
            P(),
            P("wa", None),
            P("wa", None),
            P(),
            P(),
            P(),
            P(None, "wa"),
            P("wa"),
            P("wa", None),
            P(),
            P(),
            P(),
        ),
        check_vma=False,
    )
```

profile of v0, /device:TPU:0, one launch (start us, length us, event | category | flops | bytes accessed | tf_op | source)
XLA Modules:
  0.0 1081.1 jit_solution(1554258756728142503)
XLA Ops:
  26.7 32.3 %all-gather.4 = f32[8,1,3072]{2,1,0:T(1,128)S(1)} all-gather(f32[1,1,3072]{2,1,0:T(1,128)S(1)} %get-tuple-element.610), channel_id=4, replica_groups=mesh['seq'=8,'wa'=4] {'seq'}, dimensions={0}, use_global_device_ids=true | all-gather | bytes 110592 | tf_op jit(solution)/shard_map/all_gather | solution.py:16
  101.5 10.6 multiply_add_fusion.12
  129.9 31.0 %all-gather.1 = f32[16,1,3072]{2,1,0:T(1,128)S(1)} all-gather(f32[2,1,3072]{2,1,0:T(1,128)S(1)} %copy.125), channel_id=5, replica_groups=mesh['seq'=8,'wa'=4] {'seq'}, dimensions={0}, use_global_device_ids=true | all-gather | bytes 221184 | tf_op jit(solution)/shard_map/all_gather | solution.py:16
  162.1 15.1 %broadcast_multiply_fusion = (f32[2,512,3072]{1,2,0:T(8,128)}, f32[2,512,3072]{1,2,0:T(8,128)}) fusion(f32[3072]{0:T(1024)S(1)} %mul.799, f32[2,512,3072]{1,2,0:T(8,128)} %copy-done.5, f32[2,3072]{1,0:T(2,128)S(1)} %broadcast_multiply_fusion.2, f32[512,3072]{0,1:T(8,128)} %copy.123), kind=kLoop, calls=%fused_computation.50 | loop fusion | flops 9437184 | bytes 44077056 | tf_op jit(solution)/shard_map/mul | solution.py:166
  188.2 71.6 %while.52 = (s32[]{:T(128)}, f32[8,128,128]{1,2,0:T(8,128)S(1)}, s32[8,128,128]{2,1,0:T(8,128)S(1)}, f32[255]{0:T(256)S(1)}, s32[]{:T(128)}) while((s32[]{:T(128)}, f32[8,128,128]{1,2,0:T(8,128)S(1)}, s32[8,128,128]{2,1,0:T(8,128)S(1)}, f32[255]{0:T(256)S(1)}, s32[]{:T(128)}) %tuple.204), condition=%wide.region_5.6_spmd.clone, body=%wide.region_4.5_spmd.clone.sunk | while | flops 54312960 | bytes 525385 | solution.py:194
  197.2 8.8 fusion.141
  206.1 8.8 fusion.141
  215.1 8.8 fusion.141
  287.9 112.4 %all-reduce.31.cloned.1.call-done = (f32[1024,768]{1,0:T(8,128)}, f32[1024,768]{1,0:T(8,128)}) async-done(((f32[1024,768]{1,0:T(8,128)}, f32[1024,768]{1,0:T(8,128)}), (f32[1024,768]{1,0:T(8,128)}, f32[1024,768]{1,0:T(8,128)})) %all-reduce.31.cloned.1.call-update) | async-done | bytes 6291472 | tf_op jit(solution)/shard_map/psum | solution.py:216
  408.1 17.9 %all-gather.18.cloned.1.call-done = bf16[768,1536]{1,0:T(8,128)(2,1)} async-done(((bf16[768,384]{1,0:T(8,128)(2,1)}), bf16[768,1536]{1,0:T(8,128)(2,1)}) %all-gather.18.cloned.1.call-update) | async-done | bytes 2359312 | tf_op jit(solution)/shard_map/all_gather | solution.py:226
  428.8 22.8 %all-gather.20.cloned.1.call-done = bf16[1536,768]{1,0:T(8,128)(2,1)} async-done(((bf16[384,768]{1,0:T(8,128)(2,1)}), bf16[1536,768]{1,0:T(8,128)(2,1)}) %all-gather.20.cloned.1.call-update) | async-done | bytes 2359312 | tf_op jit(solution)/shard_map/all_gather | solution.py:227
  456.8 27.0 %all-gather.22.cloned.1.call-done = f32[1024,768]{1,0:T(8,128)} async-done(((f32[256,768]{1,0:T(8,128)}), f32[1024,768]{1,0:T(8,128)}) %all-gather.22.cloned.1.call-update) | async-done | bytes 3145744 | tf_op jit(solution)/shard_map/all_gather | solution.py:233
  512.9 30.5 %all-gather.6 = f32[8,1,3072]{2,1,0:T(1,128)S(1)} all-gather(f32[1,1,3072]{2,1,0:T(1,128)S(1)} %copy-done.74), channel_id=6, replica_groups=mesh['seq'=8,'wa'=4] {'seq'}, dimensions={0}, use_global_device_ids=true | all-gather | bytes 110592 | tf_op jit(solution)/shard_map/all_gather | solution.py:16
  611.2 24.9 %all-reduce.27.cloned.1.call-done = f32[8,128,128]{1,2,0:T(8,128)} async-done(((f32[8,128,128]{1,2,0:T(8,128)}), f32[8,128,128]{1,2,0:T(8,128)}) %all-reduce.27.cloned.1.call-update) | async-done | bytes 524304 | tf_op jit(solution)/shard_map/psum | solution.py:285
  638.4 31.2 %while.53 = (s32[]{:T(128)}, f32[8,255]{1,0:T(8,128)S(1)}, s32[8,128,128]{2,1,0:T(8,128)}, bf16[8,128,128]{1,2,0:T(8,128)(2,1)S(1)}, s32[]{:T(128)}, /*index=5*/s32[]{:T(128)}) while((s32[]{:T(128)}, f32[8,255]{1,0:T(8,128)S(1)}, s32[8,128,128]{2,1,0:T(8,128)}, bf16[8,128,128]{1,2,0:T(8,128)(2,1)S(1)}, s32[]{:T(128)}, ...), condition=%wide.region_46.47_spmd.clone, body=%wide.region_45.46_spmd.clone.sunk | while | flops 12533762 | bytes 363597 | solution.py:310
  686.2 12.5 %slice.99 = f32[2,511,3072]{1,2,0:T(8,128)} slice(f32[2,512,3072]{1,2,0:T(8,128)} %bitcast_multiply_fusion.3), slice={[0:2], [1:512], [0:3072]} | slice | bytes 25116672 | tf_op jit(solution)/shard_map/slice | solution.py:77
  698.6 15.0 %fusion.13 = (f32[3072]{0:T(1024)S(1)}, f32[2,512,3072]{1,2,0:T(8,128)}) fusion(f32[2,512,3072]{1,2,0:T(8,128)} %get-tuple-element.607, f32[2,512,192]{1,2,0:T(8,128)S(1)} %bitcast.223, f32[2,511,3072]{1,2,0:T(8,128)} %slice.99, f32[3072]{0:T(1024)S(1)} %copy-done.54, f32[3072]{0:T(1024)S(1)} %mul.799), kind=kLoop, calls=%fused_computation.25 | loop fusion | flops 15725568 | bytes 38547456 | tf_op jit(solution)/shard_map/reduce_sum | solution.py:352
  714.4 12.4 %slice.100 = f32[2,510,3072]{1,2,0:T(8,128)} slice(f32[2,512,3072]{1,2,0:T(8,128)} %get-tuple-element.616), slice={[0:2], [2:512], [0:3072]} | slice | bytes 25067520 | tf_op jit(solution)/shard_map/slice | solution.py:77
  726.8 14.1 %multiply_add_fusion.8 = f32[2,512,3072]{1,2,0:T(8,128)} fusion(f32[2,512,3072]{1,2,0:T(8,128)} %get-tuple-element.616, f32[2,510,3072]{1,2,0:T(8,128)} %slice.100, f32[3072]{0:T(1024)S(1)} %copy-done.72), kind=kLoop, calls=%fused_computation.36 | loop fusion | flops 6291456 | bytes 37711872 | tf_op jit(solution)/shard_map/add | solution.py:80
  741.0 12.7 %slice.101 = f32[2,508,3072]{1,2,0:T(8,128)} slice(f32[2,512,3072]{1,2,0:T(8,128)} %multiply_add_fusion.8), slice={[0:2], [4:512], [0:3072]} | slice | bytes 24969216 | tf_op jit(solution)/shard_map/slice | solution.py:77
  753.6 14.1 %multiply_add_fusion.7 = f32[2,512,3072]{1,2,0:T(8,128)} fusion(f32[2,512,3072]{1,2,0:T(8,128)} %multiply_add_fusion.8, f32[2,508,3072]{1,2,0:T(8,128)} %slice.101, f32[3072]{0:T(1024)S(1)} %copy-done.70), kind=kLoop, calls=%fused_computation.35 | loop fusion | flops 6291456 | bytes 37662720 | tf_op jit(solution)/shard_map/add | solution.py:80
  767.7 12.6 %slice.102 = f32[2,504,3072]{1,2,0:T(8,128)} slice(f32[2,512,3072]{1,2,0:T(8,128)} %multiply_add_fusion.7), slice={[0:2], [8:512], [0:3072]} | slice | bytes 24772608 | tf_op jit(solution)/shard_map/slice | solution.py:77
  780.3 14.3 %multiply_add_fusion.6 = f32[2,512,3072]{1,2,0:T(8,128)} fusion(f32[2,512,3072]{1,2,0:T(8,128)} %multiply_add_fusion.7, f32[2,504,3072]{1,2,0:T(8,128)} %slice.102, f32[3072]{0:T(1024)S(1)} %copy-done.68), kind=kLoop, calls=%fused_computation.34 | loop fusion | flops 6291456 | bytes 37564416 | tf_op jit(solution)/shard_map/add | solution.py:80
  794.7 12.6 %slice.103 = f32[2,496,3072]{1,2,0:T(8,128)} slice(f32[2,512,3072]{1,2,0:T(8,128)} %multiply_add_fusion.6), slice={[0:2], [16:512], [0:3072]} | slice | bytes 24379392 | tf_op jit(solution)/shard_map/slice | solution.py:77
  807.2 14.0 %multiply_add_fusion.5 = f32[2,512,3072]{1,2,0:T(8,128)} fusion(f32[2,512,3072]{1,2,0:T(8,128)} %multiply_add_fusion.6, f32[2,496,3072]{1,2,0:T(8,128)} %slice.103, f32[3072]{0:T(1024)S(1)} %copy-done.66), kind=kLoop, calls=%fused_computation.33 | loop fusion | flops 6291456 | bytes 37367808 | tf_op jit(solution)/shard_map/add | solution.py:80
  821.3 13.4 %slice.104 = f32[2,480,3072]{1,2,0:T(8,128)} slice(f32[2,512,3072]{1,2,0:T(8,128)} %multiply_add_fusion.5), slice={[0:2], [32:512], [0:3072]} | slice | bytes 23592960 | tf_op jit(solution)/shard_map/slice | solution.py:77
  834.7 14.1 %multiply_add_fusion.4 = f32[2,512,3072]{1,2,0:T(8,128)} fusion(f32[2,512,3072]{1,2,0:T(8,128)} %multiply_add_fusion.5, f32[2,480,3072]{1,2,0:T(8,128)} %slice.104, f32[3072]{0:T(1024)S(1)} %copy-done.64), kind=kLoop, calls=%fused_computation.32 | loop fusion | flops 6291456 | bytes 36974592 | tf_op jit(solution)/shard_map/add | solution.py:80
  848.7 12.6 %slice.105 = f32[2,448,3072]{1,2,0:T(8,128)} slice(f32[2,512,3072]{1,2,0:T(8,128)} %multiply_add_fusion.4), slice={[0:2], [64:512], [0:3072]} | slice | bytes 22020096 | tf_op jit(solution)/shard_map/slice | solution.py:77
  861.3 9.5 multiply_add_fusion.3
  891.8 30.6 %all-gather.3 = f32[16,1,3072]{2,1,0:T(1,128)S(1)} all-gather(f32[2,1,3072]{2,1,0:T(1,128)S(1)} %copy.136), channel_id=7, replica_groups=mesh['seq'=8,'wa'=4] {'seq'}, dimensions={0}, use_global_device_ids=true | all-gather | bytes 221184 | tf_op jit(solution)/shard_map/all_gather | solution.py:16
  923.9 18.7 %fusion.12 = (f32[3072]{0:T(1024)S(1)}, f32[3072]{0:T(1024)S(1)}, f32[2,512,3072]{1,2,0:T(8,128)}) fusion(f32[2,512,3072]{1,2,0:T(8,128)} %copy-done.4, f32[2,3072]{1,0:T(2,128)S(1)} %broadcast_multiply_fusion.1, f32[512,3072]{0,1:T(8,128)} %copy.132, f32[2,512,192]{1,2,0:T(8,128)S(1)} %copy-done.12, f32[2,511,3072]{1,2,0:T(8,128)} %bitcast.211, ...), kind=kLoop, calls=%fused_computation.24 | loop fusion | flops 25159680 | bytes 44888064 | tf_op jit(solution)/shard_map/reduce_sum | solution.py:351
  943.0 108.2 %all-reduce.32 = (f32[]{:T(128)}, f32[192,16]{1,0:T(8,128)S(1)}, f32[192,16]{1,0:T(8,128)S(1)}, f32[192,16]{1,0:T(8,128)S(1)}, f32[192]{0:T(256)}, /*index=5*/f3...) all-reduce(f32[]{:T(128)S(6)} %div.88, ...), channel_id=1, replica_groups=mesh['seq'=8,'wa'=4] {'seq'}, use_global_device_ids=true, to_apply=%region_27.28 | all-reduce | flops 606528 | bytes 3672576 | tf_op jit(solution)/shard_map/psum | solution.py:359
  (513 shorter events, 370.5 us)
Async XLA Ops:
  7.2 269.6 %copy-start = (bf16[384,768]{1,0:T(8,128)(2,1)S(1)}, bf16[384,768]{1,0:T(8,128)(2,1)}, u32[]{:S(2)}) copy-start(bf16[384,768]{1,0:T(8,128)(2,1)} %param.60) | copy-start | bytes 1769476
  7.2 257.2 %all-gather.14.cloned.1.call-start = ((), (), s32[]{:S(2)}) async-start(), calls=%async_computation.4 | async-start | bytes 1966080 | tf_op jit(solution)/shard_map/all_gather | solution.py:170
  8.3 51.6 %copy-start.53 = (f32[3072]{0:T(1024)}, f32[3072]{0:T(1024)S(1)}, u32[]{:S(2)}) copy-start(f32[3072]{0:T(1024)S(1)} %reshape.342) | copy-start | bytes 36868
  9.2 50.7 %copy-start.55 = (f32[3072]{0:T(1024)}, f32[3072]{0:T(1024)S(1)}, u32[]{:S(2)}) copy-start(f32[3072]{0:T(1024)S(1)} %mul.767) | copy-start | bytes 36868
  10.2 54.6 %copy-start.71 = (f32[3072]{0:T(1024)}, f32[3072]{0:T(1024)S(1)}, u32[]{:S(2)}) copy-start(f32[3072]{0:T(1024)S(1)} %get-tuple-element.622) | copy-start | bytes 36868
  10.2 59.7 %copy-start.69 = (f32[3072]{0:T(1024)}, f32[3072]{0:T(1024)S(1)}, u32[]{:S(2)}) copy-start(f32[3072]{0:T(1024)S(1)} %get-tuple-element.629) | copy-start | bytes 36868
  10.2 64.8 %copy-start.67 = (f32[3072]{0:T(1024)}, f32[3072]{0:T(1024)S(1)}, u32[]{:S(2)}) copy-start(f32[3072]{0:T(1024)S(1)} %get-tuple-element.627) | copy-start | bytes 36868
  10.2 69.9 %copy-start.65 = (f32[3072]{0:T(1024)}, f32[3072]{0:T(1024)S(1)}, u32[]{:S(2)}) copy-start(f32[3072]{0:T(1024)S(1)} %get-tuple-element.628) | copy-start | bytes 36868
  10.2 75.0 %copy-start.63 = (f32[3072]{0:T(1024)}, f32[3072]{0:T(1024)S(1)}, u32[]{:S(2)}) copy-start(f32[3072]{0:T(1024)S(1)} %get-tuple-element.623) | copy-start | bytes 36868
  10.2 80.1 %copy-start.61 = (f32[3072]{0:T(1024)}, f32[3072]{0:T(1024)S(1)}, u32[]{:S(2)}) copy-start(f32[3072]{0:T(1024)S(1)} %get-tuple-element.624) | copy-start | bytes 36868
  10.2 87.6 %copy-start.59 = (f32[3072]{0:T(1024)}, f32[3072]{0:T(1024)S(1)}, u32[]{:S(2)}) copy-start(f32[3072]{0:T(1024)S(1)} %get-tuple-element.626) | copy-start | bytes 36868
  10.2 101.9 %copy-start.57 = (f32[3072]{0:T(1024)}, f32[3072]{0:T(1024)S(1)}, u32[]{:S(2)}) copy-start(f32[3072]{0:T(1024)S(1)} %get-tuple-element.625) | copy-start | bytes 36868
  12.3 47.6 %copy-start.11 = (f32[2,512,192]{1,2,0:T(8,128)}, f32[2,512,192]{1,2,0:T(8,128)S(1)}, u32[]{:S(2)}) copy-start(f32[2,512,192]{1,2,0:T(8,128)S(1)} %get-tuple-element.620) | copy-start | bytes 2359300
  187.0 81.3 %all-gather.16.cloned.1.call-start = ((), (), s32[]{:S(2)}) async-start(), calls=%async_computation.5 | async-start | bytes 1966080 | tf_op jit(solution)/shard_map/all_gather | solution.py:171
  187.9 212.5 %all-reduce.31.cloned.1.call-start = ((), (), s32[]{:S(2)}) async-start(), calls=%async_computation.16 | async-start | bytes 12582912 | tf_op jit(solution)/shard_map/psum | solution.py:216
  188.2 71.7 %copy-start.8 = (bf16[1024,192]{0,1:T(8,128)(2,1)S(1)}, bf16[1024,192]{0,1:T(8,128)(2,1)}, u32[]{:S(2)}) copy-start(bf16[1024,192]{0,1:T(8,128)(2,1)} %multiply_convert_fusion.4) | copy-start | bytes 1179652
  188.2 71.7 %copy-start.38 = (bf16[192,768]{1,0:T(8,128)(2,1)S(1)}, bf16[192,768]{1,0:T(8,128)(2,1)}, u32[]{:S(2)}) copy-start(bf16[192,768]{1,0:T(8,128)(2,1)} %param.59) | copy-start | bytes 884740
  279.5 120.9 %copy-start.75 = (f32[768]{0:T(1024)S(1)}, f32[768]{0:T(1024)}, u32[]{:S(2)}) copy-start(f32[768]{0:T(1024)} %param.61) | copy-start | bytes 9220
  279.5 120.8 %copy-start.76 = (f32[768]{0:T(1024)S(1)}, f32[768]{0:T(1024)}, u32[]{:S(2)}) copy-start(f32[768]{0:T(1024)} %param.58) | copy-start | bytes 9220
  279.5 146.5 %all-gather.18.cloned.1.call-start = ((), (), s32[]{:S(2)}) async-start(), calls=%async_computation.6 | async-start | bytes 2949120 | tf_op jit(solution)/shard_map/all_gather | solution.py:226
  280.1 171.5 %all-gather.20.cloned.1.call-start = ((), (), s32[]{:S(2)}) async-start(), calls=%async_computation.7 | async-start | bytes 2949120 | tf_op jit(solution)/shard_map/all_gather | solution.py:227
  280.7 203.1 %all-gather.22.cloned.1.call-start = ((), (), s32[]{:S(2)}) async-start(), calls=%async_computation.8 | async-start | bytes 3932160 | tf_op jit(solution)/shard_map/all_gather | solution.py:233
  287.9 116.3 %copy-start.9 = (bf16[1024,768]{1,0:T(8,128)(2,1)}, bf16[1024,768]{1,0:T(8,128)(2,1)S(1)}, u32[]{:S(2)}) copy-start(bf16[1024,768]{1,0:T(8,128)(2,1)S(1)} %copy.131) | copy-start | bytes 4718596
  428.8 55.0 %copy-start.91 = (f32[768]{0:T(1024)S(1)}, f32[768]{0:T(1024)}, u32[]{:S(2)}) copy-start(f32[768]{0:T(1024)} %param.67) | copy-start | bytes 9220
  455.1 110.8 %all-gather.24.cloned.1.call-start = ((), (), s32[]{:S(2)}) async-start(), calls=%async_computation.9 | async-start | bytes 3932160 | tf_op jit(solution)/shard_map/all_gather | solution.py:262
  500.4 86.5 %reduce-scatter.15.cloned.1.call-start = ((), (), s32[]{:S(2)}) async-start(), calls=%async_computation.14 | async-start | bytes 2949120
  508.2 35.2 %copy-start.20 = (f32[2,24,8,512]{3,2,1,0:T(8,128)S(1)}, f32[2,24,8,512]{3,2,1,0:T(8,128)}, u32[]{:S(2)}) copy-start(f32[2,24,8,512]{3,2,1,0:T(8,128)} %get-tuple-element.619) | copy-start | bytes 2359300
  508.2 103.0 %reduce-scatter.11.cloned.1.call-start = ((), (), s32[]{:S(2)}) async-start(), calls=%async_computation.12 | async-start | bytes 2949120 | tf_op jit(solution)/shard_map/reduce_scatter | solution.py:255
  512.8 123.2 %all-reduce.27.cloned.1.call-start = ((), (), s32[]{:S(2)}) async-start(), calls=%async_computation.11 | async-start | bytes 1048576 | tf_op jit(solution)/shard_map/psum | solution.py:285
  582.1 95.2 %reduce-scatter.9.cloned.1.call-start = ((), (), s32[]{:S(2)}) async-start(), calls=%async_computation.10 | async-start | bytes 1966080 | tf_op jit(solution)/shard_map/reduce_scatter | solution.py:326
  585.6 465.5 %reduce-scatter.13.cloned.1.call-start = ((), (), s32[]{:S(2)}) async-start(), calls=%async_computation.13 | async-start | bytes 1966080
  605.5 460.4 %all-reduce.29.cloned.1.call-start = ((), (), s32[]{:S(2)}) async-start(), calls=%async_computation.15 | async-start | bytes 10223616 | tf_op jit(solution)/shard_map/psum | solution.py:359
  (102 other events, 952.6 us)
Sparse Core Ops, SparseCore 0:
  187.1 20.5 all-gather.13
  209.9 19.7 all-gather.15
  279.6 120.6 all-reduce.30
  401.8 24.2 all-gather.17
  427.5 24.0 all-gather.19
  455.2 28.5 all-gather.21
  500.6 28.5 all-gather.23
  531.7 33.1 reduce-scatter.14
  567.5 33.0 reduce-scatter.10
  602.8 33.1 all-reduce.26
  638.6 28.2 reduce-scatter.8
  669.4 28.1 reduce-scatter.12
  703.7 181.8 all-reduce.28
where the time goes:
time: 1090 us; the launch traced here: 1080 us
  other arithmetic  270 us (25%)
  blocking collectives  244 us (22%)
  waiting for transfers between devices  206 us (19%)
  local copies, waits for them, and re-layouts  183 us (17%)
  matrix products  157 us (14%)
  between operations  17.8 us (2%)
    add x17, other arithmetic, doubling(): running = running + factor * moved  141 us
    all_gather x4, blocking collectives, carried_in(): everything = jax.tree.map(lambda part: lax.all_gather(part, axis), x)  125 us
    psum x1, waiting for transfers between devices, per_device(): mixer_sum, update_sum = lax.psum((mixer_part, update_part), 'wa')  112 us
    psum x1, blocking collectives, per_device(): lax.psum((decay_grad, feed_grad, read_grad, skip_grad, zeta_grad, zbias_g...  108 us
    slice x9, local copies, waits for them, and re-layouts, doubling(): moved = jnp.concatenate([running[:, span:], padding], axis=1)  94.2 us
    dot_general x8, matrix products, pick_bias(): return jnp.einsum('qkb,b->qk', hits, rel_bias, precision=HIGHEST)  70.2 us
    unnamed x260, local copies, waits for them, and re-layouts  41.7 us
    all_gather x1, waiting for transfers between devices, per_device(): lax.all_gather(project(up_act, down_whole), 'wa', axis=0, tiled=True)  27 us
  transfers between devices with their start and end apart: 13, of which 5 were waited for; matrix products, arithmetic and copies ran while one was open for 41% of the time, Pallas kernels for 0%

commit v1 on v0

v1 whole, which is shorter than its diff:
```python
import functools

import jax
import jax.numpy as jnp
from jax import lax
from jax.experimental import pallas as pl
from jax.experimental.pallas import tpu as pltpu
from jax.sharding import PartitionSpec as P

Z = 128
GROUP = 128
LANES = 128
CHUNKS = 8
BIAS_ROWS = 32
HIDE_ENDS, HIDE_VALUES, HIDE_ONE, HIDE_TWO, HIDE_BACK, HIDE_LAST = 20, 20, 20, 40, 60, 15
SHARE_BITS = 1
EPSILON = 1e-05
BF = jnp.bfloat16
F32 = jnp.float32
VMEM = pltpu.MemorySpace.VMEM
SMEM = pltpu.MemorySpace.SMEM


def dot(a, b):
    return jnp.dot(a, b, preferred_element_type=F32)


def dot_nt(a, b):
    return lax.dot_general(a, b, (((1,), (1,)), ((), ())), preferred_element_type=F32)


def dot_tn(a, b):
    return lax.dot_general(a, b, (((0,), (0,)), ((), ())), preferred_element_type=F32)


def sigmoid(v):
    return 1.0 / (1.0 + jnp.exp(-v))


def slope(v):
    s = sigmoid(v)
    return s * (1.0 + v * (1.0 - s))


def row(ref):
    return ref[...].reshape(1, ref.shape[0])


def colsum(v):
    return jnp.sum(v, axis=0, keepdims=True)


def normalise(v):
    center = v - jnp.mean(v, axis=-1, keepdims=True)
    inv = lax.rsqrt(jnp.mean(center * center, axis=-1, keepdims=True) + EPSILON)
    return center * inv, inv


def norm_back(grad, normed, inv, gain):
    scaled = grad * gain
    one = jnp.mean(scaled, axis=-1, keepdims=True)
    two = jnp.mean(scaled * normed, axis=-1, keepdims=True)
    return inv * (scaled - one - normed * two)


class Box:
    def __init__(self, **parts):
        self.__dict__.update(parts)


jax.tree_util.register_pytree_node(
    Box, lambda box: (tuple(vars(box).values()), tuple(vars(box))), lambda names, parts: Box(**dict(zip(names, parts)))
)


def whole(space=VMEM):
    return pl.BlockSpec(memory_space=space)


def run(kernel, ins, outs, scratch, after=(), vectors=None, limit=48, hides=0):
    body, count = kernel, len(ins)
    vectors = vectors or Box()
    outs.token = ((8, LANES), F32, VMEM)
    fetched = len(vars(vectors))
    ins = ins + [(vectors, pltpu.MemorySpace.HBM), (list(after), pl.ANY)]
    scratch = Box(
        body=scratch, vec=jax.tree.map(lambda a: pltpu.VMEM(a.shape, a.dtype), vectors),
        sem=pltpu.SemaphoreType.DMA((max(fetched, 1),)),
    )

    def kernel(*refs):
        hbm, out, s = refs[count], refs[count + 2], refs[count + 3]
        copies = [
            pltpu.make_async_copy(vars(hbm)[name], vars(s.vec)[name], s.sem.at[i]) for i, name in enumerate(vars(hbm))
        ]
        for copy in copies:
            copy.start()
        if fetched:
            s.body.vec = s.vec
            s.body.wait = lambda: [copy.wait() for copy in copies]
        out.token[...] = jnp.zeros_like(out.token)
        body(*refs[:count], out, s.body)

    specs = [jax.tree.map(lambda _, space=space: whole(space), tree) for tree, space in ins]
    trees = [tree for tree, _ in ins]
    leaf = lambda entry: isinstance(entry, tuple)
    shapes = jax.tree.map(lambda e: jax.ShapeDtypeStruct(e[0], e[1]), outs, is_leaf=leaf)
    out_specs = jax.tree.map(lambda e: whole(e[2]), outs, is_leaf=leaf)
    return pl.pallas_call(
        kernel,
        out_shape=(shapes,),
        in_specs=specs,
        out_specs=(out_specs,),
        scratch_shapes=[scratch],
        compiler_params=pltpu.CompilerParams(vmem_limit_bytes=limit * 2**20),
        cost_estimate=pl.CostEstimate(flops=1 + int(hides * 1.15e9), bytes_accessed=1, transcendentals=0),
    )(*trees)[0]


def beside(hides, *deps):
    def kernel(ins, out, s):
        pass

    return run(kernel, [(list(deps), pl.ANY)], Box(), Box(), hides=hides)


def pack(pieces, meta, regions, out):
    height = out.own.shape[0]
    for ref, at, rows, top, left in regions:
        out.packed[top : top + rows, left : left + ref.shape[1]] = ref[at : at + rows, :]

    def piece(j):
        for ref, at, rows, top, left in regions:
            low, high = max(top, j * height), min(top + rows, (j + 1) * height)
            if low < high:
                out.own[low - j * height : high - j * height, left : left + ref.shape[1]] = ref[at + low - top : at + high - top, :]

    for j in range(pieces):
        pl.when(meta[1] == j)(lambda j=j: piece(j))


def pack_first(pieces, meta, reset, value, rel, out, s):
    units = reset.shape[1]
    s.wait()
    s.rows[...] = jnp.zeros_like(s.rows)
    for left, ref in ((0, s.vec.reset), (units, s.vec.value)):
        rest = row(ref)
        for i in range(3):
            high = rest.astype(BF).astype(F32)
            s.rows[i : i + 1, left : left + units] = high
            rest = rest - high
    s.rows[3:4, :units] = row(s.vec.up).astype(F32)
    s.bias[...] = s.rows[...].astype(BF)
    out.rel[...] = jnp.zeros_like(out.rel)
    out.rel[0:1, : rel.shape[0]] = row(rel)
    wide = reset.shape[0]
    pack(pieces, meta, [(reset, 0, wide, 0, 0), (value, 0, wide, 0, units), (s.bias, 0, BIAS_ROWS, wide, 0)], out)


def pack_second(pieces, meta, update, mixer, output, out, s):
    width, units = update.shape[0], output.shape[0]
    pack(pieces, meta, [(update, 0, width, 0, 0), (mixer, 0, width, width, 0), (output, 0, units, 2 * width, 0)], out)


def pack_third(pieces, meta, up, down, out, s):
    hidden = up.shape[1]
    depth = up.shape[0] // (down.shape[1] // hidden)
    regions = [(up, at, depth, 0, at // depth * hidden) for at in range(0, up.shape[0], depth)]
    pack(pieces, meta, regions + [(down, 0, hidden, depth, 0)], out)


def lane_groups(seqs, width):
    groups = []
    rest = width % LANES
    for s in range(seqs):
        for c in range(0, width - rest, LANES):
            groups.append([(s, c, LANES, 0)])
    tile, lane = [], 0
    for s in range(seqs if rest else 0):
        if lane + rest > LANES:
            groups.append(tile)
            tile, lane = [], 0
        tile.append((s, width - rest, rest, lane))
        lane += rest
    if tile:
        groups.append(tile)
    return groups


def join(parts):
    rows = parts[0].shape[0]
    used = sum(p.shape[1] for p in parts)
    if used < LANES:
        parts = parts + [jnp.zeros((rows, LANES - used), parts[0].dtype)]
    return parts[0] if len(parts) == 1 else jnp.concatenate(parts, axis=1)


def rows_of(group, ref):
    return join([ref[:, c : c + w] for _, c, w, _ in group])


def tokens_of(group, get):
    return join([get(s, c, w) for s, c, w, _ in group])


def spread(row):
    return jnp.broadcast_to(row, (CHUNKS, LANES))


def power(v, count):
    while count > 1:
        v = v * v
        count //= 2
    return v


def shifted(v, by):
    at = lax.broadcasted_iota(jnp.int32, v.shape, 0)
    moved = pltpu.roll(v, by % CHUNKS, 0)
    keep = at >= by if by > 0 else at < CHUNKS + by
    return jnp.where(keep, moved, 0.0)


def chunk_scan(ends, chunk_decay, sign):
    run_sum, factor, step = ends, chunk_decay, 1
    while step < CHUNKS:
        run_sum = run_sum + factor * shifted(run_sum, sign * step)
        factor, step = factor * factor, step * 2
    return run_sum, shifted(run_sum, sign)


def rank_power(chunk_decay, reverse):
    at = lax.broadcasted_iota(jnp.int32, chunk_decay.shape, 0)
    at = CHUNKS - 1 - at if reverse else at
    result, factor, bit = jnp.ones_like(chunk_decay), chunk_decay, 1
    while bit < CHUNKS:
        result = jnp.where((at & bit) != 0, result * factor, result)
        factor, bit = factor * factor, bit * 2
    return result


def steps_of(length, body, carry, reverse=False, unroll=4):
    def block(i, state):
        for u in range(unroll):
            t = i * unroll + u
            state = body(length - 1 - t if reverse else t, state)
        return state

    return lax.fori_loop(0, length // unroll, block, carry)


def at_step(ref, g, t, length):
    return ref.at[g, pl.ds(t, CHUNKS, stride=length), :]


def ema_ends(groups, comps, blocks, meta, x_ref, decay_ref, out, s):
    rows = x_ref.shape[1]
    part = x_ref.shape[0] * rows // blocks
    copies = []
    for k in range(blocks):
        at = (meta[0] ^ k) * part
        source = x_ref.at[at // rows, pl.ds(pl.multiple_of(at % rows, part), part), :]
        copies.append(pltpu.make_async_copy(source, out.r[k], s.sem.at[k]))
    for copy in copies:
        copy.start()
    length = x_ref.shape[1] // CHUNKS
    for g, group in enumerate(groups):
        s.x[g] = tokens_of(group, lambda q, c, w: x_ref[q, :, c : c + w].astype(F32))
        decay = rows_of(group, decay_ref)
        decays = [spread(decay[n : n + 1]) for n in range(comps)]

        def body(t, state):
            now = at_step(s.x, g, t, length)[...]
            return tuple(decays[n] * state[n] + now for n in range(comps))

        ends = steps_of(length, body, (jnp.zeros((CHUNKS, LANES), F32),) * comps)
        for n in range(comps):
            total, before = chunk_scan(ends[n], power(decays[n], length), 1)
            out.before[g, n] = before
            out.fade[g, n : n + 1, :] = power(decay[n : n + 1], length * CHUNKS)
            out.end[g, n : n + 1, :] = total[CHUNKS - 1 :]
    for copy in copies:
        copy.wait()


def carried(parts, device_decay, rank, reverse):
    total, passed = jnp.zeros_like(device_decay), jnp.ones_like(device_decay)
    for i, part in enumerate(parts):
        counts = ((rank // (1 << i)) % 2) == (0 if reverse else 1)
        total = jnp.where(counts, total + passed * part, total)
        passed = jnp.where(counts, passed * device_decay, passed)
        device_decay = device_decay * device_decay
    return total


def ema_values(groups, comps, blocks, meta, x_ref, decay_ref, mix_ref, skip_ref, before_ref, got, out, s):
    length = x_ref.shape[1] // CHUNKS
    width = x_ref.shape[2]
    seqs, rows = x_ref.shape[0], x_ref.shape[1]
    for g, group in enumerate(groups):
        s.x[g] = tokens_of(group, lambda q, c, w: x_ref[q, :, c : c + w].astype(F32))
        decay, mix, skip = rows_of(group, decay_ref), rows_of(group, mix_ref), rows_of(group, skip_ref)
        decays = [spread(decay[n : n + 1]) for n in range(comps)]
        mixes = [spread(mix[n : n + 1]) for n in range(comps)]
        skip = spread(skip)
        state_in = carried([part[g] for part in got], power(decay, length * CHUNKS), meta[2], False)
        start = []
        for n in range(comps):
            ranks = rank_power(power(decays[n], length), False)
            start.append(before_ref[g, n] + ranks * spread(state_in[n : n + 1]))
            out.start[g, n] = start[n]

        def body(t, state):
            now = at_step(s.x, g, t, length)[...]
            state = tuple(decays[n] * state[n] + now for n in range(comps))
            terms = [mixes[n] * state[n] for n in range(comps)] + [skip * now]
            while len(terms) > 1:
                terms = [a + b for a, b in zip(terms[::2], terms[1::2])] + (terms[-1:] if len(terms) % 2 else [])
            at_step(s.y, g, t, length)[...] = terms[0]
            return state

        steps_of(length, body, tuple(start))
        for q, c, w, lane in group:
            value = s.y[g, :, lane : lane + w]
            out.value[q, :, c : c + w] = value
            s.mixed[pl.ds(q * rows, rows), c : c + w] = (value * sigmoid(value)).astype(BF)
    part = seqs * rows // blocks
    copies = [
        pltpu.make_async_copy(
            s.mixed.at[pl.ds(pl.multiple_of((meta[0] ^ k) * part, part), part), :], out.m[k], s.sem.at[k]
        )
        for k in range(blocks)
    ]
    for copy in copies:
        copy.start()
    for copy in copies:
        copy.wait()


def ema_back_ends(groups, comps, blocks, meta, grads, value_ref, decay_ref, out, s):
    length = value_ref.shape[1] // CHUNKS
    rows = value_ref.shape[1]
    part = value_ref.shape[0] * rows // blocks
    copies = [
        pltpu.make_async_copy(
            grads[k], s.grad.at[pl.ds(pl.multiple_of((meta[0] ^ k) * part, part), part), :], s.sem.at[k]
        )
        for k in range(blocks)
    ]
    for copy in copies:
        copy.start()
    for copy in copies:
        copy.wait()
    for g, group in enumerate(groups):

        def load(q, c, w):
            return s.grad[pl.ds(q * rows, rows), c : c + w].astype(F32) * slope(value_ref[q, :, c : c + w])

        out.grad[g] = tokens_of(group, load)
        decay = rows_of(group, decay_ref)
        decays = [spread(decay[n : n + 1]) for n in range(comps)]

        def body(t, state):
            now = at_step(out.grad, g, t, length)[...]
            return tuple(decays[n] * state[n] + now for n in range(comps))

        ends = steps_of(length, body, (jnp.zeros((CHUNKS, LANES), F32),) * comps, reverse=True)
        for n in range(comps):
            total, after = chunk_scan(ends[n], power(decays[n], length), -1)
            out.after[g, n] = after
            out.first[g, n : n + 1, :] = total[:1]


def ema_back(groups, comps, blocks, meta, x_ref, grad_ref, rests, decay_ref, mix_ref, skip_ref, start_ref, after_ref, got, out, s):
    length = x_ref.shape[1] // CHUNKS
    seqs, rows = x_ref.shape[0], x_ref.shape[1]
    part = seqs * rows // blocks
    copies = [
        pltpu.make_async_copy(
            rests[k], s.rest.at[pl.ds(pl.multiple_of((meta[0] ^ k) * part, part), part), :], s.sem.at[k]
        )
        for k in range(blocks)
    ]
    for copy in copies:
        copy.start()
    out.sums[...] = jnp.zeros_like(out.sums)
    half = comps // 2
    for g, group in enumerate(groups):
        s.x[g] = tokens_of(group, lambda q, c, w: x_ref[q, :, c : c + w].astype(F32))
        decay, mix, skip = rows_of(group, decay_ref), rows_of(group, mix_ref), rows_of(group, skip_ref)
        decays = [spread(decay[n : n + 1]) for n in range(comps)]
        mixes = [spread(mix[n : n + 1]) for n in range(comps)]
        skip = spread(skip)

        def forward(t, state):
            now = at_step(s.x, g, t, length)[...]
            for n in range(comps):
                s.states[t, n] = state[n]
            return tuple(decays[n] * state[n] + now for n in range(comps))

        steps_of(length, forward, tuple(start_ref[g, n] for n in range(comps)))
        grad_in = carried([p[g] for p in got], power(decay, length * CHUNKS), meta[2], True)
        for h in range(2):
            mine = range(h * half, (h + 1) * half)
            begin = []
            for n in mine:
                ranks = rank_power(power(decays[n], length), True)
                begin.append(after_ref[g, n] + ranks * spread(grad_in[n : n + 1]))
            zero = (jnp.zeros((CHUNKS, LANES), F32),) * half

            def backward(t, carry):
                grads, moments, changes, skips = carry
                now, up = at_step(s.x, g, t, length)[...], at_step(grad_ref, g, t, length)[...]
                grads = tuple(decays[n] * grads[i] + up for i, n in enumerate(mine))
                moments = tuple(moments[i] + grads[i] * now for i in range(half))
                changes = tuple(changes[i] + grads[i] * s.states[t, n] for i, n in enumerate(mine))
                terms = [mixes[n] * grads[i] for i, n in enumerate(mine)]
                if h == 0:
                    terms.append(skip * up)
                    skips = skips + up * now
                else:
                    terms.append(at_step(s.y, g, t, length)[...])
                while len(terms) > 1:
                    terms = [a + b for a, b in zip(terms[::2], terms[1::2])] + (terms[-1:] if len(terms) % 2 else [])
                at_step(s.y, g, t, length)[...] = terms[0]
                return grads, moments, changes, skips

            _, moments, changes, skips = steps_of(length, backward, (tuple(begin), zero, zero, zero[0]), reverse=True, unroll=2)
            for q, c, w, lane in group:
                for i, n in enumerate(mine):
                    out.sums[n : n + 1, c : c + w] += colsum(changes[i])[:, lane : lane + w]
                    out.sums[comps + n : comps + n + 1, c : c + w] += colsum(moments[i])[:, lane : lane + w]
                if h == 0:
                    out.sums[2 * comps : 2 * comps + 1, c : c + w] += colsum(skips)[:, lane : lane + w]
    for copy in copies:
        copy.wait()
    width = x_ref.shape[2]
    for q in range(seqs):
        out.block[q] = s.rest[pl.ds(q * rows, rows), width:]
    for g, group in enumerate(groups):
        for q, c, w, lane in group:
            rest = s.rest[pl.ds(q * rows, rows), c : c + w].astype(F32)
            out.grad[q, :, c : c + w] = s.y[g, :, lane : lane + w] + rest


def weight_copies(meta, shards, dst, sem, first):
    copies = []
    for k, pieces in enumerate(shards):
        height = dst.shape[1] // len(pieces)
        for j, piece in enumerate(pieces):
            target = dst.at[k]
            if len(pieces) > 1:
                target = dst.at[k, pl.ds(pl.multiple_of((meta[1] ^ j) * height, height), height), :]
            copies.append(pltpu.make_async_copy(piece, target, sem.at[first + len(copies)]))
    return copies


def block_copies(meta, blocks, dst, sem, first):
    return [
        pltpu.make_async_copy(block, dst.at[meta[0] ^ k], sem.at[first + k]) for k, block in enumerate(blocks)
    ]


def positions_of(ref, start, g):
    at = start + g * GROUP
    length = ref.shape[1]
    columns = pl.ds(pl.multiple_of(at % length, GROUP), GROUP)
    place = ref[0:1, columns]
    for q in range(1, ref.shape[0]):
        place = jnp.where(at // length == q, ref[q : q + 1, columns], place)
    return place


def attend_forward(peers, meta, mixed, raw, first, second, out, s):
    vec = s.vec
    blocks = block_copies(meta, mixed, s.mixed, s.sem, 0)
    blocks += block_copies(meta, raw, s.raw, s.sem, peers)
    ones = weight_copies(meta, first, s.one, s.sem, 2 * peers)
    twos = weight_copies(meta, second, s.two, s.sem, 2 * peers + len(ones))
    for copy in blocks + ones + twos:
        copy.start()
    for copy in blocks:
        copy.wait()
    width = s.mixed.shape[2]
    units = s.one.shape[2] // 2
    rows, wide = out.mixed.shape
    groups = rows // GROUP
    for b in range(peers):
        out.mixed[:, b * width : (b + 1) * width] = s.mixed[b]
        out.raw[:, b * width : (b + 1) * width] = s.raw[b]
    s.wait()
    zeta_pre = dot(out.mixed[...], vec.zeta[...]) + row(vec.zeta_bias)
    out.zeta_pre[...] = zeta_pre
    act = zeta_pre * sigmoid(zeta_pre)
    queries = (act * row(vec.query_gain) + row(vec.query_shift)).astype(BF)
    keys = (act * row(vec.key_gain)).astype(BF)
    out.queries[...] = queries
    out.keys[...] = keys
    causal = lax.broadcasted_iota(jnp.int32, (GROUP, GROUP), 0) >= lax.broadcasted_iota(jnp.int32, (GROUP, GROUP), 1)
    for g in range(groups):
        at = slice(g * GROUP, (g + 1) * GROUP)
        place = jnp.broadcast_to(positions_of(vec.positions, meta[0] * rows, g).astype(F32), (GROUP, GROUP))
        distance = jnp.clip((place.T - place).astype(jnp.int32), 0, 2 * GROUP - 2)
        low = jnp.take_along_axis(
            jnp.broadcast_to(vec.rel[0:1, :GROUP], (GROUP, GROUP)), distance & (GROUP - 1), axis=1
        )
        high = jnp.take_along_axis(
            jnp.broadcast_to(vec.rel[0:1, GROUP:], (GROUP, GROUP)), distance & (GROUP - 1), axis=1
        )
        scores = dot_nt(queries[at], keys[at]) * Z**-0.5 + jnp.where(distance < GROUP, low, high)
        scores = jnp.where(causal, scores, -jnp.inf)
        shifted_exp = jnp.exp(scores - jnp.max(scores, axis=-1, keepdims=True))
        out.probs[at, :] = shifted_exp / jnp.sum(shifted_exp, axis=-1, keepdims=True)
    for copy in ones:
        copy.wait()
    for copy in twos:
        copy.wait()
    s.pre[...] = jnp.zeros_like(s.pre)
    s.gate[...] = jnp.zeros_like(s.gate)

    def shard(k, carry):
        biases = s.one[k, wide : wide + 16, :].astype(F32)
        bias = biases[0:1] + biases[1:2] + biases[2:3]
        out.up_bias[k] = jnp.broadcast_to(biases[3:4, :units], (8, units))
        reset_pre = dot(out.mixed[...], s.one[k, :wide, :units]) + bias[:, :units]
        value_pre = dot(out.raw[...], s.one[k, :wide, units:]) + bias[:, units:]
        values = (value_pre * sigmoid(value_pre)).astype(BF)
        out.reset_pre[k] = reset_pre
        out.value_pre[k] = value_pre
        out.values[k] = values
        for g in range(groups):
            at = slice(g * GROUP, (g + 1) * GROUP)
            out.attended[k, at, :] = dot(out.probs[at, :].astype(BF), values[at])
        gated = (reset_pre * sigmoid(reset_pre) * out.attended[k]).astype(BF)
        out.gated[k] = gated
        block = s.mixed[meta[0] ^ k]
        s.gate[...] += dot(block, s.two[k, :width, :])
        s.pre[...] += dot(block, s.two[k, width : 2 * width, :]) + dot(gated, s.two[k, 2 * width :, :])
        return carry

    lax.fori_loop(0, peers, shard, 0)
    out_pre = s.pre[...] + row(vec.output_bias)
    out.out_pre[...] = out_pre
    gate = sigmoid(s.gate[...] + row(vec.update_bias))
    out.gate[...] = gate
    mid = gate * (out_pre * sigmoid(out_pre)) + (1.0 - gate) * out.raw[...].astype(F32)
    normed, inv = normalise(mid)
    out.normed[...] = normed
    out.inv[...] = inv


def feed_forward(peers, ranks, meta, lengths, third, normed_ref, inv_ref, targets, out, s):
    vec = s.vec
    rows = normed_ref.shape[0]
    seqs, seq_rows = targets.shape[0], targets.shape[1]
    seq, offset = meta[0] * rows // seq_rows, pl.multiple_of(meta[0] * rows % seq_rows, rows)
    fetch = pltpu.make_async_copy(targets.at[seq, pl.ds(offset, rows), :], s.targets, s.target_sem)
    fetch.start()
    threes = weight_copies(meta, third, s.three, s.sem, 0)
    for copy in threes:
        copy.start()
    rows, width = normed_ref.shape
    s.wait()
    units = vec.up_bias.shape[2]
    fold = width // units
    depth = width // fold
    first = normed_ref[...] * row(vec.first_gain) + row(vec.first_shift)
    s.first[...] = first.astype(BF)
    s.total[...] = first + row(vec.down_bias)
    for copy in threes:
        copy.wait()

    def forward(k, carry):
        pre = vec.up_bias[k, 0:1, :]
        for j in range(fold):
            pre = pre + dot(
                s.first[:, j * depth : (j + 1) * depth], s.three[k, :depth, j * units : (j + 1) * units]
            )
        s.up_pre[k] = pre
        act = (pre * sigmoid(pre)).astype(BF)
        s.act[k] = act
        s.total[...] += dot(act, s.three[k, depth:, :])
        return carry

    lax.fori_loop(0, peers, forward, 0)
    normed, inv = normalise(s.total[...])
    second = normed * row(vec.second_gain) + row(vec.second_shift)
    piece = width // peers
    for b in range(peers):
        out.second[b] = second[:, b * piece : (b + 1) * piece].astype(BF)
    fetch.wait()
    misfit = second - s.targets[...].astype(F32)
    place = lax.broadcasted_iota(jnp.int32, (rows, 1), 0) + (meta[2] * seq_rows + offset)
    weight = (place < lengths[seq]).astype(F32)
    tokens = lengths[0]
    for q in range(1, seqs):
        tokens = tokens + lengths[q]
    true_count = jnp.broadcast_to(tokens, (rows, 1)).astype(F32)
    losses = jnp.sum(misfit * misfit, axis=1, keepdims=True) * (weight / (2.0 * width * true_count))
    out.sums[...] = jnp.zeros_like(out.sums)
    out.sums[5:6, :] = jnp.broadcast_to(jnp.sum(losses, axis=0, keepdims=True), (1, width))
    grad_out = misfit * (weight * (seqs * seq_rows * ranks / true_count))
    out.sums[0:1, :] = colsum(grad_out * normed)
    out.sums[1:2, :] = colsum(grad_out)
    second_grad = norm_back(grad_out, normed, inv, row(vec.second_gain))
    ffn_grad = second_grad.astype(BF)
    s.grad[...] = ffn_grad
    out.sums[2:3, :] = colsum(ffn_grad.astype(F32))
    s.total[...] = second_grad

    def backward(k, carry):
        keep = k // 2
        down = dot_tn(s.act[k], s.grad[...]).astype(BF)
        up_grad = (dot_nt(s.grad[...], s.three[k, depth:, :]) * slope(s.up_pre[k])).astype(BF)
        out.up_bias[k] = jnp.broadcast_to(colsum(up_grad.astype(F32)), (8, units))
        s.upg[...] = up_grad
        ups = [dot_tn(s.first[:, j * depth : (j + 1) * depth], s.upg[...]).astype(BF) for j in range(fold)]

        def store(which):
            out.grads[which][keep, depth:, :] = down
            for j in range(fold):
                out.grads[which][keep, :depth, j * units : (j + 1) * units] = ups[j]

        pl.when(k % 2 == 0)(lambda: store(0))
        pl.when(k % 2 == 1)(lambda: store(1))
        for j in range(fold):
            s.total[:, j * depth : (j + 1) * depth] += dot_nt(
                s.upg[...], s.three[k, :depth, j * units : (j + 1) * units]
            )
        return carry

    lax.fori_loop(0, peers, backward, 0)
    first_grad = s.total[...]
    out.sums[3:4, :] = colsum(first_grad * normed_ref[...])
    out.sums[4:5, :] = colsum(first_grad)
    out.mid_grad[...] = norm_back(first_grad, normed_ref[...], inv_ref[...], row(vec.first_gain))


def attend_back_one(peers, meta, second, mixed_ref, raw_ref, mid_ref, pre_ref, gate_ref, reset_ref, attended_ref, gated_ref, out, s):
    twos = weight_copies(meta, second, s.two, s.sem, 0)
    for copy in twos:
        copy.start()
    rows, wide = mixed_ref.shape
    width = wide // peers
    for b in range(peers):
        s.mixed[b] = mixed_ref[:, b * width : (b + 1) * width]
    mid, gate, pre = mid_ref[...], gate_ref[...], pre_ref[...]
    pre_grad = (mid * gate * slope(pre)).astype(BF)
    s.pre_grad[...] = pre_grad
    gate_grad = (mid * (pre * sigmoid(pre) - raw_ref[...].astype(F32)) * gate * (1.0 - gate)).astype(BF)
    s.gate_grad[...] = gate_grad
    out.direct[...] = mid * (1.0 - gate)
    out.sums[...] = jnp.zeros_like(out.sums)
    out.sums[0:1, :] = colsum(pre_grad.astype(F32))
    out.sums[1:2, :] = colsum(gate_grad.astype(F32))
    for copy in twos:
        copy.wait()

    def shard(k, carry):
        keep = k // 2
        s.block[...] = s.mixed[meta[0] ^ k]
        update = dot_tn(s.block[...], s.gate_grad[...]).astype(BF)
        mixer = dot_tn(s.block[...], s.pre_grad[...]).astype(BF)
        output = dot_tn(gated_ref[k], s.pre_grad[...]).astype(BF)

        def store(which):
            out.grads[which][keep, :width, :] = update
            out.grads[which][keep, width : 2 * width, :] = mixer
            out.grads[which][keep, 2 * width :, :] = output

        pl.when(k % 2 == 0)(lambda: store(0))
        pl.when(k % 2 == 1)(lambda: store(1))
        out.mixed_grad[k] = dot_nt(s.gate_grad[...], s.two[k, :width, :]) + dot_nt(
            s.pre_grad[...], s.two[k, width : 2 * width, :]
        )
        gated_grad = dot_nt(s.pre_grad[...], s.two[k, 2 * width :, :])
        reset = reset_ref[k]
        out.attend_grad[k] = (gated_grad * (reset * sigmoid(reset))).astype(BF)
        reset_grad = (gated_grad * attended_ref[k] * slope(reset)).astype(BF)
        out.reset_grad[k] = reset_grad
        out.bias[k] = jnp.broadcast_to(colsum(reset_grad.astype(F32)), (8, reset_grad.shape[1]))
        return carry

    lax.fori_loop(0, peers, shard, 0)


def attend_back_two(
    peers, meta, first, mixed_ref, raw_ref, value_pre_ref, values_ref, probs_ref, agrad_ref, rgrad_ref, direct_ref, local_ref,
    queries_ref, keys_ref, zeta_pre_ref, second_ref, out, s,
):
    vec = s.vec
    ones = weight_copies(meta, first, s.one, s.sem, 0)
    for copy in ones:
        copy.start()
    rows, wide = mixed_ref.shape
    width = wide // peers
    units = values_ref.shape[2]
    groups = rows // GROUP
    s.wait()
    act = zeta_pre_ref[...] * sigmoid(zeta_pre_ref[...])
    line = lax.broadcasted_iota(jnp.int32, (2 * GROUP, GROUP), 0)
    buckets = jnp.zeros((1, 2 * GROUP), F32)
    for g in range(groups):
        at = slice(g * GROUP, (g + 1) * GROUP)

        def score(k, total):
            return total + dot_nt(agrad_ref[k, at, :], values_ref[k, at, :])

        prob_grad = lax.fori_loop(0, peers, score, jnp.zeros((GROUP, GROUP), F32))
        probs = probs_ref[at, :]
        row_dot = jnp.sum(probs * prob_grad, axis=-1, keepdims=True)
        sgrad = (probs * (prob_grad - row_dot)).astype(BF)
        s.query_grad[at, :] = dot(sgrad, keys_ref[at, :]) * Z**-0.5
        s.key_grad[at, :] = dot_tn(sgrad, queries_ref[at, :]) * Z**-0.5
        ahead = positions_of(vec.positions, meta[0] * rows, g)
        ahead = ahead - ahead[:, 0:1]
        to_row = (line == ahead).astype(BF)
        to_column = (line == 2 * GROUP - 1 - ahead).astype(BF)
        table = dot(to_row, dot_nt(sgrad, to_column).astype(BF))
        buckets = buckets + colsum(pltpu.roll(table, 1, 1, stride=1, stride_axis=0))
    out.rel[...] = jnp.broadcast_to(buckets, (8, 2 * GROUP))
    query_grad, key_grad = s.query_grad[...], s.key_grad[...]
    zeta_grad = (query_grad * row(vec.query_gain) + key_grad * row(vec.key_gain)) * slope(zeta_pre_ref[...])
    zeta_grad = zeta_grad.astype(BF)
    out.sums[...] = jnp.zeros_like(out.sums)
    out.sums[0:1, :] = colsum(zeta_grad.astype(F32))
    out.sums[1:2, :] = colsum(query_grad * act)
    out.sums[2:3, :] = colsum(query_grad)
    out.sums[3:4, :] = colsum(key_grad * act)
    out.zeta[...] = dot_tn(mixed_ref[...], zeta_grad)
    s.mixed[...] = dot_nt(zeta_grad, vec.zeta[...])
    s.raw[...] = direct_ref[...]
    for copy in ones:
        copy.wait()

    def shard(k, carry):
        keep = k // 2
        for g in range(groups):
            at = slice(g * GROUP, (g + 1) * GROUP)
            vals_grad = dot_tn(probs_ref[at, :].astype(BF), agrad_ref[k, at, :])
            s.vgrad[at, :] = (vals_grad * slope(value_pre_ref[k, at, :])).astype(BF)
        out.bias[k] = jnp.broadcast_to(colsum(s.vgrad[...].astype(F32)), (8, units))
        reset = dot_tn(mixed_ref[...], rgrad_ref[k]).astype(BF)
        value = dot_tn(raw_ref[...], s.vgrad[...]).astype(BF)

        def store(which):
            out.grads[which][keep, :, :units] = reset
            out.grads[which][keep, :, units:] = value

        pl.when(k % 2 == 0)(lambda: store(0))
        pl.when(k % 2 == 1)(lambda: store(1))
        s.mixed[...] += dot_nt(rgrad_ref[k], s.one[k, :wide, :units])
        s.raw[...] += dot_nt(s.vgrad[...], s.one[k, :wide, units:])
        return carry

    lax.fori_loop(0, peers, shard, 0)
    for b in range(peers):
        at = slice(b * width, (b + 1) * width)
        s.mixed_out[b] = (s.mixed[:, at] + local_ref[meta[0] ^ b]).astype(BF)
        s.raw_out[b, :, :width] = s.raw[:, at].astype(BF)
        s.raw_out[b, :, width:] = second_ref[b]
    sends = []
    for k in range(peers):
        sends.append(pltpu.make_async_copy(s.mixed_out.at[meta[0] ^ k], out.m[k], s.sem.at[2 * k]))
        sends.append(pltpu.make_async_copy(s.raw_out.at[meta[0] ^ k], out.r[k], s.sem.at[2 * k + 1]))
    for copy in sends:
        copy.start()
    for copy in sends:
        copy.wait()


def swap(x, axis, by):
    size = lax.axis_size(axis)
    return lax.ppermute(x, axis, [(i, i ^ by) for i in range(size)])


def later_than(x, *marks):
    for mark in marks:
        x, mark.token = lax.optimization_barrier((x, mark.token))
    return x


def exchange(blocks, axis):
    return [blocks[0]] + [swap(blocks[k], axis, k) for k in range(1, len(blocks))]


def group_totals(total, fade, axis, reverse):
    result = []
    for bit in bits_of(lax.axis_size(axis)):
        other = swap(total, axis, bit)
        result.append(other)
        upper = ((lax.axis_index(axis) // bit) % 2) == (0 if reverse else 1)
        total = jnp.where(upper, total + fade * other, other + fade * total)
        fade = fade * fade
    return result


def far_pieces(pack):
    return [swap(pack.own, "wa", k) for k in range(2, lax.axis_size("wa"), 2)]


def next_pieces(came):
    return [swap(piece, "seq", j) for piece in came for j in range(1, 1 << SHARE_BITS)]


def all_shards(pack, came, beyond):
    others = (1 << SHARE_BITS) - 1
    shards = [[pack.packed]]
    shards += [[came[i]] + beyond[i * others : (i + 1) * others] for i in range(len(came))]
    return [pieces for even in shards for pieces in (even, [swap(piece, "wa", 1) for piece in even])]


def plus(a, b):
    return (a.astype(F32) + b.astype(F32)).astype(a.dtype)


def core_sums(grads, *deps):
    return plus(grads[0], later_than(swap(grads[1], "wa", 1), *deps))


def shard_sum(parts, *deps):
    step = 2
    while parts.shape[0] > 1:
        parts = plus(parts[::2], later_than(swap(parts[1::2], "wa", step), *deps))
        step *= 2
    return parts[0]


def keep_rows(total, bit, *deps):
    here = (lax.axis_index("seq") // bit) % 2
    height = total.shape[-2] // 2
    mine = lax.dynamic_slice_in_dim(total, here * height, height, total.ndim - 2)
    theirs = lax.dynamic_slice_in_dim(total, (1 - here) * height, height, total.ndim - 2)
    return plus(mine, later_than(swap(theirs, "seq", bit), *deps))


def all_rows(total, bits):
    for bit in bits[::-1]:
        here = (lax.axis_index("seq") // bit) % 2
        other = swap(total, "seq", bit)
        total = jnp.where(
            here == 0, jnp.concatenate([total, other], axis=0), jnp.concatenate([other, total], axis=0)
        )
    return total


def sum_small(exact, rough, route):
    for axis, bit in route:
        high = lax.reduce_precision(exact, 8, 7)
        sent = jnp.concatenate([high.astype(BF), (exact - high).astype(BF), rough.astype(BF)])
        total = sent.astype(F32) + swap(sent, axis, bit).astype(F32)
        rows = exact.shape[0]
        exact, rough = total[:rows] + total[rows : 2 * rows], total[2 * rows :]
    return exact, rough


def bits_of(size):
    return [1 << b for b in range(size.bit_length() - 1)]


def per_device(
    inputs, targets, lengths, positions, ema_decay, ema_feed, ema_read, ema_skip, zeta_proj, zeta_bias, query_gain, query_shift,
    key_gain, rel_bias, reset_proj, reset_bias, value_proj, value_bias, update_proj, update_bias, mixer_proj, output_proj,
    output_bias, first_gain, first_shift, up_proj, up_bias, down_proj, down_bias, second_gain, second_shift,
):
    seqs, seq_rows, width = inputs.shape
    wide = targets.shape[2]
    comps = ema_decay.shape[1]
    peers, ranks = lax.axis_size("wa"), lax.axis_size("seq")
    me, rank = lax.axis_index("wa"), lax.axis_index("seq")
    tok_rows = seqs * seq_rows
    rows = tok_rows // peers
    n_groups = rows // GROUP
    units, hidden = reset_proj.shape[1], up_proj.shape[1]
    fold = wide // hidden
    depth = wide // fold
    total_tokens = tok_rows * ranks
    groups = lane_groups(seqs, width)
    tiles = len(groups)
    pieces = 1 << SHARE_BITS
    place = rank % pieces
    meta = jnp.stack([me, place, rank]).astype(jnp.int32)
    hbm = pltpu.MemorySpace.HBM
    sems = pltpu.SemaphoreType.DMA

    def packed(kernel, shape, arrays, scratch=None, vectors=None, **outs):
        return run(
            functools.partial(kernel, pieces),
            [(meta, SMEM)] + [(a, VMEM) for a in arrays],
            Box(packed=(shape, BF, VMEM), own=((shape[0] // pieces,) + shape[1:], BF, VMEM), **outs),
            scratch or Box(),
            vectors=vectors,
        )

    one_shape, two_shape, three_shape = (wide + BIAS_ROWS, 2 * units), (2 * width + units, wide), (depth + hidden, wide)
    pack_one = packed(
        pack_first, one_shape, [reset_proj, value_proj, rel_bias],
        Box(rows=pltpu.VMEM((BIAS_ROWS, 2 * units), F32), bias=pltpu.VMEM((BIAS_ROWS, 2 * units), BF)),
        Box(reset=reset_bias, value=value_bias, up=up_bias), rel=((8, 2 * GROUP), F32, VMEM),
    )

    decay_rows, mix_rows = ema_decay.T, (ema_feed * ema_read).T
    skip_row = ema_skip[None, :]
    ends = run(
        functools.partial(ema_ends, groups, comps, peers),
        [(meta, SMEM), (inputs, VMEM), (decay_rows, VMEM)],
        Box(r=[((rows, width), BF, hbm)] * peers, before=((tiles, comps, CHUNKS, LANES), F32, VMEM), end=((tiles, comps, LANES), F32, VMEM), fade=((tiles, comps, LANES), F32, VMEM)),
        Box(x=pltpu.VMEM((tiles, seq_rows, LANES), F32), sem=sems((peers,))),
        after=[pack_one.own],
        hides=HIDE_ENDS,
    )
    def gate(*arrays):
        ends.token, *arrays = lax.optimization_barrier((ends.token,) + arrays)
        return arrays

    pack_two = packed(pack_second, two_shape, gate(update_proj, mixer_proj, output_proj))
    pack_three = packed(pack_third, three_shape, gate(up_proj, down_proj))
    came_one = [later_than(x, ends) for x in far_pieces(pack_one)]
    pack_two.own, came_one[0] = lax.optimization_barrier((pack_two.own, came_one[0]))
    came_two = far_pieces(pack_two)
    next_one = next_pieces(came_one)
    raw_blocks = exchange(ends.r, "wa")
    earlier = group_totals(ends.end, ends.fade, "seq", False)
    earlier[-1], *raw_blocks = lax.optimization_barrier((earlier[-1], *raw_blocks))
    outs = Box(
        value=((seqs, seq_rows, width), F32, VMEM),
        start=((tiles, comps, CHUNKS, LANES), F32, VMEM),
    )
    outs.m = [((rows, width), BF, hbm)] * peers
    ema = run(
        functools.partial(ema_values, groups, comps, peers),
        [(meta, SMEM), (inputs, VMEM), (decay_rows, VMEM), (mix_rows, VMEM), (skip_row, VMEM), (ends.before, VMEM), (earlier, VMEM)],
        outs,
        Box(
            x=pltpu.VMEM((tiles, seq_rows, LANES), F32),
            y=pltpu.VMEM((tiles, seq_rows, LANES), F32),
            mixed=pltpu.VMEM((tok_rows, width), BF),
            sem=sems((peers,)),
        ),
        after=came_two + next_one,
        hides=HIDE_VALUES,
    )
    mixed_blocks = exchange(ema.m, "wa")
    held = (pack_three.own, pack_one.packed, pack_two.packed, *mixed_blocks)
    pack_three.own, pack_one.packed, pack_two.packed, *mixed_blocks = lax.optimization_barrier(held)
    came_three = far_pieces(pack_three)
    shards_one = all_shards(pack_one, came_one, next_one)
    shards_two = all_shards(pack_two, came_two, next_pieces(came_two))
    shards_three = all_shards(pack_three, came_three, next_pieces(came_three))

    count = len(jax.tree.leaves(shards_one))
    vec = Box(
        zeta=zeta_proj, zeta_bias=zeta_bias, query_gain=query_gain, query_shift=query_shift,
        key_gain=key_gain, rel=pack_one.rel, positions=positions,
        output_bias=output_bias, update_bias=update_bias,
    )
    fwd = run(
        functools.partial(attend_forward, peers),
        [(meta, SMEM), (mixed_blocks, hbm), (raw_blocks, hbm), (shards_one, hbm), (shards_two, hbm)],
        Box(
            mixed=((rows, wide), BF, VMEM), raw=((rows, wide), BF, VMEM), zeta_pre=((rows, Z), F32, VMEM),
            queries=((rows, Z), BF, VMEM), keys=((rows, Z), BF, VMEM), probs=((rows, GROUP), F32, VMEM),
            reset_pre=((peers, rows, units), F32, VMEM), value_pre=((peers, rows, units), F32, VMEM),
            values=((peers, rows, units), BF, VMEM), attended=((peers, rows, units), F32, VMEM),
            gated=((peers, rows, units), BF, VMEM), out_pre=((rows, wide), F32, VMEM), gate=((rows, wide), F32, VMEM),
            normed=((rows, wide), F32, VMEM), inv=((rows, 1), F32, VMEM), up_bias=((peers, 8, units), F32, VMEM),
        ),
        Box(
            mixed=pltpu.VMEM((peers, rows, width), BF), raw=pltpu.VMEM((peers, rows, width), BF),
            one=pltpu.VMEM((peers,) + one_shape, BF), two=pltpu.VMEM((peers,) + two_shape, BF),
            pre=pltpu.VMEM((rows, wide), F32), gate=pltpu.VMEM((rows, wide), F32),
            sem=sems((2 * peers + 2 * count,)),
        ),
        vectors=vec,
        limit=62,
    )

    vec = Box(
        first_gain=first_gain, first_shift=first_shift, down_bias=down_bias,
        second_gain=second_gain, second_shift=second_shift, up_bias=fwd.up_bias,
    )
    outs = Box(
        mid_grad=((rows, wide), F32, VMEM), second=((peers, rows, width), BF, VMEM), sums=((8, wide), F32, VMEM), up_bias=((peers, 8, hidden), F32, VMEM),
        grads=[((peers // 2,) + three_shape, BF, VMEM)] * 2,
    )
    ffn = run(
        functools.partial(feed_forward, peers, ranks),
        [(meta, SMEM), (lengths, SMEM), (shards_three, hbm), (fwd.normed, VMEM), (fwd.inv, VMEM), (targets, hbm)],
        outs,
        Box(
            three=pltpu.VMEM((peers,) + three_shape, BF), first=pltpu.VMEM((rows, wide), BF),
            total=pltpu.VMEM((rows, wide), F32), up_pre=pltpu.VMEM((peers, rows, hidden), F32),
            act=pltpu.VMEM((peers, rows, hidden), BF), grad=pltpu.VMEM((rows, wide), BF),
            upg=pltpu.VMEM((rows, hidden), BF), sem=sems((count,)), targets=pltpu.VMEM((rows, wide), BF), target_sem=sems(()),
        ),
        vectors=vec,
    )
    row_bits = bits_of(ranks)
    third_parts = core_sums(ffn.grads)

    one = run(
        functools.partial(attend_back_one, peers),
        [(meta, SMEM), (shards_two, hbm), (fwd.mixed, VMEM), (fwd.raw, VMEM), (ffn.mid_grad, VMEM), (fwd.out_pre, VMEM),
         (fwd.gate, VMEM), (fwd.reset_pre, VMEM), (fwd.attended, VMEM), (fwd.gated, VMEM)],
        Box(
            direct=((rows, wide), F32, VMEM), sums=((8, wide), F32, VMEM), mixed_grad=((peers, rows, width), F32, VMEM),
            attend_grad=((peers, rows, units), BF, VMEM), reset_grad=((peers, rows, units), BF, VMEM),
            bias=((peers, 8, units), F32, VMEM),
            grads=[((peers // 2,) + two_shape, BF, VMEM)] * 2,
        ),
        Box(
            two=pltpu.VMEM((peers,) + two_shape, BF), mixed=pltpu.VMEM((peers, rows, width), BF),
            block=pltpu.VMEM((rows, width), BF), pre_grad=pltpu.VMEM((rows, wide), BF),
            gate_grad=pltpu.VMEM((rows, wide), BF), sem=sems((count,)),
        ),
        after=[third_parts],
        hides=HIDE_ONE,
    )
    vec = Box(
        zeta=zeta_proj, query_gain=query_gain, key_gain=key_gain, positions=positions,
    )
    outs = Box(
        rel=((8, 2 * GROUP), F32, VMEM), sums=((8, Z), F32, VMEM), zeta=((wide, Z), F32, VMEM),
        bias=((peers, 8, units), F32, VMEM),
        grads=[((peers // 2, wide, 2 * units), BF, VMEM)] * 2,
    )
    outs.m = [((rows, width), BF, hbm)] * peers
    outs.r = [((rows, 2 * width), BF, hbm)] * peers
    two = run(
        functools.partial(attend_back_two, peers),
        [(meta, SMEM), (shards_one, hbm), (fwd.mixed, VMEM), (fwd.raw, VMEM), (fwd.value_pre, VMEM), (fwd.values, VMEM),
         (fwd.probs, VMEM), (one.attend_grad, VMEM), (one.reset_grad, VMEM), (one.direct, VMEM), (one.mixed_grad, VMEM),
         (fwd.queries, VMEM), (fwd.keys, VMEM), (fwd.zeta_pre, VMEM), (ffn.second, VMEM)],
        outs,
        Box(
            one=pltpu.VMEM((peers,) + one_shape, BF), query_grad=pltpu.VMEM((rows, Z), F32),
            key_grad=pltpu.VMEM((rows, Z), F32), mixed=pltpu.VMEM((rows, wide), F32), raw=pltpu.VMEM((rows, wide), F32),
            vgrad=pltpu.VMEM((rows, units), BF), mixed_out=pltpu.VMEM((peers, rows, width), BF),
            raw_out=pltpu.VMEM((peers, rows, 2 * width), BF), sem=sems((max(count, 2 * peers),)),
        ),
        vectors=vec,
    )
    grad_blocks = exchange(two.m, "wa")
    rest_blocks = exchange(two.r, "wa")
    third_rows = keep_rows(third_parts, row_bits[0], two)
    mark = beside(HIDE_TWO, two.rel)
    second_parts = core_sums(one.grads, mark)
    first_parts = core_sums(two.grads, mark)

    back = run(
        functools.partial(ema_back_ends, groups, comps, peers),
        [(meta, SMEM), (grad_blocks, hbm), (ema.value, VMEM), (decay_rows, VMEM)],
        Box(
            grad=((tiles, seq_rows, LANES), F32, VMEM), after=((tiles, comps, CHUNKS, LANES), F32, VMEM),
            first=((tiles, comps, LANES), F32, VMEM),
        ),
        Box(grad=pltpu.VMEM((tok_rows, width), BF), sem=sems((peers,))),
        after=[second_parts, first_parts],
        hides=HIDE_BACK,
    )
    later = group_totals(back.first, ends.fade, "seq", True)
    second_sum = shard_sum(second_parts)
    third_sum = shard_sum(third_rows, back)
    first_sum = keep_rows(first_parts, row_bits[0])
    last = run(
        functools.partial(ema_back, groups, comps, peers),
        [(meta, SMEM), (inputs, VMEM), (back.grad, VMEM), (rest_blocks, hbm), (decay_rows, VMEM), (mix_rows, VMEM), (skip_row, VMEM),
         (ema.start, VMEM), (back.after, VMEM), (later, VMEM)],
        Box(grad=((seqs, seq_rows, width), F32, VMEM), block=((seqs, seq_rows, width), BF, VMEM), sums=((2 * comps + 8, width), F32, VMEM)),
        Box(
            x=pltpu.VMEM((tiles, seq_rows, LANES), F32), y=pltpu.VMEM((tiles, seq_rows, LANES), F32),
            states=pltpu.VMEM((seq_rows // CHUNKS, comps, CHUNKS, LANES), F32), rest=pltpu.VMEM((tok_rows, 2 * width), BF),
            sem=sems((peers,)),
        ),
        after=[second_sum, first_sum],
        hides=HIDE_LAST,
    )

    second_rows = keep_rows(second_sum, row_bits[0], last)
    third_sum = keep_rows(third_sum, row_bits[1], last)
    first_rows = shard_sum(first_sum, last)
    totals = []
    for rows_left, bits in ((third_sum, row_bits[2:]), (second_rows, row_bits[1:]), (first_rows, row_bits[1:])):
        for bit in bits:
            rows_left = keep_rows(rows_left, bit)
        totals.append(all_rows(rows_left, row_bits))
    third_total, second_total, first_total = totals
    shard_sums = jnp.stack([ffn.up_bias[:, 0], one.bias[:, 0], two.bias[:, 0]], axis=1)
    shard_sums = shard_sums[me ^ lax.iota(jnp.int32, peers)]
    shard_tall = 3 * peers * units // Z

    tall = 16 * wide // Z
    small = [
        jnp.concatenate([ffn.sums, one.sums], axis=0).reshape(tall, Z), two.sums, two.rel.reshape(16, Z),
        shard_sums.reshape(shard_tall, Z),
    ]
    small += [mark.token, two.token, back.token, ema.token, ends.token, last.token]
    small.append(jnp.zeros((-sum(part.shape[0] for part in small) % 16, Z), F32))
    small = jnp.concatenate(small, axis=0)
    small, zeta_grad = sum_small(small, two.zeta, [("wa", bit) for bit in bits_of(peers)])
    count = small.shape[0]
    small = jnp.concatenate([small, last.sums.reshape(-1, Z)])
    small, zeta_grad = sum_small(small, zeta_grad, [("seq", bit) for bit in row_bits])
    ema_sums = small[count:].reshape(last.sums.shape)
    decay_grad = ema_sums[:comps].T * (ema_feed * ema_read)
    moment = ema_sums[comps : 2 * comps].T
    feed_grad, read_grad = moment * ema_read, moment * ema_feed
    skip_grad = ema_sums[2 * comps]

    lines = small[:tall].reshape(16, wide)
    zsums = small[tall : tall + 8]
    rel_grad = small[tall + 8 : tall + 10].reshape(2 * GROUP)[: rel_bias.shape[0]]
    shard_sums = small[tall + 24 : tall + 24 + shard_tall].reshape(peers, 3, units)[me]

    up_grad = jnp.concatenate([third_total[:depth, j * hidden : (j + 1) * hidden] for j in range(fold)], axis=0)
    return (
        last.block, last.grad, lines[5, 0] + last.token[0, 0], decay_grad, feed_grad, read_grad, skip_grad, zeta_grad, zsums[0], zsums[1], zsums[2],
        zsums[3], rel_grad, first_total[:, :units].astype(F32), shard_sums[1], first_total[:, units:].astype(F32), shard_sums[2],
        second_total[:width].astype(F32), lines[9], second_total[width : 2 * width].astype(F32), second_total[2 * width :].astype(F32), lines[8], lines[3],
        lines[4], up_grad.astype(F32), shard_sums[0], third_total[depth:].astype(F32), lines[2], lines[0], lines[1],
    )


def solution(mesh):
    return jax.shard_map(
        per_device,
        mesh=mesh,
        in_specs=(
            P(None, "seq", "wa"), P(None, "seq", None), P(), P(None, "seq"), P("wa", None), P("wa", None), P("wa", None), P("wa"),
            P(), P(), P(), P(), P(), P(), P(None, "wa"), P("wa"), P(None, "wa"), P("wa"), P("wa", None), P(), P("wa", None),
            P("wa", None), P(), P(), P(), P(None, "wa"), P("wa"), P("wa", None), P(), P(), P(),
        ),
        out_specs=(
            P(None, "seq", "wa"), P(None, "seq", "wa"), P(), P("wa", None), P("wa", None), P("wa", None), P("wa"), P(), P(), P(),
            P(), P(), P(), P(None, "wa"), P("wa"), P(None, "wa"), P("wa"), P("wa", None), P(), P("wa", None), P("wa", None), P(),
            P(), P(), P(None, "wa"), P("wa"), P("wa", None), P(), P(), P(),
        ),
        check_vma=False,
    )
```

time: 1090 us -> 370 us (0.34)
  blocking collectives: 244 us -> 0 us
  other arithmetic: 270 us -> 31 us
  matrix products: 157 us -> 0 us
  local copies, waits for them, and re-layouts: 183 us -> 40.8 us
  Pallas kernels: 0 us -> 86 us
  waiting for transfers between devices: 206 us -> 158 us
  starting transfers between devices: 0.7 us -> 48.6 us
  between operations: 17.8 us -> 4.59 us
    ppermute x0 -> x62, waiting for transfers between devices: none -> 158 us  [swap(): return lax.ppermute(x, axis, [(i, i ^ by) for i in range(size)])]
    dot_general x46 -> x0, matrix products: 157 us -> none  [the longest x8 70.2 us: pick_bias(): return jnp.einsum('qkb,b->qk', hits, rel_bias, precision=HIGHEST)]
    add x22 -> x7, other arithmetic: 146 us -> 0.37 us  [the longest x5 0.34 us: sum_small(): total = sent.astype(F32) + swap(sent, axis, bit).astype(F32)]
    psum x3 -> x0, waiting for transfers between devices: 137 us -> none  [the longest x1 112 us: per_device(): mixer_sum, update_sum = lax.psum((mixer_part, update_part), 'wa')]
    all_gather x5 -> x0, blocking collectives: 130 us -> none  [the longest x4 125 us: carried_in(): everything = jax.tree.map(lambda part: lax.all_gather(part, axis), x)]
    psum x1 -> x0, blocking collectives: 108 us -> none  [per_device(): lax.psum((decay_grad, feed_grad, read_grad, skip_grad, zeta_grad, zbias_g...]
    slice x17 -> x22, local copies, waits for them, and re-layouts: 110 us -> 4.26 us  [the longest x3 0.97 us: shard_sum(): parts = plus(parts[::2], later_than(swap(parts[1::2], 'wa', step), *deps))]
    reduce_sum x21 -> x0, other arithmetic: 87.8 us -> none  [the longest x1 18.7 us: per_device(): jnp.sum(state_grads * inputs_spread, axis=(0, 1))]
  transfers between devices with their start and end apart: 13 -> 62, of which waited for: 5 -> 27; matrix products, arithmetic and copies ran while one was open for 41% -> 10% of each run, Pallas kernels for 0% -> 18%
where the time goes in v1:
time: 370 us; the launch traced here: 369 us
  waiting for transfers between devices  158 us (43%)
  Pallas kernels  86 us (23%)
  starting transfers between devices  48.6 us (13%)
  local copies, waits for them, and re-layouts  40.8 us (11%)
  other arithmetic  31 us (8%)
  between operations  4.59 us (1%)
    ppermute x62, waiting for transfers between devices, swap(): return lax.ppermute(x, axis, [(i, i ^ by) for i in range(size)])  158 us
    pallas_call x12, Pallas kernels, run(): pl.pallas_call(kernel, out_shape=(shapes,), in_specs=specs, out_specs=(ou...  86 us
    ppermute x62, starting transfers between devices, swap(): return lax.ppermute(x, axis, [(i, i ^ by) for i in range(size)])  48.6 us
    unnamed x201, local copies, waits for them, and re-layouts  28.4 us
    convert_element_type x15, other arithmetic, plus(): return (a.astype(F32) + b.astype(F32)).astype(a.dtype)  17.5 us
  transfers between devices with their start and end apart: 62, of which 27 were waited for; matrix products, arithmetic and copies ran while one was open for 10% of the time, Pallas kernels for 18%

profile of v1, /device:TPU:0, one launch (start us, length us, event | category | flops | bytes accessed | tf_op | source)
XLA Modules:
  0.0 368.8 jit_solution(10084774210576915018)
XLA Ops:
  7.6 3.0 collective-permute-start.6
  11.8 3.0 shard_map.527
  18.7 5.7 %collective-permute-done.6.refs_3__2__0_.refs_1__2__0_ = bf16[400,768]{1,0:T(8,128)(2,1)S(1)} collective-permute-done((bf16[400,768]{1,0:T(8,128)(2,1)S(1)}, bf16[400,768]{1,0:T(8,128)(2,1)S(1)}, u32[]{:S(2)}, u32[]{:S(2)}) %collective-permute-start.6) | collective-permute-done | bytes 614432 | tf_op jit(solution)/shard_map/ppermute | solution.py:774
  31.6 2.7 collective-permute-start.2
  36.5 8.1 %collective-permute-done.4.refs_2__2_ = bf16[256,192]{1,0:T(8,128)(2,1)S(1)} collective-permute-done((bf16[256,192]{1,0:T(8,128)(2,1)S(1)}, bf16[256,192]{1,0:T(8,128)(2,1)S(1)}, u32[]{:S(2)}, u32[]{:S(2)}) %collective-permute-start.4) | collective-permute-done | bytes 98336 | tf_op jit(solution)/shard_map/ppermute | solution.py:774
  47.6 4.5 %shard_map.530 = (f32[2,512,192]{2,1,0:T(8,128)S(1)}, f32[3,16,8,128]{3,2,1,0:T(8,128)S(1)}, bf16[256,192]{1,0:T(8,128)(2,1)S(1)}, bf16[256,192]{1,0:T(8,128)(2,...) custom-call(s32[3]{0:T(128)S(1)} %pad_add_fusion.refs_0_, ...), custom_call_target="tpu_custom_call" | custom-call | flops 23000000512 | bytes 1 | tf_op jit(solution)/shard_map/pallas_call | solution.py:109
  64.7 11.0 %collective-permute-done.16.refs_4__2__1_.refs_1__2__1_ = bf16[384,768]{1,0:T(8,128)(2,1)S(1)} collective-permute-done((bf16[384,768]{1,0:T(8,128)(2,1)S(1)}, bf16[384,768]{1,0:T(8,128)(2,1)S(1)}, u32[]{:S(2)}, u32[]{:S(2)}) %collective-permute-start.16) | collective-permute-done | bytes 589856 | tf_op jit(solution)/shard_map/ppermute | solution.py:774
  79.5 14.4 %collective-permute-done.21.refs_2__2__1_ = bf16[384,768]{1,0:T(8,128)(2,1)S(1)} collective-permute-done((bf16[384,768]{1,0:T(8,128)(2,1)}, bf16[384,768]{1,0:T(8,128)(2,1)S(1)}, u32[]{:S(2)}, u32[]{:S(2)}) %collective-permute-start.21) | collective-permute-done | bytes 589856 | tf_op jit(solution)/shard_map/ppermute | solution.py:774
  96.1 13.9 %shard_map.531 = (bf16[256,768]{1,0:T(8,128)(2,1)}, bf16[256,768]{1,0:T(8,128)(2,1)}, f32[256,128]{1,0:T(8,128)}, bf16[256,128]{1,0:T(8,128)(2,1)}, bf16[256,128...) custom-call(s32[3]{0:T(128)} %copy-done.48, ...), custom_call_target="tpu_custom_call" | custom-call | flops 1 | bytes 1 | tf_op jit(solution)/shard_map/pallas_call | solution.py:109
  112.9 14.8 %shard_map.532 = (f32[256,768]{1,0:T(8,128)S(1)}, bf16[4,256,192]{2,1,0:T(8,128)(2,1)S(1)}, f32[8,768]{1,0:T(8,128)S(1)}, f32[4,8,384]{2,1,0:T(8,128)S(1)}, bf16...) custom-call(s32[3]{0:T(128)S(1)} %copy-done.49, s32[2]{0:T(128)S(1)} %copy-done.63, ...), custom_call_target="tpu_custom_call" | custom-call | flops 1 | bytes 1 | tf_op jit(solution)/shard_map/pallas_call | solution.py:109
  129.3 4.5 %collective-permute-done.24 = bf16[2,768,768]{2,1,0:T(8,128)(2,1)} collective-permute-done((bf16[2,768,768]{2,1,0:T(8,128)(2,1)}, bf16[2,768,768]{2,1,0:T(8,128)(2,1)}, u32[]{:S(2)}, u32[]{:S(2)}) %collective-permute-start.24) | collective-permute-done | bytes 2359328 | tf_op jit(solution)/shard_map/ppermute | solution.py:774
  133.7 3.0 add_convert_fusion.2.refs_11__0_
  139.7 11.8 %shard_map.533 = (f32[256,768]{1,0:T(8,128)S(1)}, f32[8,768]{1,0:T(8,128)S(1)}, f32[4,256,192]{2,1,0:T(8,128)}, bf16[4,256,384]{2,1,0:T(8,128)(2,1)S(1)}, bf16[4...) custom-call(s32[3]{0:T(128)S(1)} %copy-done.49, ...), custom_call_target="tpu_custom_call" | custom-call | flops 23000000512 | bytes 1 | tf_op jit(solution)/shard_map/pallas_call | solution.py:109
  154.2 17.2 %shard_map.534 = (f32[8,256]{1,0:T(8,128)S(1)}, f32[8,128]{1,0:T(8,128)S(1)}, f32[768,128]{1,0:T(8,128)S(1)}, f32[4,8,384]{2,1,0:T(8,128)S(1)}, bf16[2,768,768]{...) custom-call(s32[3]{0:T(128)S(1)} %copy-done.49, ...), custom_call_target="tpu_custom_call" | custom-call | flops 1 | bytes 1 | tf_op jit(solution)/shard_map/pallas_call | solution.py:109
  192.5 3.5 shard_map.536
  196.0 9.9 %collective-permute-done.39 = bf16[1,384,768]{2,1,0:T(8,128)(2,1)S(1)} collective-permute-done((bf16[1,384,768]{2,1,0:T(8,128)(2,1)S(1)}, bf16[1,384,768]{2,1,0:T(8,128)(2,1)S(1)}, u32[]{:S(2)}, u32[]{:S(2)}) %collective-permute-start.39) | collective-permute-done | bytes 589856 | tf_op jit(solution)/shard_map/ppermute | solution.py:774
  206.8 12.6 %collective-permute-done.33.refs_9__0_ = f32[3,16,128]{2,1,0:T(8,128)S(1)} collective-permute-done((f32[3,16,128]{2,1,0:T(8,128)S(1)}, f32[3,16,128]{2,1,0:T(8,128)S(1)}, u32[]{:S(2)}, u32[]{:S(2)}) %collective-permute-start.33) | collective-permute-done | bytes 24608 | tf_op jit(solution)/shard_map/ppermute | solution.py:774
  223.3 7.8 %collective-permute-done.36 = bf16[1,768,768]{2,1,0:T(8,128)(2,1)S(1)} collective-permute-done((bf16[1,768,768]{2,1,0:T(8,128)(2,1)S(1)}, bf16[1,768,768]{2,1,0:T(8,128)(2,1)S(1)}, u32[]{:S(2)}, u32[]{:S(2)}) %collective-permute-start.36) | collective-permute-done | bytes 1179680 | tf_op jit(solution)/shard_map/ppermute | solution.py:774
  233.0 2.7 collective-permute-start.35
  235.7 2.6 add_convert_fusion.4.refs_11__1_
  240.0 13.0 %shard_map.537 = (f32[2,512,192]{2,1,0:T(8,128)S(1)}, bf16[2,512,192]{2,1,0:T(8,128)(2,1)S(1)}, f32[40,192]{1,0:T(8,128)S(1)}, f32[8,128]{1,0:T(8,128)S(1)}) custom-call(s32[3]{0:T(128)S(1)} %copy-done.49, bf16[2,512,192]{2,1,0:T(8,128)(2,1)S(1)} %copy-done.31, f32[3,512,128]{2,1,0:T(8,128)S(1)} %get-tuple-element.220.refs_2_, ...), custom_call_target="tpu_custom_call" | custom-call | flops 17250000896 | bytes 1 | tf_op jit(solution)/shard_map/pallas_call | solution.py:109
  261.2 6.9 %collective-permute-done.40 = bf16[1,384,768]{2,1,0:T(8,128)(2,1)} collective-permute-done((bf16[1,384,768]{2,1,0:T(8,128)(2,1)}, bf16[1,384,768]{2,1,0:T(8,128)(2,1)}, u32[]{:S(2)}, u32[]{:S(2)}) %collective-permute-start.40) | collective-permute-done | bytes 589856 | tf_op jit(solution)/shard_map/ppermute | solution.py:774
  272.7 2.6 collective-permute-start.54
  275.3 3.9 %collective-permute-done.48 = bf16[192,768]{1,0:T(8,128)(2,1)S(1)} collective-permute-done((bf16[192,768]{1,0:T(8,128)(2,1)S(1)}, bf16[192,768]{1,0:T(8,128)(2,1)S(1)}, u32[]{:S(2)}, u32[]{:S(2)}) %collective-permute-start.48) | collective-permute-done | bytes 294944 | tf_op jit(solution)/shard_map/ppermute | solution.py:774
  280.4 11.1 %collective-permute-done.54 = bf16[96,768]{1,0:T(8,128)(2,1)S(1)} collective-permute-done((bf16[96,768]{1,0:T(8,128)(2,1)S(1)}, bf16[96,768]{1,0:T(8,128)(2,1)S(1)}, u32[]{:S(2)}, u32[]{:S(2)}) %collective-permute-start.54) | collective-permute-done | bytes 147488 | tf_op jit(solution)/shard_map/ppermute | solution.py:774
  291.6 9.4 %collective-permute-done.49 = bf16[96,768]{1,0:T(8,128)(2,1)S(1)} collective-permute-done((bf16[96,768]{1,0:T(8,128)(2,1)S(1)}, bf16[96,768]{1,0:T(8,128)(2,1)S(1)}, u32[]{:S(2)}, u32[]{:S(2)}) %collective-permute-start.49) | collective-permute-done | bytes 147488 | tf_op jit(solution)/shard_map/ppermute | solution.py:774
  301.2 2.5 collective-permute-done.55
  303.9 3.3 collective-permute-done.50
  309.6 3.7 %collective-permute-done.60 = bf16[192,768]{1,0:T(8,128)(2,1)S(1)} collective-permute-done((bf16[192,768]{1,0:T(8,128)(2,1)S(1)}, bf16[192,768]{1,0:T(8,128)(2,1)S(1)}, u32[]{:S(2)}, u32[]{:S(2)}) %collective-permute-start.60) | collective-permute-done | bytes 294944 | tf_op jit(solution)/shard_map/ppermute | solution.py:774
  315.4 10.4 %collective-permute-done.51 = bf16[192,768]{1,0:T(8,128)(2,1)S(1)} collective-permute-done((bf16[192,768]{1,0:T(8,128)(2,1)S(1)}, bf16[192,768]{1,0:T(8,128)(2,1)S(1)}, u32[]{:S(2)}, u32[]{:S(2)}) %collective-permute-start.51) | collective-permute-done | bytes 294944 | tf_op jit(solution)/shard_map/ppermute | solution.py:774
  332.9 5.3 %collective-permute-done.46 = bf16[1304,128]{1,0:T(8,128)(2,1)S(1)} collective-permute-done((bf16[1304,128]{1,0:T(8,128)(2,1)S(1)}, bf16[1304,128]{1,0:T(8,128)(2,1)S(1)}, u32[]{:S(2)}, u32[]{:S(2)}) %collective-permute-start.46) | collective-permute-done | bytes 333856 | tf_op jit(solution)/shard_map/ppermute | solution.py:774
  338.9 15.3 %collective-permute-done.57 = bf16[384,768]{1,0:T(8,128)(2,1)} collective-permute-done((bf16[384,768]{1,0:T(8,128)(2,1)S(1)}, bf16[384,768]{1,0:T(8,128)(2,1)}, u32[]{:S(2)}, u32[]{:S(2)}) %collective-permute-start.57) | collective-permute-done | bytes 589856 | tf_op jit(solution)/shard_map/ppermute | solution.py:774
  (407 shorter events, 120.4 us)
Async XLA Ops:
  7.6 16.8 %collective-permute-start.6 = (bf16[400,768]{1,0:T(8,128)(2,1)S(1)}, bf16[400,768]{1,0:T(8,128)(2,1)S(1)}, u32[]{:S(2)}, u32[]{:S(2)}) collective-permute-start(bf16[400,768]{1,0:T(8,128)(2,1)S(1)} %get-tuple-element.142.refs_4__0_), channel_id=1, source_target_pairs={{0,2},{1,3},{2,0},{3,1},{4,6},{5,7},{6,4},{7,5},{8,10},{9,11},{10,... | collective-permute-start | bytes 1843208 | tf_op jit(solution)/shard_map/ppermute | solution.py:774
  24.4 20.6 %collective-permute-start.8 = (bf16[400,768]{1,0:T(8,128)(2,1)S(1)}, bf16[400,768]{1,0:T(8,128)(2,1)S(1)}, u32[]{:S(2)}, u32[]{:S(2)}) collective-permute-start(bf16[400,768]{1,0:T(8,128)(2,1)S(1)} %collective-permute-done.6.refs_3__2__0_.refs_1__2__0_), channel_id=1, source_target_pairs={{0,4},{4,0},{8,12},{12,8},{16,20},{20,16},{24,28},{28,24},{1,5},{5... | collective-permute-start | bytes 1843208 | tf_op jit(solution)/shard_map/ppermute | solution.py:774
  26.2 18.8 %collective-permute-start.7 = (bf16[384,768]{1,0:T(8,128)(2,1)}, bf16[384,768]{1,0:T(8,128)(2,1)S(1)}, u32[]{:S(2)}, u32[]{:S(2)}) collective-permute-start(bf16[384,768]{1,0:T(8,128)(2,1)} %copy-done.65), channel_id=1, source_target_pairs={{0,2},{1,3},{2,0},{3,1},{4,6},{5,7},{6,4},{7,5},{8,10},{9,11},{10,... | collective-permute-start | bytes 1769480 | tf_op jit(solution)/shard_map/ppermute | solution.py:774
  57.4 18.3 %collective-permute-start.14 = (bf16[400,768]{1,0:T(8,128)(2,1)S(1)}, bf16[400,768]{1,0:T(8,128)(2,1)S(1)}, u32[]{:S(2)}, u32[]{:S(2)}) collective-permute-start(bf16[400,768]{1,0:T(8,128)(2,1)S(1)} %collective-permute-done.8.refs_8__1_.refs_3__2__1_.refs_1__2__1_), channel_id=1, source_target_pairs={{0,1},{1,0},{2,3},{3,2},{4,5},{5,4},{6,7},{7,6},{8,9},{9,8},{10,11... | collective-permute-start | bytes 1843208 | tf_op jit(solution)/shard_map/ppermute | solution.py:774
  62.5 16.1 %collective-permute-start.20 = (bf16[384,768]{1,0:T(8,128)(2,1)S(1)}, bf16[384,768]{1,0:T(8,128)(2,1)}, u32[]{:S(2)}, u32[]{:S(2)}) collective-permute-start(bf16[384,768]{1,0:T(8,128)(2,1)S(1)} %get-tuple-element.187), channel_id=1, source_target_pairs={{0,2},{1,3},{2,0},{3,1},{4,6},{5,7},{6,4},{7,5},{8,10},{9,11},{10,... | collective-permute-start | bytes 1769480 | tf_op jit(solution)/shard_map/ppermute | solution.py:774
  64.0 29.9 %collective-permute-start.12 = (bf16[800,768]{1,0:T(8,128)(2,1)S(1)}, bf16[800,768]{1,0:T(8,128)(2,1)S(1)}, u32[]{:S(2)}, u32[]{:S(2)}) collective-permute-start(bf16[800,768]{1,0:T(8,128)(2,1)S(1)} %get-tuple-element.170.refs_3__0__0_.refs_1__0__0_), channel_id=1, source_target_pairs={{0,1},{1,0},{2,3},{3,2},{4,5},{5,4},{6,7},{7,6},{8,9},{9,8},{10,11... | collective-permute-start | bytes 3686408 | tf_op jit(solution)/shard_map/ppermute | solution.py:774
  64.6 29.3 %collective-permute-start.15 = (bf16[768,768]{1,0:T(8,128)(2,1)S(1)}, bf16[768,768]{1,0:T(8,128)(2,1)S(1)}, u32[]{:S(2)}, u32[]{:S(2)}) collective-permute-start(bf16[768,768]{1,0:T(8,128)(2,1)S(1)} %copy-done.10), channel_id=1, source_target_pairs={{0,1},{1,0},{2,3},{3,2},{4,5},{5,4},{6,7},{7,6},{8,9},{9,8},{10,11... | collective-permute-start | bytes 3538952 | tf_op jit(solution)/shard_map/ppermute | solution.py:774
  75.7 34.3 %collective-permute-start.19 = (bf16[768,768]{1,0:T(8,128)(2,1)}, bf16[768,768]{1,0:T(8,128)(2,1)}, u32[]{:S(2)}, u32[]{:S(2)}) collective-permute-start(bf16[768,768]{1,0:T(8,128)(2,1)} %get-tuple-element.186.refs_2__0__0_), channel_id=1, source_target_pairs={{0,1},{1,0},{2,3},{3,2},{4,5},{5,4},{6,7},{7,6},{8,9},{9,8},{10,11... | collective-permute-start | bytes 3538952 | tf_op jit(solution)/shard_map/ppermute | solution.py:774
  79.4 30.6 %collective-permute-start.22 = (bf16[384,768]{1,0:T(8,128)(2,1)}, bf16[384,768]{1,0:T(8,128)(2,1)S(1)}, u32[]{:S(2)}, u32[]{:S(2)}) collective-permute-start(bf16[384,768]{1,0:T(8,128)(2,1)} %collective-permute-done.20.refs_2__2__0_), channel_id=1, source_target_pairs={{0,1},{1,0},{2,3},{3,2},{4,5},{5,4},{6,7},{7,6},{8,9},{9,8},{10,11... | collective-permute-start | bytes 1769480 | tf_op jit(solution)/shard_map/ppermute | solution.py:774
  93.9 16.1 %collective-permute-start.23 = (bf16[384,768]{1,0:T(8,128)(2,1)S(1)}, bf16[384,768]{1,0:T(8,128)(2,1)}, u32[]{:S(2)}, u32[]{:S(2)}) collective-permute-start(bf16[384,768]{1,0:T(8,128)(2,1)S(1)} %collective-permute-done.21.refs_2__2__1_), channel_id=1, source_target_pairs={{0,1},{1,0},{2,3},{3,2},{4,5},{5,4},{6,7},{7,6},{8,9},{9,8},{10,11... | collective-permute-start | bytes 1769480 | tf_op jit(solution)/shard_map/ppermute | solution.py:774
  138.6 36.9 %collective-permute-start.38 = (bf16[2,384,768]{2,1,0:T(8,128)(2,1)}, bf16[2,384,768]{2,1,0:T(8,128)(2,1)}, u32[]{:S(2)}, u32[]{:S(2)}) collective-permute-start(bf16[2,384,768]{2,1,0:T(8,128)(2,1)} %constant_dynamic-slice_fusion.7), channel_id=1, source_target_pairs={{0,4},{4,0},{8,12},{12,8},{16,20},{20,16},{24,28},{28,24},{1,5},{5... | collective-permute-start | bytes 3538952 | tf_op jit(solution)/shard_map/ppermute | solution.py:774
  172.8 16.9 %collective-permute-start.25 = (bf16[256,192]{1,0:T(8,128)(2,1)S(1)}, bf16[256,192]{1,0:T(8,128)(2,1)S(1)}, u32[]{:S(2)}, u32[]{:S(2)}) collective-permute-start(bf16[256,192]{1,0:T(8,128)(2,1)S(1)} %get-tuple-element.208), channel_id=1, source_target_pairs={{0,1},{1,0},{2,3},{3,2},{4,5},{5,4},{6,7},{7,6},{8,9},{9,8},{10,11... | collective-permute-start | bytes 294920 | tf_op jit(solution)/shard_map/ppermute | solution.py:774
  173.2 16.9 %collective-permute-start.26 = (bf16[256,192]{1,0:T(8,128)(2,1)S(1)}, bf16[256,192]{1,0:T(8,128)(2,1)S(1)}, u32[]{:S(2)}, u32[]{:S(2)}) collective-permute-start(bf16[256,192]{1,0:T(8,128)(2,1)S(1)} %get-tuple-element.209), channel_id=1, source_target_pairs={{0,2},{1,3},{2,0},{3,1},{4,6},{5,7},{6,4},{7,5},{8,10},{9,11},{10,... | collective-permute-start | bytes 294920 | tf_op jit(solution)/shard_map/ppermute | solution.py:774
  175.5 16.2 %collective-permute-start.27 = (bf16[256,192]{1,0:T(8,128)(2,1)S(1)}, bf16[256,192]{1,0:T(8,128)(2,1)S(1)}, u32[]{:S(2)}, u32[]{:S(2)}) collective-permute-start(bf16[256,192]{1,0:T(8,128)(2,1)S(1)} %get-tuple-element.210), channel_id=1, source_target_pairs={{0,3},{1,2},{2,1},{3,0},{4,7},{5,6},{6,5},{7,4},{8,11},{9,10},{10,... | collective-permute-start | bytes 294920 | tf_op jit(solution)/shard_map/ppermute | solution.py:774
  180.0 59.2 %collective-permute-start.30 = (bf16[256,384]{1,0:T(8,128)(2,1)S(1)}, bf16[256,384]{1,0:T(8,128)(2,1)S(1)}, u32[]{:S(2)}, u32[]{:S(2)}) collective-permute-start(bf16[256,384]{1,0:T(8,128)(2,1)S(1)} %get-tuple-element.222), channel_id=1, source_target_pairs={{0,1},{1,0},{2,3},{3,2},{4,5},{5,4},{6,7},{7,6},{8,9},{9,8},{10,11... | collective-permute-start | bytes 589832 | tf_op jit(solution)/shard_map/ppermute | solution.py:774
  180.4 59.6 %collective-permute-start.31 = (bf16[256,384]{1,0:T(8,128)(2,1)S(1)}, bf16[256,384]{1,0:T(8,128)(2,1)S(1)}, u32[]{:S(2)}, u32[]{:S(2)}) collective-permute-start(bf16[256,384]{1,0:T(8,128)(2,1)S(1)} %get-tuple-element.223), channel_id=1, source_target_pairs={{0,2},{1,3},{2,0},{3,1},{4,6},{5,7},{6,4},{7,5},{8,10},{9,11},{10,... | collective-permute-start | bytes 589832 | tf_op jit(solution)/shard_map/ppermute | solution.py:774
  189.6 16.2 %collective-permute-start.39 = (bf16[1,384,768]{2,1,0:T(8,128)(2,1)S(1)}, bf16[1,384,768]{2,1,0:T(8,128)(2,1)S(1)}, u32[]{:S(2)}, u32[]{:S(2)}) collective-permute-start(bf16[1,384,768]{2,1,0:T(8,128)(2,1)S(1)} %slice.270), channel_id=1, source_target_pairs={{0,2},{1,3},{2,0},{3,1},{4,6},{5,7},{6,4},{7,5},{8,10},{9,11},{10,... | collective-permute-start | bytes 1769480 | tf_op jit(solution)/shard_map/ppermute | solution.py:774
  190.1 41.0 %collective-permute-start.36 = (bf16[1,768,768]{2,1,0:T(8,128)(2,1)S(1)}, bf16[1,768,768]{2,1,0:T(8,128)(2,1)S(1)}, u32[]{:S(2)}, u32[]{:S(2)}) collective-permute-start(bf16[1,768,768]{2,1,0:T(8,128)(2,1)S(1)} %slice.269), channel_id=1, source_target_pairs={{0,2},{1,3},{2,0},{3,1},{4,6},{5,7},{6,4},{7,5},{8,10},{9,11},{10,... | collective-permute-start | bytes 3538952 | tf_op jit(solution)/shard_map/ppermute | solution.py:774
  191.7 41.4 %collective-permute-start.37 = (bf16[2,384,768]{2,1,0:T(8,128)(2,1)S(1)}, bf16[2,384,768]{2,1,0:T(8,128)(2,1)}, u32[]{:S(2)}, u32[]{:S(2)}) collective-permute-start(bf16[2,384,768]{2,1,0:T(8,128)(2,1)S(1)} %constant_dynamic-slice_fusion.8), channel_id=1, source_target_pairs={{0,4},{4,0},{8,12},{12,8},{16,20},{20,16},{24,28},{28,24},{1,5},{5... | collective-permute-start | bytes 3538952 | tf_op jit(solution)/shard_map/ppermute | solution.py:774
  223.3 16.7 %collective-permute-start.32 = (bf16[256,384]{1,0:T(8,128)(2,1)S(1)}, bf16[256,384]{1,0:T(8,128)(2,1)S(1)}, u32[]{:S(2)}, u32[]{:S(2)}) collective-permute-start(bf16[256,384]{1,0:T(8,128)(2,1)S(1)} %get-tuple-element.224), channel_id=1, source_target_pairs={{0,3},{1,2},{2,1},{3,0},{4,7},{5,6},{6,5},{7,4},{8,11},{9,10},{10,... | collective-permute-start | bytes 589832 | tf_op jit(solution)/shard_map/ppermute | solution.py:774
  231.1 25.5 %collective-permute-start.41 = (bf16[192,768]{1,0:T(8,128)(2,1)}, bf16[192,768]{1,0:T(8,128)(2,1)}, u32[]{:S(2)}, u32[]{:S(2)}) collective-permute-start(bf16[192,768]{1,0:T(8,128)(2,1)} %dynamic-slice_bitcast_fusion.2), channel_id=1, source_target_pairs={{0,8},{4,12},{8,0},{12,4},{16,24},{20,28},{24,16},{28,20},{1,9},{5... | collective-permute-start | bytes 884744 | tf_op jit(solution)/shard_map/ppermute | solution.py:774
  239.2 17.5 %collective-permute-start.42 = (bf16[384,768]{1,0:T(8,128)(2,1)}, bf16[384,768]{1,0:T(8,128)(2,1)}, u32[]{:S(2)}, u32[]{:S(2)}) collective-permute-start(bf16[384,768]{1,0:T(8,128)(2,1)} %dynamic-slice_bitcast_fusion), channel_id=1, source_target_pairs={{0,4},{4,0},{8,12},{12,8},{16,20},{20,16},{24,28},{28,24},{1,5},{5... | collective-permute-start | bytes 1769480 | tf_op jit(solution)/shard_map/ppermute | solution.py:774
  271.2 29.9 %collective-permute-start.59 = (bf16[96,768]{1,0:T(8,128)(2,1)S(1)}, bf16[96,768]{1,0:T(8,128)(2,1)S(1)}, u32[]{:S(2)}, u32[]{:S(2)}) collective-permute-start(bf16[96,768]{1,0:T(8,128)(2,1)S(1)} %add_convert_fusion.9), channel_id=1, source_target_pairs={{0,16},{4,20},{8,24},{12,28},{16,0},{20,4},{24,8},{28,12},{1,17},{... | collective-permute-start | bytes 442376 | tf_op jit(solution)/shard_map/ppermute | solution.py:774
  272.7 18.8 %collective-permute-start.54 = (bf16[96,768]{1,0:T(8,128)(2,1)S(1)}, bf16[96,768]{1,0:T(8,128)(2,1)S(1)}, u32[]{:S(2)}, u32[]{:S(2)}) collective-permute-start(bf16[96,768]{1,0:T(8,128)(2,1)S(1)} %constant_dynamic-slice_fusion.3), channel_id=1, source_target_pairs={{0,16},{4,20},{8,24},{12,28},{16,0},{20,4},{24,8},{28,12},{1,17},{... | collective-permute-start | bytes 442376 | tf_op jit(solution)/shard_map/ppermute | solution.py:774
  279.3 21.7 %collective-permute-start.49 = (bf16[96,768]{1,0:T(8,128)(2,1)S(1)}, bf16[96,768]{1,0:T(8,128)(2,1)S(1)}, u32[]{:S(2)}, u32[]{:S(2)}) collective-permute-start(bf16[96,768]{1,0:T(8,128)(2,1)S(1)} %constant_dynamic-slice_fusion.6), channel_id=1, source_target_pairs={{0,16},{4,20},{8,24},{12,28},{16,0},{20,4},{24,8},{28,12},{1,17},{... | collective-permute-start | bytes 442376 | tf_op jit(solution)/shard_map/ppermute | solution.py:774
  279.6 27.8 %collective-permute-start.44 = (bf16[1184,128]{1,0:T(8,128)(2,1)S(1)}, bf16[1184,128]{1,0:T(8,128)(2,1)S(1)}, u32[]{:S(2)}, u32[]{:S(2)}) collective-permute-start(bf16[1184,128]{1,0:T(8,128)(2,1)S(1)} %pad_maximum_fusion.1), channel_id=1, source_target_pairs={{0,2},{1,3},{2,0},{3,1},{4,6},{5,7},{6,4},{7,5},{8,10},{9,11},{10,... | collective-permute-start | bytes 909320 | tf_op jit(solution)/shard_map/ppermute | solution.py:774
  303.8 23.9 %collective-permute-start.56 = (bf16[192,768]{1,0:T(8,128)(2,1)S(1)}, bf16[192,768]{1,0:T(8,128)(2,1)S(1)}, u32[]{:S(2)}, u32[]{:S(2)}) collective-permute-start(bf16[192,768]{1,0:T(8,128)(2,1)S(1)} %maximum_select_fusion.7), channel_id=1, source_target_pairs={{0,8},{4,12},{8,0},{12,4},{16,24},{20,28},{24,16},{28,20},{1,9},{5... | collective-permute-start | bytes 884744 | tf_op jit(solution)/shard_map/ppermute | solution.py:774
  307.2 18.6 %collective-permute-start.51 = (bf16[192,768]{1,0:T(8,128)(2,1)S(1)}, bf16[192,768]{1,0:T(8,128)(2,1)S(1)}, u32[]{:S(2)}, u32[]{:S(2)}) collective-permute-start(bf16[192,768]{1,0:T(8,128)(2,1)S(1)} %maximum_select_fusion.6), channel_id=1, source_target_pairs={{0,8},{4,12},{8,0},{12,4},{16,24},{20,28},{24,16},{28,20},{1,9},{5... | collective-permute-start | bytes 884744 | tf_op jit(solution)/shard_map/ppermute | solution.py:774
  307.9 20.4 %collective-permute-start.45 = (bf16[1304,128]{1,0:T(8,128)(2,1)S(1)}, bf16[1304,128]{1,0:T(8,128)(2,1)S(1)}, u32[]{:S(2)}, u32[]{:S(2)}) collective-permute-start(bf16[1304,128]{1,0:T(8,128)(2,1)S(1)} %concatenate.86), channel_id=1, source_target_pairs={{0,4},{4,0},{8,12},{12,8},{16,20},{20,16},{24,28},{28,24},{1,5},{5... | collective-permute-start | bytes 1001480 | tf_op jit(solution)/shard_map/ppermute | solution.py:774
  326.0 32.0 %collective-permute-start.52 = (bf16[384,768]{1,0:T(8,128)(2,1)S(1)}, bf16[384,768]{1,0:T(8,128)(2,1)}, u32[]{:S(2)}, u32[]{:S(2)}) collective-permute-start(bf16[384,768]{1,0:T(8,128)(2,1)S(1)} %maximum_select_fusion.3), channel_id=1, source_target_pairs={{0,4},{4,0},{8,12},{12,8},{16,20},{20,16},{24,28},{28,24},{1,5},{5... | collective-permute-start | bytes 1769480 | tf_op jit(solution)/shard_map/ppermute | solution.py:774
  327.9 26.3 %collective-permute-start.57 = (bf16[384,768]{1,0:T(8,128)(2,1)S(1)}, bf16[384,768]{1,0:T(8,128)(2,1)}, u32[]{:S(2)}, u32[]{:S(2)}) collective-permute-start(bf16[384,768]{1,0:T(8,128)(2,1)S(1)} %maximum_select_fusion.4), channel_id=1, source_target_pairs={{0,4},{4,0},{8,12},{12,8},{16,20},{20,16},{24,28},{28,24},{1,5},{5... | collective-permute-start | bytes 1769480 | tf_op jit(solution)/shard_map/ppermute | solution.py:774
  338.9 22.3 %collective-permute-start.47 = (bf16[1304,128]{1,0:T(8,128)(2,1)S(1)}, bf16[1304,128]{1,0:T(8,128)(2,1)S(1)}, u32[]{:S(2)}, u32[]{:S(2)}) collective-permute-start(bf16[1304,128]{1,0:T(8,128)(2,1)S(1)} %concatenate.88), channel_id=1, source_target_pairs={{0,16},{4,20},{8,24},{12,28},{16,0},{20,4},{24,8},{28,12},{1,17},{... | collective-permute-start | bytes 1001480 | tf_op jit(solution)/shard_map/ppermute | solution.py:774
  (129 other events, 1204.3 us)

commit v2 on v1

--- a/solution.py
+++ b/solution.py
@@ -44,6 +44,12 @@
 
 def row(ref):
     return ref[...].reshape(1, ref.shape[0])
+
+
+def put_line(ref, at, line):
+    for j in range(0, line.shape[1], LANES):
+        piece = line[:, j : j + LANES]
+        ref[at + j // LANES : at + j // LANES + 1, : piece.shape[1]] = piece
 
 
 def colsum(v):
@@ -371,9 +377,8 @@
             out.first[g, n : n + 1, :] = total[:1]
 
 
-def ema_back(groups, comps, blocks, meta, x_ref, grad_ref, rests, decay_ref, mix_ref, skip_ref, start_ref, after_ref, got, out, s):
-    length = x_ref.shape[1] // CHUNKS
-    seqs, rows = x_ref.shape[0], x_ref.shape[1]
+def ema_join(groups, blocks, meta, part_ref, rests, out, s):
+    seqs, rows, width = out.grad.shape
     part = seqs * rows // blocks
     copies = [
         pltpu.make_async_copy(
@@ -383,6 +388,18 @@
     ]
     for copy in copies:
         copy.start()
+    for copy in copies:
+        copy.wait()
+    for q in range(seqs):
+        out.block[q] = s.rest[pl.ds(q * rows, rows), width:]
+    for g, group in enumerate(groups):
+        for q, c, w, lane in group:
+            rest = s.rest[pl.ds(q * rows, rows), c : c + w].astype(F32)
+            out.grad[q, :, c : c + w] = part_ref[g, :, lane : lane + w] + rest
+
+
+def ema_back(groups, comps, meta, x_ref, grad_ref, decay_ref, mix_ref, skip_ref, start_ref, after_ref, got, out, s):
+    length = x_ref.shape[1] // CHUNKS
     out.sums[...] = jnp.zeros_like(out.sums)
     half = comps // 2
     for g, group in enumerate(groups):
@@ -419,28 +436,19 @@
                     terms.append(skip * up)
                     skips = skips + up * now
                 else:
-                    terms.append(at_step(s.y, g, t, length)[...])
+                    terms.append(at_step(out.part, g, t, length)[...])
                 while len(terms) > 1:
                     terms = [a + b for a, b in zip(terms[::2], terms[1::2])] + (terms[-1:] if len(terms) % 2 else [])
-                at_step(s.y, g, t, length)[...] = terms[0]
+                at_step(out.part, g, t, length)[...] = terms[0]
                 return grads, moments, changes, skips
 
             _, moments, changes, skips = steps_of(length, backward, (tuple(begin), zero, zero, zero[0]), reverse=True, unroll=2)
             for q, c, w, lane in group:
                 for i, n in enumerate(mine):
-                    out.sums[n : n + 1, c : c + w] += colsum(changes[i])[:, lane : lane + w]
-                    out.sums[comps + n : comps + n + 1, c : c + w] += colsum(moments[i])[:, lane : lane + w]
+                    out.sums[c // LANES, n : n + 1, :w] += colsum(changes[i])[:, lane : lane + w]
+                    out.sums[c // LANES, comps + n : comps + n + 1, :w] += colsum(moments[i])[:, lane : lane + w]
                 if h == 0:
-                    out.sums[2 * comps : 2 * comps + 1, c : c + w] += colsum(skips)[:, lane : lane + w]
-    for copy in copies:
-        copy.wait()
-    width = x_ref.shape[2]
-    for q in range(seqs):
-        out.block[q] = s.rest[pl.ds(q * rows, rows), width:]
-    for g, group in enumerate(groups):
-        for q, c, w, lane in group:
-            rest = s.rest[pl.ds(q * rows, rows), c : c + w].astype(F32)
-            out.grad[q, :, c : c + w] = s.y[g, :, lane : lane + w] + rest
+                    out.sums[c // LANES, 2 * comps : 2 * comps + 1, :w] += colsum(skips)[:, lane : lane + w]
 
 
 def weight_copies(meta, shards, dst, sem, first):
@@ -598,21 +606,23 @@
     true_count = jnp.broadcast_to(tokens, (rows, 1)).astype(F32)
     losses = jnp.sum(misfit * misfit, axis=1, keepdims=True) * (weight / (2.0 * width * true_count))
     out.sums[...] = jnp.zeros_like(out.sums)
-    out.sums[5:6, :] = jnp.broadcast_to(jnp.sum(losses, axis=0, keepdims=True), (1, width))
+    out.up_bias[...] = jnp.zeros_like(out.up_bias)
+    lines = width // LANES
+    put_line(out.sums, 5 * lines, jnp.broadcast_to(jnp.sum(losses, axis=0, keepdims=True), (1, LANES)))
     grad_out = misfit * (weight * (seqs * seq_rows * ranks / true_count))
-    out.sums[0:1, :] = colsum(grad_out * normed)
-    out.sums[1:2, :] = colsum(grad_out)
+    put_line(out.sums, 0, colsum(grad_out * normed))
+    put_line(out.sums, lines, colsum(grad_out))
     second_grad = norm_back(grad_out, normed, inv, row(vec.second_gain))
     ffn_grad = second_grad.astype(BF)
     s.grad[...] = ffn_grad
-    out.sums[2:3, :] = colsum(ffn_grad.astype(F32))
+    put_line(out.sums, 2 * lines, colsum(ffn_grad.astype(F32)))
     s.total[...] = second_grad
 
     def backward(k, carry):
         keep = k // 2
         down = dot_tn(s.act[k], s.grad[...]).astype(BF)
         up_grad = (dot_nt(s.grad[...], s.three[k, depth:, :]) * slope(s.up_pre[k])).astype(BF)
-        out.up_bias[k] = jnp.broadcast_to(colsum(up_grad.astype(F32)), (8, units))
+        put_line(out.up_bias.at[meta[0] ^ k], 0, colsum(up_grad.astype(F32)))
         s.upg[...] = up_grad
         ups = [dot_tn(s.first[:, j * depth : (j + 1) * depth], s.upg[...]).astype(BF) for j in range(fold)]
 
@@ -631,8 +641,8 @@
 
     lax.fori_loop(0, peers, backward, 0)
     first_grad = s.total[...]
-    out.sums[3:4, :] = colsum(first_grad * normed_ref[...])
-    out.sums[4:5, :] = colsum(first_grad)
+    put_line(out.sums, 3 * lines, colsum(first_grad * normed_ref[...]))
+    put_line(out.sums, 4 * lines, colsum(first_grad))
     out.mid_grad[...] = norm_back(first_grad, normed_ref[...], inv_ref[...], row(vec.first_gain))
 
 
@@ -651,8 +661,9 @@
     s.gate_grad[...] = gate_grad
     out.direct[...] = mid * (1.0 - gate)
     out.sums[...] = jnp.zeros_like(out.sums)
-    out.sums[0:1, :] = colsum(pre_grad.astype(F32))
-    out.sums[1:2, :] = colsum(gate_grad.astype(F32))
+    out.bias[...] = jnp.zeros_like(out.bias)
+    put_line(out.sums, 0, colsum(pre_grad.astype(F32)))
+    put_line(out.sums, wide // LANES, colsum(gate_grad.astype(F32)))
     for copy in twos:
         copy.wait()
 
@@ -678,7 +689,7 @@
         out.attend_grad[k] = (gated_grad * (reset * sigmoid(reset))).astype(BF)
         reset_grad = (gated_grad * attended_ref[k] * slope(reset)).astype(BF)
         out.reset_grad[k] = reset_grad
-        out.bias[k] = jnp.broadcast_to(colsum(reset_grad.astype(F32)), (8, reset_grad.shape[1]))
+        put_line(out.bias.at[meta[0] ^ k], 0, colsum(reset_grad.astype(F32)))
         return carry
 
     lax.fori_loop(0, peers, shard, 0)
@@ -718,7 +729,9 @@
         to_column = (line == 2 * GROUP - 1 - ahead).astype(BF)
         table = dot(to_row, dot_nt(sgrad, to_column).astype(BF))
         buckets = buckets + colsum(pltpu.roll(table, 1, 1, stride=1, stride_axis=0))
-    out.rel[...] = jnp.broadcast_to(buckets, (8, 2 * GROUP))
+    out.rel[...] = jnp.zeros_like(out.rel)
+    out.bias[...] = jnp.zeros_like(out.bias)
+    put_line(out.rel, 0, buckets)
     query_grad, key_grad = s.query_grad[...], s.key_grad[...]
     zeta_grad = (query_grad * row(vec.query_gain) + key_grad * row(vec.key_gain)) * slope(zeta_pre_ref[...])
     zeta_grad = zeta_grad.astype(BF)
@@ -739,7 +752,7 @@
             at = slice(g * GROUP, (g + 1) * GROUP)
             vals_grad = dot_tn(probs_ref[at, :].astype(BF), agrad_ref[k, at, :])
             s.vgrad[at, :] = (vals_grad * slope(value_pre_ref[k, at, :])).astype(BF)
-        out.bias[k] = jnp.broadcast_to(colsum(s.vgrad[...].astype(F32)), (8, units))
+        put_line(out.bias.at[meta[0] ^ k], 0, colsum(s.vgrad[...].astype(F32)))
         reset = dot_tn(mixed_ref[...], rgrad_ref[k]).astype(BF)
         value = dot_tn(raw_ref[...], s.vgrad[...]).astype(BF)
 
@@ -784,10 +797,13 @@
     return [blocks[0]] + [swap(blocks[k], axis, k) for k in range(1, len(blocks))]
 
 
-def group_totals(total, fade, axis, reverse):
+def group_totals(total, fade, axis, reverse, nears=None):
     result = []
     for bit in bits_of(lax.axis_size(axis)):
         other = swap(total, axis, bit)
+        if nears is not None:
+            nears.append(beside(0, other))
+            other, nears[-1].token = lax.optimization_barrier((other, nears[-1].token))
         result.append(other)
         upper = ((lax.axis_index(axis) // bit) % 2) == (0 if reverse else 1)
         total = jnp.where(upper, total + fade * other, other + fade * total)
@@ -834,10 +850,10 @@
     return plus(mine, later_than(swap(theirs, "seq", bit), *deps))
 
 
-def all_rows(total, bits):
+def all_rows(total, bits, *deps):
     for bit in bits[::-1]:
         here = (lax.axis_index("seq") // bit) % 2
-        other = swap(total, "seq", bit)
+        other = later_than(swap(total, "seq", bit), *(deps if bit == bits[-1] else ()))
         total = jnp.where(
             here == 0, jnp.concatenate([total, other], axis=0), jnp.concatenate([other, total], axis=0)
         )
@@ -980,7 +996,7 @@
         second_gain=second_gain, second_shift=second_shift, up_bias=fwd.up_bias,
     )
     outs = Box(
-        mid_grad=((rows, wide), F32, VMEM), second=((peers, rows, width), BF, VMEM), sums=((8, wide), F32, VMEM), up_bias=((peers, 8, hidden), F32, VMEM),
+        mid_grad=((rows, wide), F32, VMEM), second=((peers, rows, width), BF, VMEM), sums=((6 * wide // LANES // 8 * 8 + 8, LANES), F32, VMEM), up_bias=((peers, 8, LANES), F32, VMEM),
         grads=[((peers // 2,) + three_shape, BF, VMEM)] * 2,
     )
     ffn = run(
@@ -1003,9 +1019,9 @@
         [(meta, SMEM), (shards_two, hbm), (fwd.mixed, VMEM), (fwd.raw, VMEM), (ffn.mid_grad, VMEM), (fwd.out_pre, VMEM),
          (fwd.gate, VMEM), (fwd.reset_pre, VMEM), (fwd.attended, VMEM), (fwd.gated, VMEM)],
         Box(
-            direct=((rows, wide), F32, VMEM), sums=((8, wide), F32, VMEM), mixed_grad=((peers, rows, width), F32, VMEM),
+            direct=((rows, wide), F32, VMEM), sums=((2 * wide // LANES // 8 * 8 + 8, LANES), F32, VMEM), mixed_grad=((peers, rows, width), F32, VMEM),
             attend_grad=((peers, rows, units), BF, VMEM), reset_grad=((peers, rows, units), BF, VMEM),
-            bias=((peers, 8, units), F32, VMEM),
+            bias=((peers, 8, LANES), F32, VMEM),
             grads=[((peers // 2,) + two_shape, BF, VMEM)] * 2,
         ),
         Box(
@@ -1020,8 +1036,8 @@
         zeta=zeta_proj, query_gain=query_gain, key_gain=key_gain, positions=positions,
     )
     outs = Box(
-        rel=((8, 2 * GROUP), F32, VMEM), sums=((8, Z), F32, VMEM), zeta=((wide, Z), F32, VMEM),
-        bias=((peers, 8, units), F32, VMEM),
+        rel=((8, LANES), F32, VMEM), sums=((8, Z), F32, VMEM), zeta=((wide, Z), F32, VMEM),
+        bias=((peers, 8, LANES), F32, VMEM),
         grads=[((peers // 2, wide, 2 * units), BF, VMEM)] * 2,
     )
     outs.m = [((rows, width), BF, hbm)] * peers
@@ -1041,7 +1057,6 @@
         vectors=vec,
     )
     grad_blocks = exchange(two.m, "wa")
-    rest_blocks = exchange(two.r, "wa")
     third_rows = keep_rows(third_parts, row_bits[0], two)
     mark = beside(HIDE_TWO, two.rel)
     second_parts = core_sums(one.grads, mark)
@@ -1055,69 +1070,82 @@
             first=((tiles, comps, LANES), F32, VMEM),
         ),
         Box(grad=pltpu.VMEM((tok_rows, width), BF), sem=sems((peers,))),
-        after=[second_parts, first_parts],
+        after=[second_parts, first_parts, third_rows],
         hides=HIDE_BACK,
     )
-    later = group_totals(back.first, ends.fade, "seq", True)
-    second_sum = shard_sum(second_parts)
-    third_sum = shard_sum(third_rows, back)
-    first_sum = keep_rows(first_parts, row_bits[0])
+    third_rows = shard_sum(third_rows, back)
+    nears = []
+    later = group_totals(back.first, ends.fade, "seq", True, nears)
+    near = nears[-1]
+    for bit in row_bits[1:-1]:
+        third_rows = keep_rows(third_rows, bit, nears[0])
+    third_rows = plus(third_rows, later_than(swap(third_rows, "seq", row_bits[-1]), near))
+    first_sum = keep_rows(first_parts, row_bits[0], near)
+    second_sum = shard_sum(second_parts, near)
     last = run(
-        functools.partial(ema_back, groups, comps, peers),
-        [(meta, SMEM), (inputs, VMEM), (back.grad, VMEM), (rest_blocks, hbm), (decay_rows, VMEM), (mix_rows, VMEM), (skip_row, VMEM),
+        functools.partial(ema_back, groups, comps),
+        [(meta, SMEM), (inputs, VMEM), (back.grad, VMEM), (decay_rows, VMEM), (mix_rows, VMEM), (skip_row, VMEM),
          (ema.start, VMEM), (back.after, VMEM), (later, VMEM)],
-        Box(grad=((seqs, seq_rows, width), F32, VMEM), block=((seqs, seq_rows, width), BF, VMEM), sums=((2 * comps + 8, width), F32, VMEM)),
+        Box(part=((tiles, seq_rows, LANES), F32, VMEM), sums=((-(-width // LANES), 2 * comps + 8, LANES), F32, VMEM)),
         Box(
-            x=pltpu.VMEM((tiles, seq_rows, LANES), F32), y=pltpu.VMEM((tiles, seq_rows, LANES), F32),
-            states=pltpu.VMEM((seq_rows // CHUNKS, comps, CHUNKS, LANES), F32), rest=pltpu.VMEM((tok_rows, 2 * width), BF),
-            sem=sems((peers,)),
+            x=pltpu.VMEM((tiles, seq_rows, LANES), F32),
+            states=pltpu.VMEM((seq_rows // CHUNKS, comps, CHUNKS, LANES), F32),
         ),
-        after=[second_sum, first_sum],
+        after=[third_rows, first_sum, second_sum],
         hides=HIDE_LAST,
     )
-
+    first_rows = shard_sum(first_sum, last)
     second_rows = keep_rows(second_sum, row_bits[0], last)
-    third_sum = keep_rows(third_sum, row_bits[1], last)
-    first_rows = shard_sum(first_sum, last)
+    first_rows, *rest_sent = lax.optimization_barrier((first_rows, *two.r))
+    rest_blocks = exchange(rest_sent, "wa")
+    joined = run(
+        functools.partial(ema_join, groups, peers),
+        [(meta, SMEM), (last.part, VMEM), (rest_blocks, hbm)],
+        Box(grad=((seqs, seq_rows, width), F32, VMEM), block=((seqs, seq_rows, width), BF, VMEM)),
+        Box(rest=pltpu.VMEM((tok_rows, 2 * width), BF), sem=sems((peers,))),
+    )
+
     totals = []
-    for rows_left, bits in ((third_sum, row_bits[2:]), (second_rows, row_bits[1:]), (first_rows, row_bits[1:])):
-        for bit in bits:
-            rows_left = keep_rows(rows_left, bit)
-        totals.append(all_rows(rows_left, row_bits))
+    for rows_left in (third_rows, second_rows, first_rows):
+        is_third = rows_left is third_rows
+        if not is_third:
+            for bit in row_bits[1:-1]:
+                rows_left = keep_rows(rows_left, bit)
+            rows_left = plus(rows_left, swap(rows_left, "seq", row_bits[-1]))
+        totals.append(all_rows(rows_left, row_bits[:-1], *([last] if is_third else [])))
     third_total, second_total, first_total = totals
-    shard_sums = jnp.stack([ffn.up_bias[:, 0], one.bias[:, 0], two.bias[:, 0]], axis=1)
-    shard_sums = shard_sums[me ^ lax.iota(jnp.int32, peers)]
-    shard_tall = 3 * peers * units // Z
-
-    tall = 16 * wide // Z
-    small = [
-        jnp.concatenate([ffn.sums, one.sums], axis=0).reshape(tall, Z), two.sums, two.rel.reshape(16, Z),
-        shard_sums.reshape(shard_tall, Z),
-    ]
-    small += [mark.token, two.token, back.token, ema.token, ends.token, last.token]
-    small.append(jnp.zeros((-sum(part.shape[0] for part in small) % 16, Z), F32))
-    small = jnp.concatenate(small, axis=0)
-    small, zeta_grad = sum_small(small, two.zeta, [("wa", bit) for bit in bits_of(peers)])
+    small = [ffn.sums, one.sums, two.sums, two.rel] + [a.reshape(-1, LANES) for a in (ffn.up_bias, one.bias, two.bias)]
+    places = [0]
+    for part in small:
+        places.append(places[-1] + part.shape[0])
+    small += [mark.token] + [mark.token for mark in nears] + [two.token, back.token, ema.token, ends.token, last.token]
+    small.append(jnp.zeros((-sum(part.shape[0] for part in small) % 16, LANES), F32))
+    small, zeta_grad = sum_small(jnp.concatenate(small, axis=0), two.zeta, [("wa", bit) for bit in bits_of(peers)])
     count = small.shape[0]
-    small = jnp.concatenate([small, last.sums.reshape(-1, Z)])
+    small = jnp.concatenate([small, last.sums.reshape(-1, LANES)])
     small, zeta_grad = sum_small(small, zeta_grad, [("seq", bit) for bit in row_bits])
     ema_sums = small[count:].reshape(last.sums.shape)
+    ema_sums = jnp.concatenate(list(ema_sums), axis=1)[:, :width]
     decay_grad = ema_sums[:comps].T * (ema_feed * ema_read)
     moment = ema_sums[comps : 2 * comps].T
     feed_grad, read_grad = moment * ema_read, moment * ema_feed
     skip_grad = ema_sums[2 * comps]
-
-    lines = small[:tall].reshape(16, wide)
-    zsums = small[tall : tall + 8]
-    rel_grad = small[tall + 8 : tall + 10].reshape(2 * GROUP)[: rel_bias.shape[0]]
-    shard_sums = small[tall + 24 : tall + 24 + shard_tall].reshape(peers, 3, units)[me]
+    parts = [small[a:b] for a, b in zip(places, places[1:])]
+    tall = wide // LANES
+    lines = [parts[0][i * tall : (i + 1) * tall].reshape(wide) for i in range(5)]
+    lines += [parts[1][i * tall : (i + 1) * tall].reshape(wide) for i in range(2)]
+    loss = parts[0][5 * tall, 0] + last.token[0, 0]
+    zsums, rel_grad = parts[2], parts[3][:2].reshape(2 * GROUP)[: rel_bias.shape[0]]
+    up_bias_grad, reset_bias_grad, value_bias_grad = (
+        lax.dynamic_slice_in_dim(part, me * 8, 8, 0).reshape(8 * LANES)[:units] for part in parts[4:]
+    )
 
     up_grad = jnp.concatenate([third_total[:depth, j * hidden : (j + 1) * hidden] for j in range(fold)], axis=0)
     return (
-        last.block, last.grad, lines[5, 0] + last.token[0, 0], decay_grad, feed_grad, read_grad, skip_grad, zeta_grad, zsums[0], zsums[1], zsums[2],
-        zsums[3], rel_grad, first_total[:, :units].astype(F32), shard_sums[1], first_total[:, units:].astype(F32), shard_sums[2],
-        second_total[:width].astype(F32), lines[9], second_total[width : 2 * width].astype(F32), second_total[2 * width :].astype(F32), lines[8], lines[3],
-        lines[4], up_grad.astype(F32), shard_sums[0], third_total[depth:].astype(F32), lines[2], lines[0], lines[1],
+        joined.block, joined.grad, loss, decay_grad, feed_grad, read_grad, skip_grad, zeta_grad, zsums[0], zsums[1], zsums[2],
+        zsums[3], rel_grad, first_total[:, :units].astype(F32), reset_bias_grad, first_total[:, units:].astype(F32), value_bias_grad,
+        second_total[:width].astype(F32), lines[6], second_total[width : 2 * width].astype(F32), second_total[2 * width :].astype(F32), lines[5], lines[3],
+        lines[4], up_grad.astype(F32), up_bias_grad, third_total[depth:].astype(F32), lines[2], lines[0], lines[1],
     )
 
 

time: 370 us -> 342 us (0.924)
  waiting for transfers between devices: 158 us -> 135 us
  other arithmetic: 31 us -> 23.9 us
  starting transfers between devices: 48.6 us -> 55.3 us
  local copies, waits for them, and re-layouts: 40.8 us -> 35.8 us
    ppermute x62 -> x59, waiting for transfers between devices: 158 us -> 135 us  [swap(): return lax.ppermute(x, axis, [(i, i ^ by) for i in range(size)])]
    ppermute x62 -> x59, starting transfers between devices: 48.6 us -> 55.3 us  [swap(): return lax.ppermute(x, axis, [(i, i ^ by) for i in range(size)])]
    convert_element_type x15 -> x14, other arithmetic: 17.5 us -> 11 us  [plus(): return (a.astype(F32) + b.astype(F32)).astype(a.dtype)]
    pallas_call x12 -> x16, Pallas kernels: 86 us -> 86.7 us  [run(): pl.pallas_call(kernel, out_shape=(shapes,), in_specs=specs, out_specs=(ou...]
    unnamed x201 -> x212, local copies, waits for them, and re-layouts: 28.4 us -> 28.3 us
  transfers between devices with their start and end apart: 62 -> 59, of which waited for: 27 -> 28; matrix products, arithmetic and copies ran while one was open for 10% -> 7% of each run, Pallas kernels for 18% -> 19%
where the time goes in v2:
time: 342 us
  waiting for transfers between devices  135 us (39%)
  Pallas kernels  86.7 us (25%)
  starting transfers between devices  55.3 us (16%)
  local copies, waits for them, and re-layouts  35.8 us (10%)
  other arithmetic  23.9 us (7%)
  between operations  4.47 us (1%)
    ppermute x59, waiting for transfers between devices, swap(): return lax.ppermute(x, axis, [(i, i ^ by) for i in range(size)])  135 us
    pallas_call x16, Pallas kernels, run(): pl.pallas_call(kernel, out_shape=(shapes,), in_specs=specs, out_specs=(ou...  86.7 us
    ppermute x59, starting transfers between devices, swap(): return lax.ppermute(x, axis, [(i, i ^ by) for i in range(size)])  55.3 us
    unnamed x212, local copies, waits for them, and re-layouts  28.3 us
    convert_element_type x14, other arithmetic, plus(): return (a.astype(F32) + b.astype(F32)).astype(a.dtype)  11 us
  transfers between devices with their start and end apart: 59, of which 28 were waited for; matrix products, arithmetic and copies ran while one was open for 7% of the time, Pallas kernels for 19%

profile of v2, /device:TPU:0, one launch (start us, length us, event | category | flops | bytes accessed | tf_op | source)
XLA Modules:
  0.0 341.6 jit_solution(15192372117018063740)
XLA Ops:
  7.6 3.0 collective-permute-start.6
  11.8 3.0 shard_map.527
  20.2 4.2 %collective-permute-done.6.refs_3__2__0_.refs_1__2__0_ = bf16[400,768]{1,0:T(8,128)(2,1)S(1)} collective-permute-done((bf16[400,768]{1,0:T(8,128)(2,1)S(1)}, bf16[400,768]{1,0:T(8,128)(2,1)S(1)}, u32[]{:S(2)}, u32[]{:S(2)}) %collective-permute-start.6) | collective-permute-done | bytes 614432 | tf_op jit(solution)/shard_map/ppermute | solution.py:787
  31.6 2.7 collective-permute-start.2
  36.4 8.1 %collective-permute-done.4.refs_2__2_ = bf16[256,192]{1,0:T(8,128)(2,1)S(1)} collective-permute-done((bf16[256,192]{1,0:T(8,128)(2,1)S(1)}, bf16[256,192]{1,0:T(8,128)(2,1)S(1)}, u32[]{:S(2)}, u32[]{:S(2)}) %collective-permute-start.4) | collective-permute-done | bytes 98336 | tf_op jit(solution)/shard_map/ppermute | solution.py:787
  47.5 4.5 %shard_map.530 = (f32[2,512,192]{2,1,0:T(8,128)S(1)}, f32[3,16,8,128]{3,2,1,0:T(8,128)S(1)}, bf16[256,192]{1,0:T(8,128)(2,1)S(1)}, bf16[256,192]{1,0:T(8,128)(2,...) custom-call(s32[3]{0:T(128)S(1)} %pad_add_fusion.refs_0_, ...), custom_call_target="tpu_custom_call" | custom-call | flops 23000000512 | bytes 1 | tf_op jit(solution)/shard_map/pallas_call | solution.py:115
  57.1 3.6 %collective-permute-done.10.refs_1__2_ = bf16[256,192]{1,0:T(8,128)(2,1)S(1)} collective-permute-done((bf16[256,192]{1,0:T(8,128)(2,1)S(1)}, bf16[256,192]{1,0:T(8,128)(2,1)S(1)}, u32[]{:S(2)}, u32[]{:S(2)}) %collective-permute-start.10) | collective-permute-done | bytes 98336 | tf_op jit(solution)/shard_map/ppermute | solution.py:787
  65.0 10.7 %collective-permute-done.16.refs_4__2__1_.refs_1__2__1_ = bf16[384,768]{1,0:T(8,128)(2,1)S(1)} collective-permute-done((bf16[384,768]{1,0:T(8,128)(2,1)S(1)}, bf16[384,768]{1,0:T(8,128)(2,1)S(1)}, u32[]{:S(2)}, u32[]{:S(2)}) %collective-permute-start.16) | collective-permute-done | bytes 589856 | tf_op jit(solution)/shard_map/ppermute | solution.py:787
  76.3 2.7 collective-permute-done.20.refs_2__2__0_
  81.2 12.9 %collective-permute-done.21.refs_2__2__1_ = bf16[384,768]{1,0:T(8,128)(2,1)S(1)} collective-permute-done((bf16[384,768]{1,0:T(8,128)(2,1)}, bf16[384,768]{1,0:T(8,128)(2,1)S(1)}, u32[]{:S(2)}, u32[]{:S(2)}) %collective-permute-start.21) | collective-permute-done | bytes 589856 | tf_op jit(solution)/shard_map/ppermute | solution.py:787
  96.2 13.9 %shard_map.531 = (bf16[256,768]{1,0:T(8,128)(2,1)}, bf16[256,768]{1,0:T(8,128)(2,1)}, f32[256,128]{1,0:T(8,128)}, bf16[256,128]{1,0:T(8,128)(2,1)}, bf16[256,128...) custom-call(s32[3]{0:T(128)} %copy-done.48, ...), custom_call_target="tpu_custom_call" | custom-call | flops 1 | bytes 1 | tf_op jit(solution)/shard_map/pallas_call | solution.py:115
  113.0 14.8 %shard_map.532 = (f32[256,768]{1,0:T(8,128)S(1)}, bf16[4,256,192]{2,1,0:T(8,128)(2,1)S(1)}, f32[40,128]{1,0:T(8,128)S(1)}, f32[4,8,128]{2,1,0:T(8,128)S(1)}, bf1...) custom-call(s32[3]{0:T(128)S(1)} %copy-done.49, s32[2]{0:T(128)S(1)} %copy-done.63, ...), custom_call_target="tpu_custom_call" | custom-call | flops 1 | bytes 1 | tf_op jit(solution)/shard_map/pallas_call | solution.py:115
  129.3 4.5 %collective-permute-done.24 = bf16[2,768,768]{2,1,0:T(8,128)(2,1)} collective-permute-done((bf16[2,768,768]{2,1,0:T(8,128)(2,1)}, bf16[2,768,768]{2,1,0:T(8,128)(2,1)}, u32[]{:S(2)}, u32[]{:S(2)}) %collective-permute-start.24) | collective-permute-done | bytes 2359328 | tf_op jit(solution)/shard_map/ppermute | solution.py:787
  133.8 3.0 add_convert_fusion.2.refs_11__0_
  139.9 11.8 %shard_map.533 = (f32[256,768]{1,0:T(8,128)S(1)}, f32[16,128]{1,0:T(8,128)S(1)}, f32[4,256,192]{2,1,0:T(8,128)}, bf16[4,256,384]{2,1,0:T(8,128)(2,1)S(1)}, bf16[...) custom-call(s32[3]{0:T(128)S(1)} %copy-done.49, ...), custom_call_target="tpu_custom_call" | custom-call | flops 23000000512 | bytes 1 | tf_op jit(solution)/shard_map/pallas_call | solution.py:115
  154.5 17.3 %shard_map.534 = (f32[8,128]{1,0:T(8,128)S(1)}, f32[8,128]{1,0:T(8,128)S(1)}, f32[768,128]{1,0:T(8,128)S(1)}, f32[4,8,128]{2,1,0:T(8,128)S(1)}, bf16[2,768,768]{...) custom-call(s32[3]{0:T(128)S(1)} %copy-done.49, ...), custom_call_target="tpu_custom_call" | custom-call | flops 1 | bytes 1 | tf_op jit(solution)/shard_map/pallas_call | solution.py:115
  178.3 3.8 %add_convert_fusion.refs_5__1_ = bf16[2,768,768]{2,1,0:T(8,128)(2,1)} fusion(bf16[2,768,768]{2,1,0:T(8,128)(2,1)} %copy-done.82, bf16[2,768,768]{2,1,0:T(8,128)(2,1)S(1)} %copy-done.81), kind=kLoop, calls=%fused_computation | loop fusion | flops 4718592 | bytes 7077888 | tf_op jit(solution)/shard_map/convert_element_type | solution.py:830
  183.3 3.5 %shard_map.536 = (f32[3,512,128]{2,1,0:T(8,128)S(1)}, f32[3,16,8,128]{3,2,1,0:T(8,128)S(1)}, f32[3,16,128]{2,1,0:T(8,128)S(1)}, f32[8,128]{1,0:T(8,128)S(1)}) custom-call(s32[3]{0:T(128)S(1)} %copy-done.49, bf16[256,192]{1,0:T(8,128)(2,1)S(1)} %get-tuple-element.227.refs_1__0_, bf16[256,192]{1,0:T(8,128)(2,1)S(1)} %collective-permute-done.25.refs_1__1_, ...), custom_call_target="tpu_custom_call" | custom-call | flops 69000003584 | bytes 1 | tf_op jit(solution)/shard_map/pallas_call | solution.py:115
  186.9 6.8 %collective-permute-done.34 = bf16[1,384,768]{2,1,0:T(8,128)(2,1)S(1)} collective-permute-done((bf16[1,384,768]{2,1,0:T(8,128)(2,1)S(1)}, bf16[1,384,768]{2,1,0:T(8,128)(2,1)S(1)}, u32[]{:S(2)}, u32[]{:S(2)}) %collective-permute-start.34) | collective-permute-done | bytes 589856 | tf_op jit(solution)/shard_map/ppermute | solution.py:787
  199.7 3.9 %collective-permute-done.32.refs_0__0_.refs_8__1_ = f32[3,16,128]{2,1,0:T(8,128)S(1)} collective-permute-done((f32[3,16,128]{2,1,0:T(8,128)S(1)}, f32[3,16,128]{2,1,0:T(8,128)S(1)}, u32[]{:S(2)}, u32[]{:S(2)}) %collective-permute-start.32) | collective-permute-done | bytes 24608 | tf_op jit(solution)/shard_map/ppermute | solution.py:787
  208.6 12.3 %collective-permute-done.36 = bf16[192,768]{1,0:T(8,128)(2,1)S(1)} collective-permute-done((bf16[192,768]{1,0:T(8,128)(2,1)S(1)}, bf16[192,768]{1,0:T(8,128)(2,1)S(1)}, u32[]{:S(2)}, u32[]{:S(2)}) %collective-permute-start.36) | collective-permute-done | bytes 294944 | tf_op jit(solution)/shard_map/ppermute | solution.py:787
  227.4 11.2 %shard_map.540 = (f32[3,512,128]{2,1,0:T(8,128)S(1)}, f32[2,40,128]{2,1,0:T(8,128)S(1)}, f32[8,128]{1,0:T(8,128)S(1)}) custom-call(s32[3]{0:T(128)S(1)} %copy-done.49, bf16[2,512,192]{2,1,0:T(8,128)(2,1)S(1)} %copy-done.31, f32[3,512,128]{2,1,0:T(8,128)S(1)} %get-tuple-element.242.refs_2_, f32[16,192]{1,0:T(8,128)S(1)} %bitcast.76, f32[16,192]{1,0:T(8,128)S(1)} %bitcast.71, ...), custom_call_target="tpu_custom_call" | custom-call | flops 17250000896 | bytes 1 | tf_op jit(solution)/shard_map/pallas_call | solution.py:115
  247.7 2.9 collective-permute-done.41.refs_2__2_
  250.6 3.4 %collective-permute-done.42.refs_2__3_ = bf16[256,384]{1,0:T(8,128)(2,1)S(1)} collective-permute-done((bf16[256,384]{1,0:T(8,128)(2,1)S(1)}, bf16[256,384]{1,0:T(8,128)(2,1)S(1)}, u32[]{:S(2)}, u32[]{:S(2)}) %collective-permute-start.42) | collective-permute-done | bytes 196640 | tf_op jit(solution)/shard_map/ppermute | solution.py:787
  259.7 2.7 collective-permute-start.55
  266.3 16.8 %collective-permute-done.55 = bf16[192,768]{1,0:T(8,128)(2,1)S(1)} collective-permute-done((bf16[192,768]{1,0:T(8,128)(2,1)S(1)}, bf16[192,768]{1,0:T(8,128)(2,1)S(1)}, u32[]{:S(2)}, u32[]{:S(2)}) %collective-permute-start.55) | collective-permute-done | bytes 294944 | tf_op jit(solution)/shard_map/ppermute | solution.py:787
  283.5 5.8 %collective-permute-done.51 = bf16[192,768]{1,0:T(8,128)(2,1)S(1)} collective-permute-done((bf16[192,768]{1,0:T(8,128)(2,1)S(1)}, bf16[192,768]{1,0:T(8,128)(2,1)S(1)}, u32[]{:S(2)}, u32[]{:S(2)}) %collective-permute-start.51) | collective-permute-done | bytes 294944 | tf_op jit(solution)/shard_map/ppermute | solution.py:787
  293.9 7.6 %collective-permute-done.47 = bf16[1408,128]{1,0:T(8,128)(2,1)S(1)} collective-permute-done((bf16[1408,128]{1,0:T(8,128)(2,1)S(1)}, bf16[1408,128]{1,0:T(8,128)(2,1)S(1)}, u32[]{:S(2)}, u32[]{:S(2)}) %collective-permute-start.47) | collective-permute-done | bytes 360480 | tf_op jit(solution)/shard_map/ppermute | solution.py:787
  307.1 3.7 %collective-permute-done.48 = bf16[1408,128]{1,0:T(8,128)(2,1)S(1)} collective-permute-done((bf16[1408,128]{1,0:T(8,128)(2,1)S(1)}, bf16[1408,128]{1,0:T(8,128)(2,1)S(1)}, u32[]{:S(2)}, u32[]{:S(2)}) %collective-permute-start.48) | collective-permute-done | bytes 360480 | tf_op jit(solution)/shard_map/ppermute | solution.py:787
  311.0 3.2 collective-permute-start.49
  314.2 6.9 %collective-permute-done.57 = bf16[384,768]{1,0:T(8,128)(2,1)S(1)} collective-permute-done((bf16[384,768]{1,0:T(8,128)(2,1)S(1)}, bf16[384,768]{1,0:T(8,128)(2,1)S(1)}, u32[]{:S(2)}, u32[]{:S(2)}) %collective-permute-start.57) | collective-permute-done | bytes 589856 | tf_op jit(solution)/shard_map/ppermute | solution.py:787
  323.7 7.4 %collective-permute-done.53 = bf16[384,768]{1,0:T(8,128)(2,1)S(1)} collective-permute-done((bf16[384,768]{1,0:T(8,128)(2,1)S(1)}, bf16[384,768]{1,0:T(8,128)(2,1)S(1)}, u32[]{:S(2)}, u32[]{:S(2)}) %collective-permute-start.53) | collective-permute-done | bytes 589856 | tf_op jit(solution)/shard_map/ppermute | solution.py:787
  (394 shorter events, 114.8 us)
Async XLA Ops:
  7.6 16.8 %collective-permute-start.6 = (bf16[400,768]{1,0:T(8,128)(2,1)S(1)}, bf16[400,768]{1,0:T(8,128)(2,1)S(1)}, u32[]{:S(2)}, u32[]{:S(2)}) collective-permute-start(bf16[400,768]{1,0:T(8,128)(2,1)S(1)} %get-tuple-element.162.refs_4__0_), channel_id=1, source_target_pairs={{0,2},{1,3},{2,0},{3,1},{4,6},{5,7},{6,4},{7,5},{8,10},{9,11},{10,... | collective-permute-start | bytes 1843208 | tf_op jit(solution)/shard_map/ppermute | solution.py:787
  24.4 20.5 %collective-permute-start.8 = (bf16[400,768]{1,0:T(8,128)(2,1)S(1)}, bf16[400,768]{1,0:T(8,128)(2,1)S(1)}, u32[]{:S(2)}, u32[]{:S(2)}) collective-permute-start(bf16[400,768]{1,0:T(8,128)(2,1)S(1)} %collective-permute-done.6.refs_3__2__0_.refs_1__2__0_), channel_id=1, source_target_pairs={{0,4},{4,0},{8,12},{12,8},{16,20},{20,16},{24,28},{28,24},{1,5},{5... | collective-permute-start | bytes 1843208 | tf_op jit(solution)/shard_map/ppermute | solution.py:787
  26.1 18.8 %collective-permute-start.7 = (bf16[384,768]{1,0:T(8,128)(2,1)}, bf16[384,768]{1,0:T(8,128)(2,1)S(1)}, u32[]{:S(2)}, u32[]{:S(2)}) collective-permute-start(bf16[384,768]{1,0:T(8,128)(2,1)} %copy-done.65), channel_id=1, source_target_pairs={{0,2},{1,3},{2,0},{3,1},{4,6},{5,7},{6,4},{7,5},{8,10},{9,11},{10,... | collective-permute-start | bytes 1769480 | tf_op jit(solution)/shard_map/ppermute | solution.py:787
  57.0 19.2 %collective-permute-start.14 = (bf16[400,768]{1,0:T(8,128)(2,1)S(1)}, bf16[400,768]{1,0:T(8,128)(2,1)S(1)}, u32[]{:S(2)}, u32[]{:S(2)}) collective-permute-start(bf16[400,768]{1,0:T(8,128)(2,1)S(1)} %collective-permute-done.8.refs_8__1_.refs_3__2__1_.refs_1__2__1_), channel_id=1, source_target_pairs={{0,1},{1,0},{2,3},{3,2},{4,5},{5,4},{6,7},{7,6},{8,9},{9,8},{10,11... | collective-permute-start | bytes 1843208 | tf_op jit(solution)/shard_map/ppermute | solution.py:787
  60.7 15.0 %collective-permute-start.16 = (bf16[384,768]{1,0:T(8,128)(2,1)S(1)}, bf16[384,768]{1,0:T(8,128)(2,1)S(1)}, u32[]{:S(2)}, u32[]{:S(2)}) collective-permute-start(bf16[384,768]{1,0:T(8,128)(2,1)S(1)} %collective-permute-done.7.refs_8__0_.refs_4__2__0_.refs_1__2__0_), channel_id=1, source_target_pairs={{0,4},{4,0},{8,12},{12,8},{16,20},{20,16},{24,28},{28,24},{1,5},{5... | collective-permute-start | bytes 1769480 | tf_op jit(solution)/shard_map/ppermute | solution.py:787
  63.3 15.7 %collective-permute-start.20 = (bf16[384,768]{1,0:T(8,128)(2,1)S(1)}, bf16[384,768]{1,0:T(8,128)(2,1)}, u32[]{:S(2)}, u32[]{:S(2)}) collective-permute-start(bf16[384,768]{1,0:T(8,128)(2,1)S(1)} %get-tuple-element.207), channel_id=1, source_target_pairs={{0,2},{1,3},{2,0},{3,1},{4,6},{5,7},{6,4},{7,5},{8,10},{9,11},{10,... | collective-permute-start | bytes 1769480 | tf_op jit(solution)/shard_map/ppermute | solution.py:787
  64.8 29.3 %collective-permute-start.12 = (bf16[800,768]{1,0:T(8,128)(2,1)S(1)}, bf16[800,768]{1,0:T(8,128)(2,1)S(1)}, u32[]{:S(2)}, u32[]{:S(2)}) collective-permute-start(bf16[800,768]{1,0:T(8,128)(2,1)S(1)} %get-tuple-element.190.refs_3__0__0_.refs_1__0__0_), channel_id=1, source_target_pairs={{0,1},{1,0},{2,3},{3,2},{4,5},{5,4},{6,7},{7,6},{8,9},{9,8},{10,11... | collective-permute-start | bytes 3686408 | tf_op jit(solution)/shard_map/ppermute | solution.py:787
  75.7 18.3 %collective-permute-start.15 = (bf16[768,768]{1,0:T(8,128)(2,1)S(1)}, bf16[768,768]{1,0:T(8,128)(2,1)S(1)}, u32[]{:S(2)}, u32[]{:S(2)}) collective-permute-start(bf16[768,768]{1,0:T(8,128)(2,1)S(1)} %copy-done.10), channel_id=1, source_target_pairs={{0,1},{1,0},{2,3},{3,2},{4,5},{5,4},{6,7},{7,6},{8,9},{9,8},{10,11... | collective-permute-start | bytes 3538952 | tf_op jit(solution)/shard_map/ppermute | solution.py:787
  75.7 34.4 %collective-permute-start.19 = (bf16[768,768]{1,0:T(8,128)(2,1)}, bf16[768,768]{1,0:T(8,128)(2,1)}, u32[]{:S(2)}, u32[]{:S(2)}) collective-permute-start(bf16[768,768]{1,0:T(8,128)(2,1)} %get-tuple-element.206.refs_2__0__0_), channel_id=1, source_target_pairs={{0,1},{1,0},{2,3},{3,2},{4,5},{5,4},{6,7},{7,6},{8,9},{9,8},{10,11... | collective-permute-start | bytes 3538952 | tf_op jit(solution)/shard_map/ppermute | solution.py:787
  79.0 15.0 %collective-permute-start.21 = (bf16[384,768]{1,0:T(8,128)(2,1)}, bf16[384,768]{1,0:T(8,128)(2,1)S(1)}, u32[]{:S(2)}, u32[]{:S(2)}) collective-permute-start(bf16[384,768]{1,0:T(8,128)(2,1)} %collective-permute-done.20.refs_2__2__0_), channel_id=1, source_target_pairs={{0,4},{4,0},{8,12},{12,8},{16,20},{20,16},{24,28},{28,24},{1,5},{5... | collective-permute-start | bytes 1769480 | tf_op jit(solution)/shard_map/ppermute | solution.py:787
  81.0 29.1 %collective-permute-start.22 = (bf16[384,768]{1,0:T(8,128)(2,1)}, bf16[384,768]{1,0:T(8,128)(2,1)S(1)}, u32[]{:S(2)}, u32[]{:S(2)}) collective-permute-start(bf16[384,768]{1,0:T(8,128)(2,1)} %collective-permute-done.20.refs_2__2__0_), channel_id=1, source_target_pairs={{0,1},{1,0},{2,3},{3,2},{4,5},{5,4},{6,7},{7,6},{8,9},{9,8},{10,11... | collective-permute-start | bytes 1769480 | tf_op jit(solution)/shard_map/ppermute | solution.py:787
  94.0 16.1 %collective-permute-start.23 = (bf16[384,768]{1,0:T(8,128)(2,1)S(1)}, bf16[384,768]{1,0:T(8,128)(2,1)}, u32[]{:S(2)}, u32[]{:S(2)}) collective-permute-start(bf16[384,768]{1,0:T(8,128)(2,1)S(1)} %collective-permute-done.21.refs_2__2__1_), channel_id=1, source_target_pairs={{0,1},{1,0},{2,3},{3,2},{4,5},{5,4},{6,7},{7,6},{8,9},{9,8},{10,11... | collective-permute-start | bytes 1769480 | tf_op jit(solution)/shard_map/ppermute | solution.py:787
  138.2 35.5 %collective-permute-start.30 = (bf16[2,384,768]{2,1,0:T(8,128)(2,1)S(1)}, bf16[2,384,768]{2,1,0:T(8,128)(2,1)S(1)}, u32[]{:S(2)}, u32[]{:S(2)}) collective-permute-start(bf16[2,384,768]{2,1,0:T(8,128)(2,1)S(1)} %constant_dynamic-slice_fusion.6), channel_id=1, source_target_pairs={{0,4},{4,0},{8,12},{12,8},{16,20},{20,16},{24,28},{28,24},{1,5},{5... | collective-permute-start | bytes 3538952 | tf_op jit(solution)/shard_map/ppermute | solution.py:787
  154.3 20.3 %collective-permute-start.28 = (bf16[2,768,768]{2,1,0:T(8,128)(2,1)}, bf16[2,768,768]{2,1,0:T(8,128)(2,1)S(1)}, u32[]{:S(2)}, u32[]{:S(2)}) collective-permute-start(bf16[2,768,768]{2,1,0:T(8,128)(2,1)} %get-tuple-element.233), channel_id=1, source_target_pairs={{0,1},{1,0},{2,3},{3,2},{4,5},{5,4},{6,7},{7,6},{8,9},{9,8},{10,11... | collective-permute-start | bytes 7077896 | tf_op jit(solution)/shard_map/ppermute | solution.py:787
  174.7 19.1 %collective-permute-start.34 = (bf16[1,384,768]{2,1,0:T(8,128)(2,1)S(1)}, bf16[1,384,768]{2,1,0:T(8,128)(2,1)S(1)}, u32[]{:S(2)}, u32[]{:S(2)}) collective-permute-start(bf16[1,384,768]{2,1,0:T(8,128)(2,1)S(1)} %slice.261), channel_id=1, source_target_pairs={{0,2},{1,3},{2,0},{3,1},{4,6},{5,7},{6,4},{7,5},{8,10},{9,11},{10,... | collective-permute-start | bytes 1769480 | tf_op jit(solution)/shard_map/ppermute | solution.py:787
  196.6 26.6 %collective-permute-start.37 = (bf16[2,384,768]{2,1,0:T(8,128)(2,1)S(1)}, bf16[2,384,768]{2,1,0:T(8,128)(2,1)S(1)}, u32[]{:S(2)}, u32[]{:S(2)}) collective-permute-start(bf16[2,384,768]{2,1,0:T(8,128)(2,1)S(1)} %constant_dynamic-slice_fusion.5), channel_id=1, source_target_pairs={{0,4},{4,0},{8,12},{12,8},{16,20},{20,16},{24,28},{28,24},{1,5},{5... | collective-permute-start | bytes 3538952 | tf_op jit(solution)/shard_map/ppermute | solution.py:787
  197.7 26.7 %collective-permute-start.38 = (bf16[1,768,768]{2,1,0:T(8,128)(2,1)S(1)}, bf16[1,768,768]{2,1,0:T(8,128)(2,1)S(1)}, u32[]{:S(2)}, u32[]{:S(2)}) collective-permute-start(bf16[1,768,768]{2,1,0:T(8,128)(2,1)S(1)} %slice.263), channel_id=1, source_target_pairs={{0,2},{1,3},{2,0},{3,1},{4,6},{5,7},{6,4},{7,5},{8,10},{9,11},{10,... | collective-permute-start | bytes 3538952 | tf_op jit(solution)/shard_map/ppermute | solution.py:787
  206.3 14.6 %collective-permute-start.36 = (bf16[192,768]{1,0:T(8,128)(2,1)S(1)}, bf16[192,768]{1,0:T(8,128)(2,1)S(1)}, u32[]{:S(2)}, u32[]{:S(2)}) collective-permute-start(bf16[192,768]{1,0:T(8,128)(2,1)S(1)} %fusion.2), channel_id=1, source_target_pairs={{0,16},{4,20},{8,24},{12,28},{16,0},{20,4},{24,8},{28,12},{1,17},{... | collective-permute-start | bytes 884744 | tf_op jit(solution)/shard_map/ppermute | solution.py:787
  220.9 17.9 %collective-permute-start.43 = (bf16[192,768]{1,0:T(8,128)(2,1)S(1)}, bf16[192,768]{1,0:T(8,128)(2,1)S(1)}, u32[]{:S(2)}, u32[]{:S(2)}) collective-permute-start(bf16[192,768]{1,0:T(8,128)(2,1)S(1)} %add_convert_fusion.12.refs_10__0_), channel_id=1, source_target_pairs={{0,8},{4,12},{8,0},{12,4},{16,24},{20,28},{24,16},{28,20},{1,9},{5... | collective-permute-start | bytes 884744 | tf_op jit(solution)/shard_map/ppermute | solution.py:787
  225.1 13.6 %collective-permute-start.39 = (bf16[1,384,768]{2,1,0:T(8,128)(2,1)S(1)}, bf16[1,384,768]{2,1,0:T(8,128)(2,1)S(1)}, u32[]{:S(2)}, u32[]{:S(2)}) collective-permute-start(bf16[1,384,768]{2,1,0:T(8,128)(2,1)S(1)} %slice.265), channel_id=1, source_target_pairs={{0,2},{1,3},{2,0},{3,1},{4,6},{5,7},{6,4},{7,5},{8,10},{9,11},{10,... | collective-permute-start | bytes 1769480 | tf_op jit(solution)/shard_map/ppermute | solution.py:787
  239.8 18.8 %collective-permute-start.54 = (bf16[192,768]{1,0:T(8,128)(2,1)}, bf16[192,768]{1,0:T(8,128)(2,1)}, u32[]{:S(2)}, u32[]{:S(2)}) collective-permute-start(bf16[192,768]{1,0:T(8,128)(2,1)} %constant_dynamic-slice_fusion.1), channel_id=1, source_target_pairs={{0,8},{4,12},{8,0},{12,4},{16,24},{20,28},{24,16},{28,20},{1,9},{5... | collective-permute-start | bytes 884744 | tf_op jit(solution)/shard_map/ppermute | solution.py:787
  241.8 20.6 %collective-permute-start.50 = (bf16[192,768]{1,0:T(8,128)(2,1)}, bf16[192,768]{1,0:T(8,128)(2,1)}, u32[]{:S(2)}, u32[]{:S(2)}) collective-permute-start(bf16[192,768]{1,0:T(8,128)(2,1)} %constant_dynamic-slice_fusion.4), channel_id=1, source_target_pairs={{0,8},{4,12},{8,0},{12,4},{16,24},{20,28},{24,16},{28,20},{1,9},{5... | collective-permute-start | bytes 884744 | tf_op jit(solution)/shard_map/ppermute | solution.py:787
  246.2 43.4 %collective-permute-start.58 = (bf16[384,768]{1,0:T(8,128)(2,1)S(1)}, bf16[384,768]{1,0:T(8,128)(2,1)}, u32[]{:S(2)}, u32[]{:S(2)}) collective-permute-start(bf16[384,768]{1,0:T(8,128)(2,1)S(1)} %maximum_select_fusion.5), channel_id=1, source_target_pairs={{0,4},{4,0},{8,12},{12,8},{16,20},{20,16},{24,28},{28,24},{1,5},{5... | collective-permute-start | bytes 1769480 | tf_op jit(solution)/shard_map/ppermute | solution.py:787
  250.6 13.3 %collective-permute-start.45 = (bf16[1248,128]{1,0:T(8,128)(2,1)}, bf16[1248,128]{1,0:T(8,128)(2,1)}, u32[]{:S(2)}, u32[]{:S(2)}) collective-permute-start(bf16[1248,128]{1,0:T(8,128)(2,1)} %pad_maximum_fusion.3), channel_id=1, source_target_pairs={{0,1},{1,0},{2,3},{3,2},{4,5},{5,4},{6,7},{7,6},{8,9},{9,8},{10,11... | collective-permute-start | bytes 958472 | tf_op jit(solution)/shard_map/ppermute | solution.py:787
  259.7 23.4 %collective-permute-start.55 = (bf16[192,768]{1,0:T(8,128)(2,1)S(1)}, bf16[192,768]{1,0:T(8,128)(2,1)S(1)}, u32[]{:S(2)}, u32[]{:S(2)}) collective-permute-start(bf16[192,768]{1,0:T(8,128)(2,1)S(1)} %add_convert_fusion.9), channel_id=1, source_target_pairs={{0,16},{4,20},{8,24},{12,28},{16,0},{20,4},{24,8},{28,12},{1,17},{... | collective-permute-start | bytes 884744 | tf_op jit(solution)/shard_map/ppermute | solution.py:787
  263.4 25.9 %collective-permute-start.51 = (bf16[192,768]{1,0:T(8,128)(2,1)S(1)}, bf16[192,768]{1,0:T(8,128)(2,1)S(1)}, u32[]{:S(2)}, u32[]{:S(2)}) collective-permute-start(bf16[192,768]{1,0:T(8,128)(2,1)S(1)} %add_convert_fusion.11), channel_id=1, source_target_pairs={{0,16},{4,20},{8,24},{12,28},{16,0},{20,4},{24,8},{28,12},{1,17},{... | collective-permute-start | bytes 884744 | tf_op jit(solution)/shard_map/ppermute | solution.py:787
  265.0 26.2 %collective-permute-start.46 = (bf16[1248,128]{1,0:T(8,128)(2,1)S(1)}, bf16[1248,128]{1,0:T(8,128)(2,1)S(1)}, u32[]{:S(2)}, u32[]{:S(2)}) collective-permute-start(bf16[1248,128]{1,0:T(8,128)(2,1)S(1)} %pad_maximum_fusion.4), channel_id=1, source_target_pairs={{0,2},{1,3},{2,0},{3,1},{4,6},{5,7},{6,4},{7,5},{8,10},{9,11},{10,... | collective-permute-start | bytes 958472 | tf_op jit(solution)/shard_map/ppermute | solution.py:787
  283.2 21.3 %collective-permute-start.56 = (bf16[192,768]{1,0:T(8,128)(2,1)S(1)}, bf16[192,768]{1,0:T(8,128)(2,1)S(1)}, u32[]{:S(2)}, u32[]{:S(2)}) collective-permute-start(bf16[192,768]{1,0:T(8,128)(2,1)S(1)} %add_convert_fusion.8), channel_id=1, source_target_pairs={{0,8},{4,12},{8,0},{12,4},{16,24},{20,28},{24,16},{28,20},{1,9},{5... | collective-permute-start | bytes 884744 | tf_op jit(solution)/shard_map/ppermute | solution.py:787
  289.4 17.0 %collective-permute-start.52 = (bf16[192,768]{1,0:T(8,128)(2,1)S(1)}, bf16[192,768]{1,0:T(8,128)(2,1)S(1)}, u32[]{:S(2)}, u32[]{:S(2)}) collective-permute-start(bf16[192,768]{1,0:T(8,128)(2,1)S(1)} %add_convert_fusion.10), channel_id=1, source_target_pairs={{0,8},{4,12},{8,0},{12,4},{16,24},{20,28},{24,16},{28,20},{1,9},{5... | collective-permute-start | bytes 884744 | tf_op jit(solution)/shard_map/ppermute | solution.py:787
  304.7 16.3 %collective-permute-start.57 = (bf16[384,768]{1,0:T(8,128)(2,1)S(1)}, bf16[384,768]{1,0:T(8,128)(2,1)S(1)}, u32[]{:S(2)}, u32[]{:S(2)}) collective-permute-start(bf16[384,768]{1,0:T(8,128)(2,1)S(1)} %maximum_select_fusion.4), channel_id=1, source_target_pairs={{0,4},{4,0},{8,12},{12,8},{16,20},{20,16},{24,28},{28,24},{1,5},{5... | collective-permute-start | bytes 1769480 | tf_op jit(solution)/shard_map/ppermute | solution.py:787
  306.6 24.5 %collective-permute-start.53 = (bf16[384,768]{1,0:T(8,128)(2,1)S(1)}, bf16[384,768]{1,0:T(8,128)(2,1)S(1)}, u32[]{:S(2)}, u32[]{:S(2)}) collective-permute-start(bf16[384,768]{1,0:T(8,128)(2,1)S(1)} %maximum_select_fusion.3), channel_id=1, source_target_pairs={{0,4},{4,0},{8,12},{12,8},{16,20},{20,16},{24,28},{28,24},{1,5},{5... | collective-permute-start | bytes 1769480 | tf_op jit(solution)/shard_map/ppermute | solution.py:787
  311.0 22.1 %collective-permute-start.49 = (bf16[1408,128]{1,0:T(8,128)(2,1)S(1)}, bf16[1408,128]{1,0:T(8,128)(2,1)S(1)}, u32[]{:S(2)}, u32[]{:S(2)}) collective-permute-start(bf16[1408,128]{1,0:T(8,128)(2,1)S(1)} %pad_maximum_fusion.2), channel_id=1, source_target_pairs={{0,16},{4,20},{8,24},{12,28},{16,0},{20,4},{24,8},{28,12},{1,17},{... | collective-permute-start | bytes 1081352 | tf_op jit(solution)/shard_map/ppermute | solution.py:787
  (124 other events, 1106.3 us)

commit v3 on v2

--- a/solution.py
+++ b/solution.py
@@ -12,7 +12,7 @@
 LANES = 128
 CHUNKS = 8
 BIAS_ROWS = 32
-HIDE_ENDS, HIDE_VALUES, HIDE_ONE, HIDE_TWO, HIDE_BACK, HIDE_LAST = 20, 20, 20, 40, 60, 15
+HIDE_ENDS, HIDE_VALUES, HIDE_ATTEND, HIDE_ONE, HIDE_TWO, HIDE_BACK, HIDE_LAST = 20, 20, 20, 20, 40, 60, 15
 SHARE_BITS = 1
 EPSILON = 1e-05
 BF = jnp.bfloat16
@@ -961,8 +961,9 @@
     pack_three.own, pack_one.packed, pack_two.packed, *mixed_blocks = lax.optimization_barrier(held)
     came_three = far_pieces(pack_three)
     shards_one = all_shards(pack_one, came_one, next_one)
-    shards_two = all_shards(pack_two, came_two, next_pieces(came_two))
-    shards_three = all_shards(pack_three, came_three, next_pieces(came_three))
+    next_two = next_pieces(came_two)
+    next_two[0], came_three[0] = lax.optimization_barrier((next_two[0], came_three[0]))
+    shards_two = all_shards(pack_two, came_two, next_two)
 
     count = len(jax.tree.leaves(shards_one))
     vec = Box(
@@ -989,7 +990,10 @@
         ),
         vectors=vec,
         limit=62,
-    )
+        hides=HIDE_ATTEND,
+    )
+    next_three = [later_than(x, fwd) for x in next_pieces(came_three)]
+    shards_three = all_shards(pack_three, came_three, next_three)
 
     vec = Box(
         first_gain=first_gain, first_shift=first_shift, down_bias=down_bias,
@@ -1073,14 +1077,14 @@
         after=[second_parts, first_parts, third_rows],
         hides=HIDE_BACK,
     )
-    third_rows = shard_sum(third_rows, back)
     nears = []
     later = group_totals(back.first, ends.fade, "seq", True, nears)
     near = nears[-1]
+    third_rows = shard_sum(third_rows, nears[0])
     for bit in row_bits[1:-1]:
-        third_rows = keep_rows(third_rows, bit, nears[0])
+        third_rows = keep_rows(third_rows, bit, nears[1])
     third_rows = plus(third_rows, later_than(swap(third_rows, "seq", row_bits[-1]), near))
-    first_sum = keep_rows(first_parts, row_bits[0], near)
+    first_sum = keep_rows(first_parts, row_bits[0], nears[1])
     second_sum = shard_sum(second_parts, near)
     last = run(
         functools.partial(ema_back, groups, comps),
@@ -1096,6 +1100,12 @@
     )
     first_rows = shard_sum(first_sum, last)
     second_rows = keep_rows(second_sum, row_bits[0], last)
+    def summed(total):
+        for bit in row_bits[1:-1]:
+            total = keep_rows(total, bit)
+        return plus(total, swap(total, "seq", row_bits[-1]))
+
+    first_rows, second_rows = summed(first_rows), summed(second_rows)
     first_rows, *rest_sent = lax.optimization_barrier((first_rows, *two.r))
     rest_blocks = exchange(rest_sent, "wa")
     joined = run(
@@ -1105,20 +1115,13 @@
         Box(rest=pltpu.VMEM((tok_rows, 2 * width), BF), sem=sems((peers,))),
     )
 
-    totals = []
-    for rows_left in (third_rows, second_rows, first_rows):
-        is_third = rows_left is third_rows
-        if not is_third:
-            for bit in row_bits[1:-1]:
-                rows_left = keep_rows(rows_left, bit)
-            rows_left = plus(rows_left, swap(rows_left, "seq", row_bits[-1]))
-        totals.append(all_rows(rows_left, row_bits[:-1], *([last] if is_third else [])))
-    third_total, second_total, first_total = totals
+    third_total = all_rows(third_rows, row_bits[:-1], last)
+    second_total, first_total = all_rows(second_rows, row_bits[:-1]), all_rows(first_rows, row_bits[:-1])
     small = [ffn.sums, one.sums, two.sums, two.rel] + [a.reshape(-1, LANES) for a in (ffn.up_bias, one.bias, two.bias)]
     places = [0]
     for part in small:
         places.append(places[-1] + part.shape[0])
-    small += [mark.token] + [mark.token for mark in nears] + [two.token, back.token, ema.token, ends.token, last.token]
+    small += [mark.token] + [mark.token for mark in nears] + [two.token, back.token, ema.token, ends.token, last.token, fwd.token]
     small.append(jnp.zeros((-sum(part.shape[0] for part in small) % 16, LANES), F32))
     small, zeta_grad = sum_small(jnp.concatenate(small, axis=0), two.zeta, [("wa", bit) for bit in bits_of(peers)])
     count = small.shape[0]

time: 342 us -> 332 us (0.971)
  starting transfers between devices: 55.3 us -> 50 us
  local copies, waits for them, and re-layouts: 35.8 us -> 32 us
    ppermute x59, starting transfers between devices: 55.3 us -> 50 us  [swap(): return lax.ppermute(x, axis, [(i, i ^ by) for i in range(size)])]
    ppermute x59, waiting for transfers between devices: 135 us -> 132 us  [swap(): return lax.ppermute(x, axis, [(i, i ^ by) for i in range(size)])]
    unnamed x212 -> x204, local copies, waits for them, and re-layouts: 28.3 us -> 25.3 us
    convert_element_type x14 -> x15, other arithmetic: 11 us -> 12 us  [plus(): return (a.astype(F32) + b.astype(F32)).astype(a.dtype)]
  transfers between devices with their start and end apart: 59 -> 59, of which waited for: 28 -> 26; matrix products, arithmetic and copies ran while one was open for 7% -> 8% of each run, Pallas kernels for 19% -> 20%
where the time goes in v3:
time: 332 us; the launch traced here: 331 us
  waiting for transfers between devices  132 us (40%)
  Pallas kernels  87.4 us (26%)
  starting transfers between devices  50 us (15%)
  local copies, waits for them, and re-layouts  32 us (10%)
  other arithmetic  25.8 us (8%)
  between operations  4.33 us (1%)
    ppermute x59, waiting for transfers between devices, swap(): return lax.ppermute(x, axis, [(i, i ^ by) for i in range(size)])  132 us
    pallas_call x16, Pallas kernels, run(): pl.pallas_call(kernel, out_shape=(shapes,), in_specs=specs, out_specs=(ou...  87.4 us
    ppermute x59, starting transfers between devices, swap(): return lax.ppermute(x, axis, [(i, i ^ by) for i in range(size)])  50 us
    unnamed x204, local copies, waits for them, and re-layouts  25.3 us
    convert_element_type x15, other arithmetic, plus(): return (a.astype(F32) + b.astype(F32)).astype(a.dtype)  12 us
  transfers between devices with their start and end apart: 59, of which 26 were waited for; matrix products, arithmetic and copies ran while one was open for 8% of the time, Pallas kernels for 20%

profile of v3, /device:TPU:0, one launch (start us, length us, event | category | flops | bytes accessed | tf_op | source)
XLA Modules:
  0.0 331.4 jit_solution(7169030071187480474)
XLA Ops:
  7.8 3.0 collective-permute-start.6
  11.1 3.0 shard_map.527
  20.6 4.3 %collective-permute-done.6.refs_3__2__0_.refs_1__2__0_ = bf16[400,768]{1,0:T(8,128)(2,1)S(1)} collective-permute-done((bf16[400,768]{1,0:T(8,128)(2,1)}, bf16[400,768]{1,0:T(8,128)(2,1)S(1)}, u32[]{:S(2)}, u32[]{:S(2)}) %collective-permute-start.6) | collective-permute-done | bytes 614432 | tf_op jit(solution)/shard_map/ppermute | solution.py:787
  32.0 2.7 collective-permute-start.2
  36.8 7.8 %collective-permute-done.4.refs_2__2_ = bf16[256,192]{1,0:T(8,128)(2,1)S(1)} collective-permute-done((bf16[256,192]{1,0:T(8,128)(2,1)S(1)}, bf16[256,192]{1,0:T(8,128)(2,1)S(1)}, u32[]{:S(2)}, u32[]{:S(2)}) %collective-permute-start.4) | collective-permute-done | bytes 98336 | tf_op jit(solution)/shard_map/ppermute | solution.py:787
  47.8 4.5 %shard_map.530 = (f32[2,512,192]{2,1,0:T(8,128)S(1)}, f32[3,16,8,128]{3,2,1,0:T(8,128)S(1)}, bf16[256,192]{1,0:T(8,128)(2,1)S(1)}, bf16[256,192]{1,0:T(8,128)(2,...) custom-call(s32[3]{0:T(128)S(1)} %pad_add_fusion.refs_0_, ...), custom_call_target="tpu_custom_call" | custom-call | flops 23000000512 | bytes 1 | tf_op jit(solution)/shard_map/pallas_call | solution.py:115
  57.8 2.5 collective-permute-done.10.refs_1__2_
  65.2 13.6 %collective-permute-done.16.refs_4__2__1_.refs_1__2__1_ = bf16[384,768]{1,0:T(8,128)(2,1)S(1)} collective-permute-done((bf16[384,768]{1,0:T(8,128)(2,1)}, bf16[384,768]{1,0:T(8,128)(2,1)S(1)}, u32[]{:S(2)}, u32[]{:S(2)}) %collective-permute-start.16) | collective-permute-done | bytes 589856 | tf_op jit(solution)/shard_map/ppermute | solution.py:787
  80.1 2.6 collective-permute-done.18.refs_4__3__0_.refs_1__3__0_
  85.6 14.0 %shard_map.531 = (bf16[256,768]{1,0:T(8,128)(2,1)}, bf16[256,768]{1,0:T(8,128)(2,1)}, f32[256,128]{1,0:T(8,128)}, bf16[256,128]{1,0:T(8,128)(2,1)}, bf16[256,128...) custom-call(s32[3]{0:T(128)} %copy-done.36, ...), custom_call_target="tpu_custom_call" | custom-call | flops 23000000512 | bytes 1 | tf_op jit(solution)/shard_map/pallas_call | solution.py:115
  104.6 14.9 %shard_map.532 = (f32[256,768]{1,0:T(8,128)S(1)}, bf16[4,256,192]{2,1,0:T(8,128)(2,1)S(1)}, f32[40,128]{1,0:T(8,128)S(1)}, f32[4,8,128]{2,1,0:T(8,128)S(1)}, bf1...) custom-call(s32[3]{0:T(128)S(1)} %copy-done.37, s32[2]{0:T(128)S(1)} %copy-done.48, ...), custom_call_target="tpu_custom_call" | custom-call | flops 1 | bytes 1 | tf_op jit(solution)/shard_map/pallas_call | solution.py:115
  119.9 4.6 %collective-permute-done.24 = bf16[2,768,768]{2,1,0:T(8,128)(2,1)} collective-permute-done((bf16[2,768,768]{2,1,0:T(8,128)(2,1)}, bf16[2,768,768]{2,1,0:T(8,128)(2,1)}, u32[]{:S(2)}, u32[]{:S(2)}) %collective-permute-start.24) | collective-permute-done | bytes 2359328 | tf_op jit(solution)/shard_map/ppermute | solution.py:787
  124.4 3.0 add_convert_fusion.2.refs_11__0_
  130.5 11.7 %shard_map.533 = (f32[256,768]{1,0:T(8,128)S(1)}, f32[16,128]{1,0:T(8,128)S(1)}, f32[4,256,192]{2,1,0:T(8,128)}, bf16[4,256,384]{2,1,0:T(8,128)(2,1)S(1)}, bf16[...) custom-call(s32[3]{0:T(128)S(1)} %copy-done.37, ...), custom_call_target="tpu_custom_call" | custom-call | flops 23000000512 | bytes 1 | tf_op jit(solution)/shard_map/pallas_call | solution.py:115
  145.1 17.4 %shard_map.534 = (f32[8,128]{1,0:T(8,128)S(1)}, f32[8,128]{1,0:T(8,128)S(1)}, f32[768,128]{1,0:T(8,128)S(1)}, f32[4,8,128]{2,1,0:T(8,128)S(1)}, bf16[2,768,768]{...) custom-call(s32[3]{0:T(128)S(1)} %copy-done.37, ...), custom_call_target="tpu_custom_call" | custom-call | flops 1 | bytes 1 | tf_op jit(solution)/shard_map/pallas_call | solution.py:115
  169.3 3.9 %add_convert_fusion.refs_5__1_ = bf16[2,768,768]{2,1,0:T(8,128)(2,1)} fusion(bf16[2,768,768]{2,1,0:T(8,128)(2,1)} %collective-permute-done.29, bf16[2,768,768]{2,1,0:T(8,128)(2,1)S(1)} %copy-done.77), kind=kLoop, calls=%fused_computation | loop fusion | flops 4718592 | bytes 7077888 | tf_op jit(solution)/shard_map/convert_element_type | solution.py:830
  174.4 3.5 %shard_map.536 = (f32[3,512,128]{2,1,0:T(8,128)S(1)}, f32[3,16,8,128]{3,2,1,0:T(8,128)S(1)}, f32[3,16,128]{2,1,0:T(8,128)S(1)}, f32[8,128]{1,0:T(8,128)S(1)}) custom-call(s32[3]{0:T(128)S(1)} %copy-done.37, bf16[256,192]{1,0:T(8,128)(2,1)S(1)} %get-tuple-element.236.refs_1__0_, bf16[256,192]{1,0:T(8,128)(2,1)S(1)} %collective-permute-done.25.refs_1__1_, ...), custom_call_target="tpu_custom_call" | custom-call | flops 69000003584 | bytes 1 | tf_op jit(solution)/shard_map/pallas_call | solution.py:115
  181.8 3.2 collective-permute-done.34
  188.4 6.5 %collective-permute-done.32.refs_0__0_.refs_8__1_ = f32[3,16,128]{2,1,0:T(8,128)S(1)} collective-permute-done((f32[3,16,128]{2,1,0:T(8,128)S(1)}, f32[3,16,128]{2,1,0:T(8,128)S(1)}, u32[]{:S(2)}, u32[]{:S(2)}) %collective-permute-start.32) | collective-permute-done | bytes 24608 | tf_op jit(solution)/shard_map/ppermute | solution.py:787
  195.1 2.7 collective-permute-start.36
  198.2 12.5 %collective-permute-done.33.refs_0__0_.refs_8__2_ = f32[3,16,128]{2,1,0:T(8,128)S(1)} collective-permute-done((f32[3,16,128]{2,1,0:T(8,128)S(1)}, f32[3,16,128]{2,1,0:T(8,128)S(1)}, u32[]{:S(2)}, u32[]{:S(2)}) %collective-permute-start.33) | collective-permute-done | bytes 24608 | tf_op jit(solution)/shard_map/ppermute | solution.py:787
  214.5 11.4 %shard_map.540 = (f32[3,512,128]{2,1,0:T(8,128)S(1)}, f32[2,40,128]{2,1,0:T(8,128)S(1)}, f32[8,128]{1,0:T(8,128)S(1)}) custom-call(s32[3]{0:T(128)S(1)} %copy-done.37, bf16[2,512,192]{2,1,0:T(8,128)(2,1)S(1)} %copy-done.20, f32[3,512,128]{2,1,0:T(8,128)S(1)} %get-tuple-element.251.refs_2_, f32[16,192]{1,0:T(8,128)S(1)} %bitcast.79, f32[16,192]{1,0:T(8,128)S(1)} %bitcast.74, ...), custom_call_target="tpu_custom_call" | custom-call | flops 17250000896 | bytes 1 | tf_op jit(solution)/shard_map/pallas_call | solution.py:115
  232.7 10.2 %collective-permute-done.54 = bf16[192,768]{1,0:T(8,128)(2,1)S(1)} collective-permute-done((bf16[192,768]{1,0:T(8,128)(2,1)S(1)}, bf16[192,768]{1,0:T(8,128)(2,1)S(1)}, u32[]{:S(2)}, u32[]{:S(2)}) %collective-permute-start.54) | collective-permute-done | bytes 294944 | tf_op jit(solution)/shard_map/ppermute | solution.py:787
  243.2 3.2 collective-permute-done.40
  246.5 3.1 collective-permute-start.41
  250.3 14.0 %collective-permute-done.55 = bf16[192,768]{1,0:T(8,128)(2,1)S(1)} collective-permute-done((bf16[192,768]{1,0:T(8,128)(2,1)S(1)}, bf16[192,768]{1,0:T(8,128)(2,1)S(1)}, u32[]{:S(2)}, u32[]{:S(2)}) %collective-permute-start.55) | collective-permute-done | bytes 294944 | tf_op jit(solution)/shard_map/ppermute | solution.py:787
  264.4 3.0 collective-permute-done.41
  271.7 8.0 %collective-permute-done.49 = bf16[1440,128]{1,0:T(8,128)(2,1)S(1)} collective-permute-done((bf16[1440,128]{1,0:T(8,128)(2,1)S(1)}, bf16[1440,128]{1,0:T(8,128)(2,1)S(1)}, u32[]{:S(2)}, u32[]{:S(2)}) %collective-permute-start.49) | collective-permute-done | bytes 368672 | tf_op jit(solution)/shard_map/ppermute | solution.py:787
  284.2 2.6 collective-permute-done.44.refs_2__3_
  286.8 2.5 shard_map.541
  297.9 11.0 %collective-permute-done.57 = bf16[384,768]{1,0:T(8,128)(2,1)S(1)} collective-permute-done((bf16[384,768]{1,0:T(8,128)(2,1)S(1)}, bf16[384,768]{1,0:T(8,128)(2,1)S(1)}, u32[]{:S(2)}, u32[]{:S(2)}) %collective-permute-start.57) | collective-permute-done | bytes 589856 | tf_op jit(solution)/shard_map/ppermute | solution.py:787
  311.6 9.4 %collective-permute-done.53 = bf16[384,768]{1,0:T(8,128)(2,1)S(1)} collective-permute-done((bf16[384,768]{1,0:T(8,128)(2,1)S(1)}, bf16[384,768]{1,0:T(8,128)(2,1)S(1)}, u32[]{:S(2)}, u32[]{:S(2)}) %collective-permute-start.53) | collective-permute-done | bytes 589856 | tf_op jit(solution)/shard_map/ppermute | solution.py:787
  (386 shorter events, 107.0 us)
Async XLA Ops:
  7.8 17.0 %collective-permute-start.6 = (bf16[400,768]{1,0:T(8,128)(2,1)}, bf16[400,768]{1,0:T(8,128)(2,1)S(1)}, u32[]{:S(2)}, u32[]{:S(2)}) collective-permute-start(bf16[400,768]{1,0:T(8,128)(2,1)} %get-tuple-element.167.refs_4__0_), channel_id=1, source_target_pairs={{0,2},{1,3},{2,0},{3,1},{4,6},{5,7},{6,4},{7,5},{8,10},{9,11},{10,... | collective-permute-start | bytes 1843208 | tf_op jit(solution)/shard_map/ppermute | solution.py:787
  24.8 20.3 %collective-permute-start.8 = (bf16[400,768]{1,0:T(8,128)(2,1)S(1)}, bf16[400,768]{1,0:T(8,128)(2,1)S(1)}, u32[]{:S(2)}, u32[]{:S(2)}) collective-permute-start(bf16[400,768]{1,0:T(8,128)(2,1)S(1)} %collective-permute-done.6.refs_3__2__0_.refs_1__2__0_), channel_id=1, source_target_pairs={{0,4},{4,0},{8,12},{12,8},{16,20},{20,16},{24,28},{28,24},{1,5},{5... | collective-permute-start | bytes 1843208 | tf_op jit(solution)/shard_map/ppermute | solution.py:787
  26.6 18.6 %collective-permute-start.7 = (bf16[384,768]{1,0:T(8,128)(2,1)S(1)}, bf16[384,768]{1,0:T(8,128)(2,1)}, u32[]{:S(2)}, u32[]{:S(2)}) collective-permute-start(bf16[384,768]{1,0:T(8,128)(2,1)S(1)} %get-tuple-element.189), channel_id=1, source_target_pairs={{0,2},{1,3},{2,0},{3,1},{4,6},{5,7},{6,4},{7,5},{8,10},{9,11},{10,... | collective-permute-start | bytes 1769480 | tf_op jit(solution)/shard_map/ppermute | solution.py:787
  62.7 20.7 %collective-permute-start.12 = (bf16[800,768]{1,0:T(8,128)(2,1)S(1)}, bf16[800,768]{1,0:T(8,128)(2,1)S(1)}, u32[]{:S(2)}, u32[]{:S(2)}) collective-permute-start(bf16[800,768]{1,0:T(8,128)(2,1)S(1)} %get-tuple-element.195.refs_3__0__0_.refs_1__0__0_), channel_id=1, source_target_pairs={{0,1},{1,0},{2,3},{3,2},{4,5},{5,4},{6,7},{7,6},{8,9},{9,8},{10,11... | collective-permute-start | bytes 3686408 | tf_op jit(solution)/shard_map/ppermute | solution.py:787
  62.9 15.8 %collective-permute-start.16 = (bf16[384,768]{1,0:T(8,128)(2,1)}, bf16[384,768]{1,0:T(8,128)(2,1)S(1)}, u32[]{:S(2)}, u32[]{:S(2)}) collective-permute-start(bf16[384,768]{1,0:T(8,128)(2,1)} %collective-permute-done.7.refs_8__0_.refs_4__2__0_.refs_1__2__0_), channel_id=1, source_target_pairs={{0,4},{4,0},{8,12},{12,8},{16,20},{20,16},{24,28},{28,24},{1,5},{5... | collective-permute-start | bytes 1769480 | tf_op jit(solution)/shard_map/ppermute | solution.py:787
  63.7 15.9 %collective-permute-start.13 = (bf16[400,768]{1,0:T(8,128)(2,1)S(1)}, bf16[400,768]{1,0:T(8,128)(2,1)S(1)}, u32[]{:S(2)}, u32[]{:S(2)}) collective-permute-start(bf16[400,768]{1,0:T(8,128)(2,1)S(1)} %collective-permute-done.6.refs_3__2__0_.refs_1__2__0_), channel_id=1, source_target_pairs={{0,1},{1,0},{2,3},{3,2},{4,5},{5,4},{6,7},{7,6},{8,9},{9,8},{10,11... | collective-permute-start | bytes 1843208 | tf_op jit(solution)/shard_map/ppermute | solution.py:787
  63.8 15.8 %collective-permute-start.17 = (bf16[384,768]{1,0:T(8,128)(2,1)S(1)}, bf16[384,768]{1,0:T(8,128)(2,1)}, u32[]{:S(2)}, u32[]{:S(2)}) collective-permute-start(bf16[384,768]{1,0:T(8,128)(2,1)S(1)} %get-tuple-element.205), channel_id=1, source_target_pairs={{0,2},{1,3},{2,0},{3,1},{4,6},{5,7},{6,4},{7,5},{8,10},{9,11},{10,... | collective-permute-start | bytes 1769480 | tf_op jit(solution)/shard_map/ppermute | solution.py:787
  65.1 18.3 %collective-permute-start.15 = (bf16[768,768]{1,0:T(8,128)(2,1)S(1)}, bf16[768,768]{1,0:T(8,128)(2,1)S(1)}, u32[]{:S(2)}, u32[]{:S(2)}) collective-permute-start(bf16[768,768]{1,0:T(8,128)(2,1)S(1)} %copy-done.52), channel_id=1, source_target_pairs={{0,1},{1,0},{2,3},{3,2},{4,5},{5,4},{6,7},{7,6},{8,9},{9,8},{10,11... | collective-permute-start | bytes 3538952 | tf_op jit(solution)/shard_map/ppermute | solution.py:787
  82.7 17.3 %collective-permute-start.20 = (bf16[768,768]{1,0:T(8,128)(2,1)}, bf16[768,768]{1,0:T(8,128)(2,1)}, u32[]{:S(2)}, u32[]{:S(2)}) collective-permute-start(bf16[768,768]{1,0:T(8,128)(2,1)} %get-tuple-element.213.refs_2__0__0_), channel_id=1, source_target_pairs={{0,1},{1,0},{2,3},{3,2},{4,5},{5,4},{6,7},{7,6},{8,9},{9,8},{10,11... | collective-permute-start | bytes 3538952 | tf_op jit(solution)/shard_map/ppermute | solution.py:787
  82.8 16.8 %collective-permute-start.21 = (bf16[384,768]{1,0:T(8,128)(2,1)}, bf16[384,768]{1,0:T(8,128)(2,1)S(1)}, u32[]{:S(2)}, u32[]{:S(2)}) collective-permute-start(bf16[384,768]{1,0:T(8,128)(2,1)} %collective-permute-done.17.refs_2__2__0_), channel_id=1, source_target_pairs={{0,4},{4,0},{8,12},{12,8},{16,20},{20,16},{24,28},{28,24},{1,5},{5... | collective-permute-start | bytes 1769480 | tf_op jit(solution)/shard_map/ppermute | solution.py:787
  83.3 16.7 %collective-permute-start.22 = (bf16[384,768]{1,0:T(8,128)(2,1)}, bf16[384,768]{1,0:T(8,128)(2,1)}, u32[]{:S(2)}, u32[]{:S(2)}) collective-permute-start(bf16[384,768]{1,0:T(8,128)(2,1)} %collective-permute-done.17.refs_2__2__0_), channel_id=1, source_target_pairs={{0,1},{1,0},{2,3},{3,2},{4,5},{5,4},{6,7},{7,6},{8,9},{9,8},{10,11... | collective-permute-start | bytes 1769480 | tf_op jit(solution)/shard_map/ppermute | solution.py:787
  128.8 36.0 %collective-permute-start.30 = (bf16[2,384,768]{2,1,0:T(8,128)(2,1)S(1)}, bf16[2,384,768]{2,1,0:T(8,128)(2,1)}, u32[]{:S(2)}, u32[]{:S(2)}) collective-permute-start(bf16[2,384,768]{2,1,0:T(8,128)(2,1)S(1)} %constant_dynamic-slice_fusion.5), channel_id=1, source_target_pairs={{0,4},{4,0},{8,12},{12,8},{16,20},{20,16},{24,28},{28,24},{1,5},{5... | collective-permute-start | bytes 3538952 | tf_op jit(solution)/shard_map/ppermute | solution.py:787
  144.9 22.8 %collective-permute-start.28 = (bf16[2,768,768]{2,1,0:T(8,128)(2,1)}, bf16[2,768,768]{2,1,0:T(8,128)(2,1)S(1)}, u32[]{:S(2)}, u32[]{:S(2)}) collective-permute-start(bf16[2,768,768]{2,1,0:T(8,128)(2,1)} %get-tuple-element.242), channel_id=1, source_target_pairs={{0,1},{1,0},{2,3},{3,2},{4,5},{5,4},{6,7},{7,6},{8,9},{9,8},{10,11... | collective-permute-start | bytes 7077896 | tf_op jit(solution)/shard_map/ppermute | solution.py:787
  167.7 17.3 %collective-permute-start.34 = (bf16[1,384,768]{2,1,0:T(8,128)(2,1)}, bf16[1,384,768]{2,1,0:T(8,128)(2,1)}, u32[]{:S(2)}, u32[]{:S(2)}) collective-permute-start(bf16[1,384,768]{2,1,0:T(8,128)(2,1)} %slice.261), channel_id=1, source_target_pairs={{0,2},{1,3},{2,0},{3,1},{4,6},{5,7},{6,4},{7,5},{8,10},{9,11},{10,... | collective-permute-start | bytes 1769480 | tf_op jit(solution)/shard_map/ppermute | solution.py:787
  179.1 32.4 %collective-permute-start.38 = (bf16[1,768,768]{2,1,0:T(8,128)(2,1)S(1)}, bf16[1,768,768]{2,1,0:T(8,128)(2,1)S(1)}, u32[]{:S(2)}, u32[]{:S(2)}) collective-permute-start(bf16[1,768,768]{2,1,0:T(8,128)(2,1)S(1)} %slice.263), channel_id=1, source_target_pairs={{0,2},{1,3},{2,0},{3,1},{4,6},{5,7},{6,4},{7,5},{8,10},{9,11},{10,... | collective-permute-start | bytes 3538952 | tf_op jit(solution)/shard_map/ppermute | solution.py:787
  179.6 32.2 %collective-permute-start.37 = (bf16[2,384,768]{2,1,0:T(8,128)(2,1)S(1)}, bf16[2,384,768]{2,1,0:T(8,128)(2,1)S(1)}, u32[]{:S(2)}, u32[]{:S(2)}) collective-permute-start(bf16[2,384,768]{2,1,0:T(8,128)(2,1)S(1)} %constant_dynamic-slice_fusion.4), channel_id=1, source_target_pairs={{0,4},{4,0},{8,12},{12,8},{16,20},{20,16},{24,28},{28,24},{1,5},{5... | collective-permute-start | bytes 3538952 | tf_op jit(solution)/shard_map/ppermute | solution.py:787
  195.1 15.6 %collective-permute-start.36 = (bf16[192,768]{1,0:T(8,128)(2,1)S(1)}, bf16[192,768]{1,0:T(8,128)(2,1)S(1)}, u32[]{:S(2)}, u32[]{:S(2)}) collective-permute-start(bf16[192,768]{1,0:T(8,128)(2,1)S(1)} %fusion.2), channel_id=1, source_target_pairs={{0,16},{4,20},{8,24},{12,28},{16,0},{20,4},{24,8},{28,12},{1,17},{... | collective-permute-start | bytes 884744 | tf_op jit(solution)/shard_map/ppermute | solution.py:787
  210.7 17.9 %collective-permute-start.45 = (bf16[192,768]{1,0:T(8,128)(2,1)S(1)}, bf16[192,768]{1,0:T(8,128)(2,1)S(1)}, u32[]{:S(2)}, u32[]{:S(2)}) collective-permute-start(bf16[192,768]{1,0:T(8,128)(2,1)S(1)} %add_convert_fusion.11.refs_10__0_), channel_id=1, source_target_pairs={{0,8},{4,12},{8,0},{12,4},{16,24},{20,28},{24,16},{28,20},{1,9},{5... | collective-permute-start | bytes 884744 | tf_op jit(solution)/shard_map/ppermute | solution.py:787
  212.3 15.0 %collective-permute-start.39 = (bf16[1,384,768]{2,1,0:T(8,128)(2,1)S(1)}, bf16[1,384,768]{2,1,0:T(8,128)(2,1)S(1)}, u32[]{:S(2)}, u32[]{:S(2)}) collective-permute-start(bf16[1,384,768]{2,1,0:T(8,128)(2,1)S(1)} %slice.265), channel_id=1, source_target_pairs={{0,2},{1,3},{2,0},{3,1},{4,6},{5,7},{6,4},{7,5},{8,10},{9,11},{10,... | collective-permute-start | bytes 1769480 | tf_op jit(solution)/shard_map/ppermute | solution.py:787
  228.9 38.8 %collective-permute-start.58 = (bf16[384,768]{1,0:T(8,128)(2,1)S(1)}, bf16[384,768]{1,0:T(8,128)(2,1)S(1)}, u32[]{:S(2)}, u32[]{:S(2)}) collective-permute-start(bf16[384,768]{1,0:T(8,128)(2,1)S(1)} %maximum_select_fusion.5), channel_id=1, source_target_pairs={{0,4},{4,0},{8,12},{12,8},{16,20},{20,16},{24,28},{28,24},{1,5},{5... | collective-permute-start | bytes 1769480 | tf_op jit(solution)/shard_map/ppermute | solution.py:787
  230.8 15.6 %collective-permute-start.40 = (bf16[192,768]{1,0:T(8,128)(2,1)S(1)}, bf16[192,768]{1,0:T(8,128)(2,1)S(1)}, u32[]{:S(2)}, u32[]{:S(2)}) collective-permute-start(bf16[192,768]{1,0:T(8,128)(2,1)S(1)} %dynamic-slice_bitcast_fusion.1), channel_id=1, source_target_pairs={{0,8},{4,12},{8,0},{12,4},{16,24},{20,28},{24,16},{28,20},{1,9},{5... | collective-permute-start | bytes 884744 | tf_op jit(solution)/shard_map/ppermute | solution.py:787
  232.6 16.9 %collective-permute-start.47 = (bf16[1280,128]{1,0:T(8,128)(2,1)S(1)}, bf16[1280,128]{1,0:T(8,128)(2,1)S(1)}, u32[]{:S(2)}, u32[]{:S(2)}) collective-permute-start(bf16[1280,128]{1,0:T(8,128)(2,1)S(1)} %pad_maximum_fusion.3), channel_id=1, source_target_pairs={{0,1},{1,0},{2,3},{3,2},{4,5},{5,4},{6,7},{7,6},{8,9},{9,8},{10,11... | collective-permute-start | bytes 983048 | tf_op jit(solution)/shard_map/ppermute | solution.py:787
  242.9 21.3 %collective-permute-start.55 = (bf16[192,768]{1,0:T(8,128)(2,1)S(1)}, bf16[192,768]{1,0:T(8,128)(2,1)S(1)}, u32[]{:S(2)}, u32[]{:S(2)}) collective-permute-start(bf16[192,768]{1,0:T(8,128)(2,1)S(1)} %add_convert_fusion.9), channel_id=1, source_target_pairs={{0,16},{4,20},{8,24},{12,28},{16,0},{20,4},{24,8},{28,12},{1,17},{... | collective-permute-start | bytes 884744 | tf_op jit(solution)/shard_map/ppermute | solution.py:787
  246.5 21.0 %collective-permute-start.41 = (bf16[192,768]{1,0:T(8,128)(2,1)S(1)}, bf16[192,768]{1,0:T(8,128)(2,1)S(1)}, u32[]{:S(2)}, u32[]{:S(2)}) collective-permute-start(bf16[192,768]{1,0:T(8,128)(2,1)S(1)} %fusion.1), channel_id=1, source_target_pairs={{0,16},{4,20},{8,24},{12,28},{16,0},{20,4},{24,8},{28,12},{1,17},{... | collective-permute-start | bytes 884744 | tf_op jit(solution)/shard_map/ppermute | solution.py:787
  249.7 19.0 %collective-permute-start.48 = (bf16[1280,128]{1,0:T(8,128)(2,1)S(1)}, bf16[1280,128]{1,0:T(8,128)(2,1)S(1)}, u32[]{:S(2)}, u32[]{:S(2)}) collective-permute-start(bf16[1280,128]{1,0:T(8,128)(2,1)S(1)} %pad_maximum_fusion.4), channel_id=1, source_target_pairs={{0,2},{1,3},{2,0},{3,1},{4,6},{5,7},{6,4},{7,5},{8,10},{9,11},{10,... | collective-permute-start | bytes 983048 | tf_op jit(solution)/shard_map/ppermute | solution.py:787
  264.4 27.1 %collective-permute-start.56 = (bf16[192,768]{1,0:T(8,128)(2,1)S(1)}, bf16[192,768]{1,0:T(8,128)(2,1)}, u32[]{:S(2)}, u32[]{:S(2)}) collective-permute-start(bf16[192,768]{1,0:T(8,128)(2,1)S(1)} %add_convert_fusion.8), channel_id=1, source_target_pairs={{0,8},{4,12},{8,0},{12,4},{16,24},{20,28},{24,16},{28,20},{1,9},{5... | collective-permute-start | bytes 884744 | tf_op jit(solution)/shard_map/ppermute | solution.py:787
  267.6 26.7 %collective-permute-start.52 = (bf16[192,768]{1,0:T(8,128)(2,1)S(1)}, bf16[192,768]{1,0:T(8,128)(2,1)}, u32[]{:S(2)}, u32[]{:S(2)}) collective-permute-start(bf16[192,768]{1,0:T(8,128)(2,1)S(1)} %add_convert_fusion.10), channel_id=1, source_target_pairs={{0,8},{4,12},{8,0},{12,4},{16,24},{20,28},{24,16},{28,20},{1,9},{5... | collective-permute-start | bytes 884744 | tf_op jit(solution)/shard_map/ppermute | solution.py:787
  267.7 16.4 %collective-permute-start.43 = (bf16[256,384]{1,0:T(8,128)(2,1)S(1)}, bf16[256,384]{1,0:T(8,128)(2,1)S(1)}, u32[]{:S(2)}, u32[]{:S(2)}) collective-permute-start(bf16[256,384]{1,0:T(8,128)(2,1)S(1)} %get-tuple-element.277), channel_id=1, source_target_pairs={{0,2},{1,3},{2,0},{3,1},{4,6},{5,7},{6,4},{7,5},{8,10},{9,11},{10,... | collective-permute-start | bytes 589832 | tf_op jit(solution)/shard_map/ppermute | solution.py:787
  281.1 15.1 %collective-permute-start.50 = (bf16[1440,128]{1,0:T(8,128)(2,1)}, bf16[1440,128]{1,0:T(8,128)(2,1)}, u32[]{:S(2)}, u32[]{:S(2)}) collective-permute-start(bf16[1440,128]{1,0:T(8,128)(2,1)} %pad_maximum_fusion.1), channel_id=1, source_target_pairs={{0,8},{4,12},{8,0},{12,4},{16,24},{20,28},{24,16},{28,20},{1,9},{5... | collective-permute-start | bytes 1105928 | tf_op jit(solution)/shard_map/ppermute | solution.py:787
  292.7 16.2 %collective-permute-start.57 = (bf16[384,768]{1,0:T(8,128)(2,1)S(1)}, bf16[384,768]{1,0:T(8,128)(2,1)S(1)}, u32[]{:S(2)}, u32[]{:S(2)}) collective-permute-start(bf16[384,768]{1,0:T(8,128)(2,1)S(1)} %maximum_select_fusion.4), channel_id=1, source_target_pairs={{0,4},{4,0},{8,12},{12,8},{16,20},{20,16},{24,28},{28,24},{1,5},{5... | collective-permute-start | bytes 1769480 | tf_op jit(solution)/shard_map/ppermute | solution.py:787
  295.5 25.4 %collective-permute-start.53 = (bf16[384,768]{1,0:T(8,128)(2,1)S(1)}, bf16[384,768]{1,0:T(8,128)(2,1)S(1)}, u32[]{:S(2)}, u32[]{:S(2)}) collective-permute-start(bf16[384,768]{1,0:T(8,128)(2,1)S(1)} %maximum_select_fusion.3), channel_id=1, source_target_pairs={{0,4},{4,0},{8,12},{12,8},{16,20},{20,16},{24,28},{28,24},{1,5},{5... | collective-permute-start | bytes 1769480 | tf_op jit(solution)/shard_map/ppermute | solution.py:787
  297.3 25.6 %collective-permute-start.51 = (bf16[1440,128]{1,0:T(8,128)(2,1)S(1)}, bf16[1440,128]{1,0:T(8,128)(2,1)S(1)}, u32[]{:S(2)}, u32[]{:S(2)}) collective-permute-start(bf16[1440,128]{1,0:T(8,128)(2,1)S(1)} %pad_maximum_fusion.2), channel_id=1, source_target_pairs={{0,16},{4,20},{8,24},{12,28},{16,0},{20,4},{24,8},{28,12},{1,17},{... | collective-permute-start | bytes 1105928 | tf_op jit(solution)/shard_map/ppermute | solution.py:787
  (119 other events, 1046.0 us)

commit v4 on v3

--- a/solution.py
+++ b/solution.py
@@ -12,7 +12,7 @@
 LANES = 128
 CHUNKS = 8
 BIAS_ROWS = 32
-HIDE_ENDS, HIDE_VALUES, HIDE_ATTEND, HIDE_ONE, HIDE_TWO, HIDE_BACK, HIDE_LAST = 20, 20, 20, 20, 40, 60, 15
+HIDE_ENDS, HIDE_VALUES, HIDE_ATTEND, HIDE_ONE, HIDE_TWO, HIDE_BACK, HIDE_LAST, HIDE_JOIN = 20, 20, 20, 20, 40, 60, 15, 30
 SHARE_BITS = 1
 EPSILON = 1e-05
 BF = jnp.bfloat16
@@ -957,12 +957,13 @@
         hides=HIDE_VALUES,
     )
     mixed_blocks = exchange(ema.m, "wa")
-    held = (pack_three.own, pack_one.packed, pack_two.packed, *mixed_blocks)
-    pack_three.own, pack_one.packed, pack_two.packed, *mixed_blocks = lax.optimization_barrier(held)
-    came_three = far_pieces(pack_three)
+    next_two = [later_than(x, ema) for x in next_pieces(came_two)]
+    pack_three.own, came_two[0] = lax.optimization_barrier((pack_three.own, came_two[0]))
+    came_three = [later_than(x, ema) for x in far_pieces(pack_three)]
+    held = (pack_two.packed, next_two[0], came_three[0], *mixed_blocks)
+    pack_two.packed, next_two[0], came_three[0], *mixed_blocks = lax.optimization_barrier(held)
     shards_one = all_shards(pack_one, came_one, next_one)
-    next_two = next_pieces(came_two)
-    next_two[0], came_three[0] = lax.optimization_barrier((next_two[0], came_three[0]))
+    shards_one[1][0] = later_than(shards_one[1][0], ema)
     shards_two = all_shards(pack_two, came_two, next_two)
 
     count = len(jax.tree.leaves(shards_one))
@@ -1108,15 +1109,19 @@
     first_rows, second_rows = summed(first_rows), summed(second_rows)
     first_rows, *rest_sent = lax.optimization_barrier((first_rows, *two.r))
     rest_blocks = exchange(rest_sent, "wa")
+    third_total = all_rows(third_rows, row_bits[:-1], last)
+    second_rows, first_rows = all_rows(second_rows, row_bits[1:-1]), all_rows(first_rows, row_bits[1:-1])
     joined = run(
         functools.partial(ema_join, groups, peers),
         [(meta, SMEM), (last.part, VMEM), (rest_blocks, hbm)],
         Box(grad=((seqs, seq_rows, width), F32, VMEM), block=((seqs, seq_rows, width), BF, VMEM)),
         Box(rest=pltpu.VMEM((tok_rows, 2 * width), BF), sem=sems((peers,))),
-    )
-
-    third_total = all_rows(third_rows, row_bits[:-1], last)
-    second_total, first_total = all_rows(second_rows, row_bits[:-1]), all_rows(first_rows, row_bits[:-1])
+        after=[second_rows, first_rows],
+        hides=HIDE_JOIN,
+    )
+
+    second_total = all_rows(second_rows, row_bits[:1], joined)
+    first_total = all_rows(first_rows, row_bits[:1], joined)
     small = [ffn.sums, one.sums, two.sums, two.rel] + [a.reshape(-1, LANES) for a in (ffn.up_bias, one.bias, two.bias)]
     places = [0]
     for part in small:
@@ -1137,7 +1142,7 @@
     tall = wide // LANES
     lines = [parts[0][i * tall : (i + 1) * tall].reshape(wide) for i in range(5)]
     lines += [parts[1][i * tall : (i + 1) * tall].reshape(wide) for i in range(2)]
-    loss = parts[0][5 * tall, 0] + last.token[0, 0]
+    loss = parts[0][5 * tall, 0] + joined.token[0, 0]
     zsums, rel_grad = parts[2], parts[3][:2].reshape(2 * GROUP)[: rel_bias.shape[0]]
     up_bias_grad, reset_bias_grad, value_bias_grad = (
         lax.dynamic_slice_in_dim(part, me * 8, 8, 0).reshape(8 * LANES)[:units] for part in parts[4:]

time: 332 us -> 309 us (0.931)
  waiting for transfers between devices: 132 us -> 111 us
    ppermute x59, waiting for transfers between devices: 132 us -> 111 us  [swap(): return lax.ppermute(x, axis, [(i, i ^ by) for i in range(size)])]
    unnamed x204 -> x214, local copies, waits for them, and re-layouts: 25.3 us -> 23.8 us
  transfers between devices with their start and end apart: 59 -> 59, of which waited for: 26 -> 28; matrix products, arithmetic and copies ran while one was open for 8% -> 8% of each run, Pallas kernels for 20% -> 23%
where the time goes in v4:
time: 309 us; the launch traced here: 308 us
  waiting for transfers between devices  111 us (36%)
  Pallas kernels  86.3 us (28%)
  starting transfers between devices  50.5 us (16%)
  local copies, waits for them, and re-layouts  29.6 us (10%)
  other arithmetic  26.5 us (9%)
  between operations  4.43 us (1%)
    ppermute x59, waiting for transfers between devices, swap(): return lax.ppermute(x, axis, [(i, i ^ by) for i in range(size)])  111 us
    pallas_call x16, Pallas kernels, run(): pl.pallas_call(kernel, out_shape=(shapes,), in_specs=specs, out_specs=(ou...  86.3 us
    ppermute x59, starting transfers between devices, swap(): return lax.ppermute(x, axis, [(i, i ^ by) for i in range(size)])  50.5 us
    unnamed x214, local copies, waits for them, and re-layouts  23.8 us
    convert_element_type x15, other arithmetic, plus(): return (a.astype(F32) + b.astype(F32)).astype(a.dtype)  11.9 us
  transfers between devices with their start and end apart: 59, of which 28 were waited for; matrix products, arithmetic and copies ran while one was open for 8% of the time, Pallas kernels for 23%

profile of v4, /device:TPU:0, one launch (start us, length us, event | category | flops | bytes accessed | tf_op | source)
XLA Modules:
  0.0 308.3 jit_solution(5857602141268327220)
XLA Ops:
  7.8 3.0 collective-permute-start.1
  11.1 3.0 shard_map.527
  19.3 5.6 %collective-permute-done.1.refs_3__2__0_.refs_1__2__0_ = bf16[400,768]{1,0:T(8,128)(2,1)S(1)} collective-permute-done((bf16[400,768]{1,0:T(8,128)(2,1)}, bf16[400,768]{1,0:T(8,128)(2,1)S(1)}, u32[]{:S(2)}, u32[]{:S(2)}) %collective-permute-start.1) | collective-permute-done | bytes 614432 | tf_op jit(solution)/shard_map/ppermute | solution.py:787
  32.0 2.7 collective-permute-start.7
  40.8 3.2 %collective-permute-done.10.refs_2__3_ = bf16[256,192]{1,0:T(8,128)(2,1)S(1)} collective-permute-done((bf16[256,192]{1,0:T(8,128)(2,1)}, bf16[256,192]{1,0:T(8,128)(2,1)S(1)}, u32[]{:S(2)}, u32[]{:S(2)}) %collective-permute-start.10) | collective-permute-done | bytes 98336 | tf_op jit(solution)/shard_map/ppermute | solution.py:787
  48.5 4.7 %shard_map.530 = (f32[2,512,192]{2,1,0:T(8,128)S(1)}, f32[3,16,8,128]{3,2,1,0:T(8,128)S(1)}, bf16[256,192]{1,0:T(8,128)(2,1)S(1)}, bf16[256,192]{1,0:T(8,128)(2,...) custom-call(s32[3]{0:T(128)S(1)} %pad_add_fusion.refs_0_, ...), custom_call_target="tpu_custom_call" | custom-call | flops 23000000512 | bytes 1 | tf_op jit(solution)/shard_map/pallas_call | solution.py:115
  56.1 5.4 %collective-permute-done.4.refs_4__2__1_.refs_1__2__1_ = bf16[384,768]{1,0:T(8,128)(2,1)S(1)} collective-permute-done((bf16[384,768]{1,0:T(8,128)(2,1)}, bf16[384,768]{1,0:T(8,128)(2,1)S(1)}, u32[]{:S(2)}, u32[]{:S(2)}) %collective-permute-start.4) | collective-permute-done | bytes 589856 | tf_op jit(solution)/shard_map/ppermute | solution.py:787
  62.9 3.5 %collective-permute-done.16.refs_1__3_ = bf16[256,192]{1,0:T(8,128)(2,1)S(1)} collective-permute-done((bf16[256,192]{1,0:T(8,128)(2,1)S(1)}, bf16[256,192]{1,0:T(8,128)(2,1)S(1)}, u32[]{:S(2)}, u32[]{:S(2)}) %collective-permute-start.16) | collective-permute-done | bytes 98336 | tf_op jit(solution)/shard_map/ppermute | solution.py:787
  67.5 3.5 %collective-permute-done.12.refs_3__3__0_.refs_1__3__0_ = bf16[400,768]{1,0:T(8,128)(2,1)S(1)} collective-permute-done((bf16[400,768]{1,0:T(8,128)(2,1)S(1)}, bf16[400,768]{1,0:T(8,128)(2,1)S(1)}, u32[]{:S(2)}, u32[]{:S(2)}) %collective-permute-start.12) | collective-permute-done | bytes 614432 | tf_op jit(solution)/shard_map/ppermute | solution.py:787
  74.6 13.7 %shard_map.531 = (bf16[256,768]{1,0:T(8,128)(2,1)}, bf16[256,768]{1,0:T(8,128)(2,1)}, f32[256,128]{1,0:T(8,128)}, bf16[256,128]{1,0:T(8,128)(2,1)}, bf16[256,128...) custom-call(s32[3]{0:T(128)} %copy-done.36, ...), custom_call_target="tpu_custom_call" | custom-call | flops 23000000512 | bytes 1 | tf_op jit(solution)/shard_map/pallas_call | solution.py:115
  93.3 14.5 %shard_map.532 = (f32[256,768]{1,0:T(8,128)S(1)}, bf16[4,256,192]{2,1,0:T(8,128)(2,1)S(1)}, f32[40,128]{1,0:T(8,128)S(1)}, f32[4,8,128]{2,1,0:T(8,128)S(1)}, bf1...) custom-call(s32[3]{0:T(128)S(1)} %copy-done.37, s32[2]{0:T(128)S(1)} %copy-done.48, ...), custom_call_target="tpu_custom_call" | custom-call | flops 1 | bytes 1 | tf_op jit(solution)/shard_map/pallas_call | solution.py:115
  108.1 4.7 %collective-permute-done.24 = bf16[2,768,768]{2,1,0:T(8,128)(2,1)} collective-permute-done((bf16[2,768,768]{2,1,0:T(8,128)(2,1)}, bf16[2,768,768]{2,1,0:T(8,128)(2,1)}, u32[]{:S(2)}, u32[]{:S(2)}) %collective-permute-start.24) | collective-permute-done | bytes 2359328 | tf_op jit(solution)/shard_map/ppermute | solution.py:787
  112.8 3.0 add_convert_fusion.2.refs_11__0_
  118.8 11.7 %shard_map.533 = (f32[256,768]{1,0:T(8,128)S(1)}, f32[16,128]{1,0:T(8,128)S(1)}, f32[4,256,192]{2,1,0:T(8,128)}, bf16[4,256,384]{2,1,0:T(8,128)(2,1)S(1)}, bf16[...) custom-call(s32[3]{0:T(128)S(1)} %copy-done.37, ...), custom_call_target="tpu_custom_call" | custom-call | flops 23000000512 | bytes 1 | tf_op jit(solution)/shard_map/pallas_call | solution.py:115
  133.3 17.1 %shard_map.534 = (f32[8,128]{1,0:T(8,128)S(1)}, f32[8,128]{1,0:T(8,128)S(1)}, f32[768,128]{1,0:T(8,128)S(1)}, f32[4,8,128]{2,1,0:T(8,128)S(1)}, bf16[2,768,768]{...) custom-call(s32[3]{0:T(128)S(1)} %copy-done.37, ...), custom_call_target="tpu_custom_call" | custom-call | flops 1 | bytes 1 | tf_op jit(solution)/shard_map/pallas_call | solution.py:115
  156.2 3.9 %add_convert_fusion.refs_5__1_ = bf16[2,768,768]{2,1,0:T(8,128)(2,1)} fusion(bf16[2,768,768]{2,1,0:T(8,128)(2,1)} %collective-permute-done.29, bf16[2,768,768]{2,1,0:T(8,128)(2,1)S(1)} %copy-done.81), kind=kLoop, calls=%fused_computation | loop fusion | flops 4718592 | bytes 7077888 | tf_op jit(solution)/shard_map/convert_element_type | solution.py:830
  161.4 3.5 %shard_map.536 = (f32[3,512,128]{2,1,0:T(8,128)S(1)}, f32[3,16,8,128]{3,2,1,0:T(8,128)S(1)}, f32[3,16,128]{2,1,0:T(8,128)S(1)}, f32[8,128]{1,0:T(8,128)S(1)}) custom-call(s32[3]{0:T(128)S(1)} %copy-done.37, bf16[256,192]{1,0:T(8,128)(2,1)S(1)} %get-tuple-element.253.refs_1__0_, bf16[256,192]{1,0:T(8,128)(2,1)S(1)} %collective-permute-done.25.refs_1__1_, ...), custom_call_target="tpu_custom_call" | custom-call | flops 69000003584 | bytes 1 | tf_op jit(solution)/shard_map/pallas_call | solution.py:115
  168.8 4.0 %collective-permute-done.34 = bf16[1,384,768]{2,1,0:T(8,128)(2,1)S(1)} collective-permute-done((bf16[1,384,768]{2,1,0:T(8,128)(2,1)S(1)}, bf16[1,384,768]{2,1,0:T(8,128)(2,1)S(1)}, u32[]{:S(2)}, u32[]{:S(2)}) %collective-permute-start.34) | collective-permute-done | bytes 589856 | tf_op jit(solution)/shard_map/ppermute | solution.py:787
  175.2 6.6 %collective-permute-done.32.refs_0__0_.refs_8__1_ = f32[3,16,128]{2,1,0:T(8,128)S(1)} collective-permute-done((f32[3,16,128]{2,1,0:T(8,128)S(1)}, f32[3,16,128]{2,1,0:T(8,128)S(1)}, u32[]{:S(2)}, u32[]{:S(2)}) %collective-permute-start.32) | collective-permute-done | bytes 24608 | tf_op jit(solution)/shard_map/ppermute | solution.py:787
  181.9 2.6 collective-permute-start.36
  185.0 12.7 %collective-permute-done.33.refs_0__0_.refs_8__2_ = f32[3,16,128]{2,1,0:T(8,128)S(1)} collective-permute-done((f32[3,16,128]{2,1,0:T(8,128)S(1)}, f32[3,16,128]{2,1,0:T(8,128)S(1)}, u32[]{:S(2)}, u32[]{:S(2)}) %collective-permute-start.33) | collective-permute-done | bytes 24608 | tf_op jit(solution)/shard_map/ppermute | solution.py:787
  202.6 11.5 %shard_map.540 = (f32[3,512,128]{2,1,0:T(8,128)S(1)}, f32[2,40,128]{2,1,0:T(8,128)S(1)}, f32[8,128]{1,0:T(8,128)S(1)}) custom-call(s32[3]{0:T(128)S(1)} %copy-done.37, bf16[2,512,192]{2,1,0:T(8,128)(2,1)S(1)} %copy-done.20, f32[3,512,128]{2,1,0:T(8,128)S(1)} %get-tuple-element.268.refs_2_, f32[16,192]{1,0:T(8,128)S(1)} %bitcast.79, f32[16,192]{1,0:T(8,128)S(1)} %bitcast.74, ...), custom_call_target="tpu_custom_call" | custom-call | flops 17250000896 | bytes 1 | tf_op jit(solution)/shard_map/pallas_call | solution.py:115
  220.2 10.7 %collective-permute-done.40 = bf16[192,768]{1,0:T(8,128)(2,1)S(1)} collective-permute-done((bf16[192,768]{1,0:T(8,128)(2,1)S(1)}, bf16[192,768]{1,0:T(8,128)(2,1)S(1)}, u32[]{:S(2)}, u32[]{:S(2)}) %collective-permute-start.40) | collective-permute-done | bytes 294944 | tf_op jit(solution)/shard_map/ppermute | solution.py:787
  231.3 3.2 %collective-permute-done.46 = bf16[192,768]{1,0:T(8,128)(2,1)S(1)} collective-permute-done((bf16[192,768]{1,0:T(8,128)(2,1)S(1)}, bf16[192,768]{1,0:T(8,128)(2,1)S(1)}, u32[]{:S(2)}, u32[]{:S(2)}) %collective-permute-start.46) | collective-permute-done | bytes 294944 | tf_op jit(solution)/shard_map/ppermute | solution.py:787
  234.5 3.1 collective-permute-start.47
  238.5 13.9 %collective-permute-done.41 = bf16[192,768]{1,0:T(8,128)(2,1)S(1)} collective-permute-done((bf16[192,768]{1,0:T(8,128)(2,1)S(1)}, bf16[192,768]{1,0:T(8,128)(2,1)S(1)}, u32[]{:S(2)}, u32[]{:S(2)}) %collective-permute-start.41) | collective-permute-done | bytes 294944 | tf_op jit(solution)/shard_map/ppermute | solution.py:787
  252.5 3.0 collective-permute-done.47
  261.0 4.0 %collective-permute-done.48 = bf16[192,768]{1,0:T(8,128)(2,1)S(1)} collective-permute-done((bf16[192,768]{1,0:T(8,128)(2,1)S(1)}, bf16[192,768]{1,0:T(8,128)(2,1)S(1)}, u32[]{:S(2)}, u32[]{:S(2)}) %collective-permute-start.48) | collective-permute-done | bytes 294944 | tf_op jit(solution)/shard_map/ppermute | solution.py:787
  266.9 2.4 collective-permute-done.53
  271.8 2.3 collective-permute-start.54
  278.3 3.3 %collective-permute-done.54 = bf16[1440,128]{1,0:T(8,128)(2,1)} collective-permute-done((bf16[1440,128]{1,0:T(8,128)(2,1)}, bf16[1440,128]{1,0:T(8,128)(2,1)}, u32[]{:S(2)}, u32[]{:S(2)}) %collective-permute-start.54) | collective-permute-done | bytes 368672 | tf_op jit(solution)/shard_map/ppermute | solution.py:787
  287.0 7.4 %collective-permute-done.56 = bf16[384,768]{1,0:T(8,128)(2,1)} collective-permute-done((bf16[384,768]{1,0:T(8,128)(2,1)S(1)}, bf16[384,768]{1,0:T(8,128)(2,1)}, u32[]{:S(2)}, u32[]{:S(2)}) %collective-permute-start.56) | collective-permute-done | bytes 589856 | tf_op jit(solution)/shard_map/ppermute | solution.py:787
  (396 shorter events, 106.6 us)
Async XLA Ops:
  7.8 17.0 %collective-permute-start.1 = (bf16[400,768]{1,0:T(8,128)(2,1)}, bf16[400,768]{1,0:T(8,128)(2,1)S(1)}, u32[]{:S(2)}, u32[]{:S(2)}) collective-permute-start(bf16[400,768]{1,0:T(8,128)(2,1)} %get-tuple-element.179.refs_4__0_), channel_id=1, source_target_pairs={{0,2},{1,3},{2,0},{3,1},{4,6},{5,7},{6,4},{7,5},{8,10},{9,11},{10,... | collective-permute-start | bytes 1843208 | tf_op jit(solution)/shard_map/ppermute | solution.py:787
  24.9 23.5 %collective-permute-start.11 = (bf16[400,768]{1,0:T(8,128)(2,1)S(1)}, bf16[400,768]{1,0:T(8,128)(2,1)S(1)}, u32[]{:S(2)}, u32[]{:S(2)}) collective-permute-start(bf16[400,768]{1,0:T(8,128)(2,1)S(1)} %collective-permute-done.1.refs_3__2__0_.refs_1__2__0_), channel_id=1, source_target_pairs={{0,4},{4,0},{8,12},{12,8},{16,20},{20,16},{24,28},{28,24},{1,5},{5... | collective-permute-start | bytes 1843208 | tf_op jit(solution)/shard_map/ppermute | solution.py:787
  26.6 19.8 %collective-permute-start.2 = (bf16[384,768]{1,0:T(8,128)(2,1)}, bf16[384,768]{1,0:T(8,128)(2,1)}, u32[]{:S(2)}, u32[]{:S(2)}) collective-permute-start(bf16[384,768]{1,0:T(8,128)(2,1)} %copy-done.60), channel_id=1, source_target_pairs={{0,2},{1,3},{2,0},{3,1},{4,6},{5,7},{6,4},{7,5},{8,10},{9,11},{10,... | collective-permute-start | bytes 1769480 | tf_op jit(solution)/shard_map/ppermute | solution.py:787
  44.1 23.4 %collective-permute-start = (bf16[800,768]{1,0:T(8,128)(2,1)S(1)}, bf16[800,768]{1,0:T(8,128)(2,1)S(1)}, u32[]{:S(2)}, u32[]{:S(2)}) collective-permute-start(bf16[800,768]{1,0:T(8,128)(2,1)S(1)} %get-tuple-element.178.refs_3__0__0_.refs_1__0__0_), channel_id=1, source_target_pairs={{0,1},{1,0},{2,3},{3,2},{4,5},{5,4},{6,7},{7,6},{8,9},{9,8},{10,11... | collective-permute-start | bytes 3686408 | tf_op jit(solution)/shard_map/ppermute | solution.py:787
  46.3 15.3 %collective-permute-start.3 = (bf16[384,768]{1,0:T(8,128)(2,1)S(1)}, bf16[384,768]{1,0:T(8,128)(2,1)}, u32[]{:S(2)}, u32[]{:S(2)}) collective-permute-start(bf16[384,768]{1,0:T(8,128)(2,1)S(1)} %get-tuple-element.192), channel_id=1, source_target_pairs={{0,2},{1,3},{2,0},{3,1},{4,6},{5,7},{6,4},{7,5},{8,10},{9,11},{10,... | collective-permute-start | bytes 1769480 | tf_op jit(solution)/shard_map/ppermute | solution.py:787
  47.8 13.7 %collective-permute-start.4 = (bf16[384,768]{1,0:T(8,128)(2,1)}, bf16[384,768]{1,0:T(8,128)(2,1)S(1)}, u32[]{:S(2)}, u32[]{:S(2)}) collective-permute-start(bf16[384,768]{1,0:T(8,128)(2,1)} %collective-permute-done.2.refs_8__0_.refs_4__2__0_.refs_1__2__0_), channel_id=1, source_target_pairs={{0,4},{4,0},{8,12},{12,8},{16,20},{20,16},{24,28},{28,24},{1,5},{5... | collective-permute-start | bytes 1769480 | tf_op jit(solution)/shard_map/ppermute | solution.py:787
  71.0 17.6 %collective-permute-start.20 = (bf16[768,768]{1,0:T(8,128)(2,1)}, bf16[768,768]{1,0:T(8,128)(2,1)}, u32[]{:S(2)}, u32[]{:S(2)}) collective-permute-start(bf16[768,768]{1,0:T(8,128)(2,1)} %get-tuple-element.230.refs_2__0__0_), channel_id=1, source_target_pairs={{0,1},{1,0},{2,3},{3,2},{4,5},{5,4},{6,7},{7,6},{8,9},{9,8},{10,11... | collective-permute-start | bytes 3538952 | tf_op jit(solution)/shard_map/ppermute | solution.py:787
  71.1 17.2 %collective-permute-start.21 = (bf16[384,768]{1,0:T(8,128)(2,1)}, bf16[384,768]{1,0:T(8,128)(2,1)S(1)}, u32[]{:S(2)}, u32[]{:S(2)}) collective-permute-start(bf16[384,768]{1,0:T(8,128)(2,1)} %collective-permute-done.3.refs_2__2__0_), channel_id=1, source_target_pairs={{0,4},{4,0},{8,12},{12,8},{16,20},{20,16},{24,28},{28,24},{1,5},{5... | collective-permute-start | bytes 1769480 | tf_op jit(solution)/shard_map/ppermute | solution.py:787
  71.9 16.7 %collective-permute-start.22 = (bf16[384,768]{1,0:T(8,128)(2,1)}, bf16[384,768]{1,0:T(8,128)(2,1)S(1)}, u32[]{:S(2)}, u32[]{:S(2)}) collective-permute-start(bf16[384,768]{1,0:T(8,128)(2,1)} %collective-permute-done.3.refs_2__2__0_), channel_id=1, source_target_pairs={{0,1},{1,0},{2,3},{3,2},{4,5},{5,4},{6,7},{7,6},{8,9},{9,8},{10,11... | collective-permute-start | bytes 1769480 | tf_op jit(solution)/shard_map/ppermute | solution.py:787
  117.3 35.2 %collective-permute-start.30 = (bf16[2,384,768]{2,1,0:T(8,128)(2,1)S(1)}, bf16[2,384,768]{2,1,0:T(8,128)(2,1)}, u32[]{:S(2)}, u32[]{:S(2)}) collective-permute-start(bf16[2,384,768]{2,1,0:T(8,128)(2,1)S(1)} %constant_dynamic-slice_fusion.5), channel_id=1, source_target_pairs={{0,4},{4,0},{8,12},{12,8},{16,20},{20,16},{24,28},{28,24},{1,5},{5... | collective-permute-start | bytes 3538952 | tf_op jit(solution)/shard_map/ppermute | solution.py:787
  133.2 21.6 %collective-permute-start.28 = (bf16[2,768,768]{2,1,0:T(8,128)(2,1)}, bf16[2,768,768]{2,1,0:T(8,128)(2,1)S(1)}, u32[]{:S(2)}, u32[]{:S(2)}) collective-permute-start(bf16[2,768,768]{2,1,0:T(8,128)(2,1)} %get-tuple-element.259), channel_id=1, source_target_pairs={{0,1},{1,0},{2,3},{3,2},{4,5},{5,4},{6,7},{7,6},{8,9},{9,8},{10,11... | collective-permute-start | bytes 7077896 | tf_op jit(solution)/shard_map/ppermute | solution.py:787
  154.8 18.0 %collective-permute-start.34 = (bf16[1,384,768]{2,1,0:T(8,128)(2,1)S(1)}, bf16[1,384,768]{2,1,0:T(8,128)(2,1)S(1)}, u32[]{:S(2)}, u32[]{:S(2)}) collective-permute-start(bf16[1,384,768]{2,1,0:T(8,128)(2,1)S(1)} %slice.261), channel_id=1, source_target_pairs={{0,2},{1,3},{2,0},{3,1},{4,6},{5,7},{6,4},{7,5},{8,10},{9,11},{10,... | collective-permute-start | bytes 1769480 | tf_op jit(solution)/shard_map/ppermute | solution.py:787
  165.9 32.6 %collective-permute-start.38 = (bf16[1,768,768]{2,1,0:T(8,128)(2,1)S(1)}, bf16[1,768,768]{2,1,0:T(8,128)(2,1)S(1)}, u32[]{:S(2)}, u32[]{:S(2)}) collective-permute-start(bf16[1,768,768]{2,1,0:T(8,128)(2,1)S(1)} %slice.263), channel_id=1, source_target_pairs={{0,2},{1,3},{2,0},{3,1},{4,6},{5,7},{6,4},{7,5},{8,10},{9,11},{10,... | collective-permute-start | bytes 3538952 | tf_op jit(solution)/shard_map/ppermute | solution.py:787
  166.7 32.1 %collective-permute-start.37 = (bf16[2,384,768]{2,1,0:T(8,128)(2,1)S(1)}, bf16[2,384,768]{2,1,0:T(8,128)(2,1)}, u32[]{:S(2)}, u32[]{:S(2)}) collective-permute-start(bf16[2,384,768]{2,1,0:T(8,128)(2,1)S(1)} %constant_dynamic-slice_fusion.4), channel_id=1, source_target_pairs={{0,4},{4,0},{8,12},{12,8},{16,20},{20,16},{24,28},{28,24},{1,5},{5... | collective-permute-start | bytes 3538952 | tf_op jit(solution)/shard_map/ppermute | solution.py:787
  181.9 15.8 %collective-permute-start.36 = (bf16[192,768]{1,0:T(8,128)(2,1)S(1)}, bf16[192,768]{1,0:T(8,128)(2,1)S(1)}, u32[]{:S(2)}, u32[]{:S(2)}) collective-permute-start(bf16[192,768]{1,0:T(8,128)(2,1)S(1)} %fusion.2), channel_id=1, source_target_pairs={{0,16},{4,20},{8,24},{12,28},{16,0},{20,4},{24,8},{28,12},{1,17},{... | collective-permute-start | bytes 884744 | tf_op jit(solution)/shard_map/ppermute | solution.py:787
  184.6 13.1 %collective-permute-start.33 = (f32[3,16,128]{2,1,0:T(8,128)S(1)}, f32[3,16,128]{2,1,0:T(8,128)S(1)}, u32[]{:S(2)}, u32[]{:S(2)}) collective-permute-start(f32[3,16,128]{2,1,0:T(8,128)S(1)} %add_select_fusion), channel_id=1, source_target_pairs={{0,16},{4,20},{8,24},{12,28},{16,0},{20,4},{24,8},{28,12},{1,17},{... | collective-permute-start | bytes 73736 | tf_op jit(solution)/shard_map/ppermute | solution.py:787
  197.8 19.0 %collective-permute-start.50 = (bf16[192,768]{1,0:T(8,128)(2,1)S(1)}, bf16[192,768]{1,0:T(8,128)(2,1)S(1)}, u32[]{:S(2)}, u32[]{:S(2)}) collective-permute-start(bf16[192,768]{1,0:T(8,128)(2,1)S(1)} %add_convert_fusion.11.refs_10__0_), channel_id=1, source_target_pairs={{0,8},{4,12},{8,0},{12,4},{16,24},{20,28},{24,16},{28,20},{1,9},{5... | collective-permute-start | bytes 884744 | tf_op jit(solution)/shard_map/ppermute | solution.py:787
  200.5 15.0 %collective-permute-start.39 = (bf16[1,384,768]{2,1,0:T(8,128)(2,1)S(1)}, bf16[1,384,768]{2,1,0:T(8,128)(2,1)S(1)}, u32[]{:S(2)}, u32[]{:S(2)}) collective-permute-start(bf16[1,384,768]{2,1,0:T(8,128)(2,1)S(1)} %slice.265), channel_id=1, source_target_pairs={{0,2},{1,3},{2,0},{3,1},{4,6},{5,7},{6,4},{7,5},{8,10},{9,11},{10,... | collective-permute-start | bytes 1769480 | tf_op jit(solution)/shard_map/ppermute | solution.py:787
  202.0 14.8 %collective-permute-start.45 = (bf16[384,768]{1,0:T(8,128)(2,1)S(1)}, bf16[384,768]{1,0:T(8,128)(2,1)S(1)}, u32[]{:S(2)}, u32[]{:S(2)}) collective-permute-start(bf16[384,768]{1,0:T(8,128)(2,1)S(1)} %dynamic-slice_bitcast_fusion), channel_id=1, source_target_pairs={{0,4},{4,0},{8,12},{12,8},{16,20},{20,16},{24,28},{28,24},{1,5},{5... | collective-permute-start | bytes 1769480 | tf_op jit(solution)/shard_map/ppermute | solution.py:787
  216.9 38.8 %collective-permute-start.58 = (bf16[384,768]{1,0:T(8,128)(2,1)S(1)}, bf16[384,768]{1,0:T(8,128)(2,1)S(1)}, u32[]{:S(2)}, u32[]{:S(2)}) collective-permute-start(bf16[384,768]{1,0:T(8,128)(2,1)S(1)} %maximum_select_fusion.5), channel_id=1, source_target_pairs={{0,4},{4,0},{8,12},{12,8},{16,20},{20,16},{24,28},{28,24},{1,5},{5... | collective-permute-start | bytes 1769480 | tf_op jit(solution)/shard_map/ppermute | solution.py:787
  217.7 13.2 %collective-permute-start.40 = (bf16[192,768]{1,0:T(8,128)(2,1)S(1)}, bf16[192,768]{1,0:T(8,128)(2,1)S(1)}, u32[]{:S(2)}, u32[]{:S(2)}) collective-permute-start(bf16[192,768]{1,0:T(8,128)(2,1)S(1)} %dynamic-slice_bitcast_fusion.1), channel_id=1, source_target_pairs={{0,8},{4,12},{8,0},{12,4},{16,24},{20,28},{24,16},{28,20},{1,9},{5... | collective-permute-start | bytes 884744 | tf_op jit(solution)/shard_map/ppermute | solution.py:787
  218.8 15.6 %collective-permute-start.46 = (bf16[192,768]{1,0:T(8,128)(2,1)S(1)}, bf16[192,768]{1,0:T(8,128)(2,1)S(1)}, u32[]{:S(2)}, u32[]{:S(2)}) collective-permute-start(bf16[192,768]{1,0:T(8,128)(2,1)S(1)} %constant_dynamic-slice_fusion.3), channel_id=1, source_target_pairs={{0,8},{4,12},{8,0},{12,4},{16,24},{20,28},{24,16},{28,20},{1,9},{5... | collective-permute-start | bytes 884744 | tf_op jit(solution)/shard_map/ppermute | solution.py:787
  220.2 17.4 %collective-permute-start.51 = (bf16[1280,128]{1,0:T(8,128)(2,1)S(1)}, bf16[1280,128]{1,0:T(8,128)(2,1)S(1)}, u32[]{:S(2)}, u32[]{:S(2)}) collective-permute-start(bf16[1280,128]{1,0:T(8,128)(2,1)S(1)} %pad_maximum_fusion.3), channel_id=1, source_target_pairs={{0,1},{1,0},{2,3},{3,2},{4,5},{5,4},{6,7},{7,6},{8,9},{9,8},{10,11... | collective-permute-start | bytes 983048 | tf_op jit(solution)/shard_map/ppermute | solution.py:787
  231.0 21.3 %collective-permute-start.41 = (bf16[192,768]{1,0:T(8,128)(2,1)S(1)}, bf16[192,768]{1,0:T(8,128)(2,1)S(1)}, u32[]{:S(2)}, u32[]{:S(2)}) collective-permute-start(bf16[192,768]{1,0:T(8,128)(2,1)S(1)} %fusion.1), channel_id=1, source_target_pairs={{0,16},{4,20},{8,24},{12,28},{16,0},{20,4},{24,8},{28,12},{1,17},{... | collective-permute-start | bytes 884744 | tf_op jit(solution)/shard_map/ppermute | solution.py:787
  234.5 21.0 %collective-permute-start.47 = (bf16[192,768]{1,0:T(8,128)(2,1)S(1)}, bf16[192,768]{1,0:T(8,128)(2,1)S(1)}, u32[]{:S(2)}, u32[]{:S(2)}) collective-permute-start(bf16[192,768]{1,0:T(8,128)(2,1)S(1)} %add_convert_fusion.9), channel_id=1, source_target_pairs={{0,16},{4,20},{8,24},{12,28},{16,0},{20,4},{24,8},{28,12},{1,17},{... | collective-permute-start | bytes 884744 | tf_op jit(solution)/shard_map/ppermute | solution.py:787
  237.7 20.3 %collective-permute-start.52 = (bf16[1280,128]{1,0:T(8,128)(2,1)S(1)}, bf16[1280,128]{1,0:T(8,128)(2,1)S(1)}, u32[]{:S(2)}, u32[]{:S(2)}) collective-permute-start(bf16[1280,128]{1,0:T(8,128)(2,1)S(1)} %pad_maximum_fusion.4), channel_id=1, source_target_pairs={{0,2},{1,3},{2,0},{3,1},{4,6},{5,7},{6,4},{7,5},{8,10},{9,11},{10,... | collective-permute-start | bytes 983048 | tf_op jit(solution)/shard_map/ppermute | solution.py:787
  252.4 12.8 %collective-permute-start.49 = (bf16[192,768]{1,0:T(8,128)(2,1)S(1)}, bf16[192,768]{1,0:T(8,128)(2,1)S(1)}, u32[]{:S(2)}, u32[]{:S(2)}) collective-permute-start(bf16[192,768]{1,0:T(8,128)(2,1)S(1)} %add_convert_fusion.10), channel_id=1, source_target_pairs={{0,8},{4,12},{8,0},{12,4},{16,24},{20,28},{24,16},{28,20},{1,9},{5... | collective-permute-start | bytes 884744 | tf_op jit(solution)/shard_map/ppermute | solution.py:787
  255.7 16.2 %collective-permute-start.42 = (bf16[256,384]{1,0:T(8,128)(2,1)S(1)}, bf16[256,384]{1,0:T(8,128)(2,1)S(1)}, u32[]{:S(2)}, u32[]{:S(2)}) collective-permute-start(bf16[256,384]{1,0:T(8,128)(2,1)S(1)} %get-tuple-element.293), channel_id=1, source_target_pairs={{0,1},{1,0},{2,3},{3,2},{4,5},{5,4},{6,7},{7,6},{8,9},{9,8},{10,11... | collective-permute-start | bytes 589832 | tf_op jit(solution)/shard_map/ppermute | solution.py:787
  255.8 18.3 %collective-permute-start.43 = (bf16[256,384]{1,0:T(8,128)(2,1)S(1)}, bf16[256,384]{1,0:T(8,128)(2,1)S(1)}, u32[]{:S(2)}, u32[]{:S(2)}) collective-permute-start(bf16[256,384]{1,0:T(8,128)(2,1)S(1)} %get-tuple-element.294), channel_id=1, source_target_pairs={{0,2},{1,3},{2,0},{3,1},{4,6},{5,7},{6,4},{7,5},{8,10},{9,11},{10,... | collective-permute-start | bytes 589832 | tf_op jit(solution)/shard_map/ppermute | solution.py:787
  265.2 18.0 %collective-permute-start.57 = (bf16[384,768]{1,0:T(8,128)(2,1)S(1)}, bf16[384,768]{1,0:T(8,128)(2,1)}, u32[]{:S(2)}, u32[]{:S(2)}) collective-permute-start(bf16[384,768]{1,0:T(8,128)(2,1)S(1)} %maximum_select_fusion.3.refs_4__0_), channel_id=1, source_target_pairs={{0,4},{4,0},{8,12},{12,8},{16,20},{20,16},{24,28},{28,24},{1,5},{5... | collective-permute-start | bytes 1769480 | tf_op jit(solution)/shard_map/ppermute | solution.py:787
  269.4 25.0 %collective-permute-start.56 = (bf16[384,768]{1,0:T(8,128)(2,1)S(1)}, bf16[384,768]{1,0:T(8,128)(2,1)}, u32[]{:S(2)}, u32[]{:S(2)}) collective-permute-start(bf16[384,768]{1,0:T(8,128)(2,1)S(1)} %maximum_select_fusion.4.refs_4__1_), channel_id=1, source_target_pairs={{0,4},{4,0},{8,12},{12,8},{16,20},{20,16},{24,28},{28,24},{1,5},{5... | collective-permute-start | bytes 1769480 | tf_op jit(solution)/shard_map/ppermute | solution.py:787
  282.8 17.1 %collective-permute-start.55 = (bf16[1440,128]{1,0:T(8,128)(2,1)S(1)}, bf16[1440,128]{1,0:T(8,128)(2,1)S(1)}, u32[]{:S(2)}, u32[]{:S(2)}) collective-permute-start(bf16[1440,128]{1,0:T(8,128)(2,1)S(1)} %pad_maximum_fusion.2), channel_id=1, source_target_pairs={{0,16},{4,20},{8,24},{12,28},{16,0},{20,4},{24,8},{28,12},{1,17},{... | collective-permute-start | bytes 1105928 | tf_op jit(solution)/shard_map/ppermute | solution.py:787
  (124 other events, 1012.9 us)

commit v5 on v4

--- a/solution.py
+++ b/solution.py
@@ -906,6 +906,7 @@
             Box(packed=(shape, BF, VMEM), own=((shape[0] // pieces,) + shape[1:], BF, VMEM), **outs),
             scratch or Box(),
             vectors=vectors,
+            limit=62,
         )
 
     one_shape, two_shape, three_shape = (wide + BIAS_ROWS, 2 * units), (2 * width + units, wide), (depth + hidden, wide)
@@ -1036,6 +1037,7 @@
         ),
         after=[third_parts],
         hides=HIDE_ONE,
+        limit=56,
     )
     vec = Box(
         zeta=zeta_proj, query_gain=query_gain, key_gain=key_gain, positions=positions,

time: 309 us -> 306 us (level)
  Pallas kernels: 86.3 us -> 92.1 us
  waiting for transfers between devices: 111 us -> 106 us
  local copies, waits for them, and re-layouts: 29.6 us -> 25.3 us
    pallas_call x16, Pallas kernels: 86.3 us -> 92.1 us  [run(): pl.pallas_call(kernel, out_shape=(shapes,), in_specs=specs, out_specs=(ou...]
    ppermute x59, waiting for transfers between devices: 111 us -> 106 us  [swap(): return lax.ppermute(x, axis, [(i, i ^ by) for i in range(size)])]
    unnamed x214 -> x174, local copies, waits for them, and re-layouts: 23.8 us -> 19.4 us
  transfers between devices with their start and end apart: 59 -> 59, of which waited for: 28 -> 27; matrix products, arithmetic and copies ran while one was open for 8% -> 8% of each run, Pallas kernels for 23% -> 24%
where the time goes in v5:
time: 306 us
  waiting for transfers between devices  106 us (35%)
  Pallas kernels  92.1 us (30%)
  starting transfers between devices  51 us (17%)
  other arithmetic  26.7 us (9%)
  local copies, waits for them, and re-layouts  25.3 us (8%)
  between operations  4.35 us (1%)
    ppermute x59, waiting for transfers between devices, swap(): return lax.ppermute(x, axis, [(i, i ^ by) for i in range(size)])  106 us
    pallas_call x16, Pallas kernels, run(): pl.pallas_call(kernel, out_shape=(shapes,), in_specs=specs, out_specs=(ou...  92.1 us
    ppermute x59, starting transfers between devices, swap(): return lax.ppermute(x, axis, [(i, i ^ by) for i in range(size)])  51 us
    unnamed x174, local copies, waits for them, and re-layouts  19.4 us
    convert_element_type x15, other arithmetic, plus(): return (a.astype(F32) + b.astype(F32)).astype(a.dtype)  12.3 us
  transfers between devices with their start and end apart: 59, of which 27 were waited for; matrix products, arithmetic and copies ran while one was open for 8% of the time, Pallas kernels for 24%

profile of v5, /device:TPU:0, one launch (start us, length us, event | category | flops | bytes accessed | tf_op | source)
XLA Modules:
  0.0 305.6 jit_solution(18386597426895851281)
XLA Ops:
  1.3 3.4 %shard_map.526 = (bf16[800,768]{1,0:T(8,128)(2,1)}, bf16[400,768]{1,0:T(8,128)(2,1)}, f32[8,256]{1,0:T(8,128)}, f32[8,128]{1,0:T(8,128)}) custom-call(s32[3]{0:T(128)} %pad_add_fusion.refs_0_, bf16[768,384]{1,0:T(8,128)(2,1)} %refs_1_.5, bf16[768,384]{1,0:T(8,128)(2,1)} %refs_2_.1, f32[255]{0:T(256)} %refs_3_.1, f32[384]{0:T(512)} %refs_4__0_.1, ...), custom_call_target="tpu_custom_call" | custom-call | flops 1 | bytes 1 | tf_op jit(solution)/shard_map/pallas_call | solution.py:115
  4.7 3.0 collective-permute-start.1
  9.2 3.0 shard_map.527
  15.1 2.6 shard_map.529
  17.7 4.1 %collective-permute-done.1.refs_3__2__0_.refs_1__2__0_ = bf16[400,768]{1,0:T(8,128)(2,1)S(1)} collective-permute-done((bf16[400,768]{1,0:T(8,128)(2,1)}, bf16[400,768]{1,0:T(8,128)(2,1)S(1)}, u32[]{:S(2)}, u32[]{:S(2)}) %collective-permute-start.1) | collective-permute-done | bytes 614432 | tf_op jit(solution)/shard_map/ppermute | solution.py:787
  29.0 2.7 collective-permute-start.7
  36.9 4.0 %collective-permute-done.10.refs_2__3_ = bf16[256,192]{1,0:T(8,128)(2,1)S(1)} collective-permute-done((bf16[256,192]{1,0:T(8,128)(2,1)S(1)}, bf16[256,192]{1,0:T(8,128)(2,1)S(1)}, u32[]{:S(2)}, u32[]{:S(2)}) %collective-permute-start.10) | collective-permute-done | bytes 98336 | tf_op jit(solution)/shard_map/ppermute | solution.py:787
  49.4 4.7 %shard_map.530 = (f32[2,512,192]{2,1,0:T(8,128)S(1)}, f32[3,16,8,128]{3,2,1,0:T(8,128)S(1)}, bf16[256,192]{1,0:T(8,128)(2,1)S(1)}, bf16[256,192]{1,0:T(8,128)(2,...) custom-call(s32[3]{0:T(128)S(1)} %copy-done.28, ...), custom_call_target="tpu_custom_call" | custom-call | flops 23000000512 | bytes 1 | tf_op jit(solution)/shard_map/pallas_call | solution.py:115
  58.9 4.4 %collective-permute-done.15.refs_1__2_ = bf16[256,192]{1,0:T(8,128)(2,1)S(1)} collective-permute-done((bf16[256,192]{1,0:T(8,128)(2,1)S(1)}, bf16[256,192]{1,0:T(8,128)(2,1)S(1)}, u32[]{:S(2)}, u32[]{:S(2)}) %collective-permute-start.15) | collective-permute-done | bytes 98336 | tf_op jit(solution)/shard_map/ppermute | solution.py:787
  67.2 3.3 %collective-permute-done.12.refs_3__3__0_.refs_1__3__0_ = bf16[400,768]{1,0:T(8,128)(2,1)S(1)} collective-permute-done((bf16[400,768]{1,0:T(8,128)(2,1)S(1)}, bf16[400,768]{1,0:T(8,128)(2,1)S(1)}, u32[]{:S(2)}, u32[]{:S(2)}) %collective-permute-start.12) | collective-permute-done | bytes 614432 | tf_op jit(solution)/shard_map/ppermute | solution.py:787
  75.0 13.7 %shard_map.531 = (bf16[256,768]{1,0:T(8,128)(2,1)}, bf16[256,768]{1,0:T(8,128)(2,1)}, f32[256,128]{1,0:T(8,128)}, bf16[256,128]{1,0:T(8,128)(2,1)}, bf16[256,128...) custom-call(s32[3]{0:T(128)} %pad_add_fusion.refs_0_, ...), custom_call_target="tpu_custom_call" | custom-call | flops 23000000512 | bytes 1 | tf_op jit(solution)/shard_map/pallas_call | solution.py:115
  93.7 14.6 %shard_map.532 = (f32[256,768]{1,0:T(8,128)S(1)}, bf16[4,256,192]{2,1,0:T(8,128)(2,1)S(1)}, f32[40,128]{1,0:T(8,128)S(1)}, f32[4,8,128]{2,1,0:T(8,128)S(1)}, bf1...) custom-call(s32[3]{0:T(128)S(1)} %copy-done.29, s32[2]{0:T(128)S(1)} %copy-done.37, ...), custom_call_target="tpu_custom_call" | custom-call | flops 1 | bytes 1 | tf_op jit(solution)/shard_map/pallas_call | solution.py:115
  108.5 4.7 %collective-permute-done.24 = bf16[2,768,768]{2,1,0:T(8,128)(2,1)} collective-permute-done((bf16[2,768,768]{2,1,0:T(8,128)(2,1)}, bf16[2,768,768]{2,1,0:T(8,128)(2,1)}, u32[]{:S(2)}, u32[]{:S(2)}) %collective-permute-start.24) | collective-permute-done | bytes 2359328 | tf_op jit(solution)/shard_map/ppermute | solution.py:787
  113.3 2.9 add_convert_fusion.2.refs_11__0_
  118.5 13.6 %shard_map.533 = (f32[256,768]{1,0:T(8,128)}, f32[16,128]{1,0:T(8,128)}, f32[4,256,192]{2,1,0:T(8,128)}, bf16[4,256,384]{2,1,0:T(8,128)(2,1)}, bf16[4,256,384]{2...) custom-call(s32[3]{0:T(128)} %pad_add_fusion.refs_0_, ...), custom_call_target="tpu_custom_call" | custom-call | flops 23000000512 | bytes 1 | tf_op jit(solution)/shard_map/pallas_call | solution.py:115
  132.3 16.9 %shard_map.534 = (f32[8,128]{1,0:T(8,128)S(1)}, f32[8,128]{1,0:T(8,128)S(1)}, f32[768,128]{1,0:T(8,128)S(1)}, f32[4,8,128]{2,1,0:T(8,128)S(1)}, bf16[2,768,768]{...) custom-call(s32[3]{0:T(128)S(1)} %copy-done.30, ...), custom_call_target="tpu_custom_call" | custom-call | flops 1 | bytes 1 | tf_op jit(solution)/shard_map/pallas_call | solution.py:115
  154.4 3.8 %add_convert_fusion.refs_5__1_ = bf16[2,768,768]{2,1,0:T(8,128)(2,1)} fusion(bf16[2,768,768]{2,1,0:T(8,128)(2,1)} %collective-permute-done.29, bf16[2,768,768]{2,1,0:T(8,128)(2,1)S(1)} %copy-done.56), kind=kLoop, calls=%fused_computation | loop fusion | flops 4718592 | bytes 7077888 | tf_op jit(solution)/shard_map/convert_element_type | solution.py:830
  160.6 3.5 %shard_map.536 = (f32[3,512,128]{2,1,0:T(8,128)S(1)}, f32[3,16,8,128]{3,2,1,0:T(8,128)S(1)}, f32[3,16,128]{2,1,0:T(8,128)S(1)}, f32[8,128]{1,0:T(8,128)S(1)}) custom-call(s32[3]{0:T(128)S(1)} %copy-done.30, bf16[256,192]{1,0:T(8,128)(2,1)S(1)} %get-tuple-element.253.refs_1__0_, bf16[256,192]{1,0:T(8,128)(2,1)S(1)} %collective-permute-done.25.refs_1__1_, ...), custom_call_target="tpu_custom_call" | custom-call | flops 69000003584 | bytes 1 | tf_op jit(solution)/shard_map/pallas_call | solution.py:115
  168.0 3.6 %collective-permute-done.34 = bf16[1,384,768]{2,1,0:T(8,128)(2,1)S(1)} collective-permute-done((bf16[1,384,768]{2,1,0:T(8,128)(2,1)S(1)}, bf16[1,384,768]{2,1,0:T(8,128)(2,1)S(1)}, u32[]{:S(2)}, u32[]{:S(2)}) %collective-permute-start.34) | collective-permute-done | bytes 589856 | tf_op jit(solution)/shard_map/ppermute | solution.py:787
  174.0 6.5 %collective-permute-done.32.refs_0__0_.refs_8__1_ = f32[3,16,128]{2,1,0:T(8,128)S(1)} collective-permute-done((f32[3,16,128]{2,1,0:T(8,128)S(1)}, f32[3,16,128]{2,1,0:T(8,128)S(1)}, u32[]{:S(2)}, u32[]{:S(2)}) %collective-permute-start.32) | collective-permute-done | bytes 24608 | tf_op jit(solution)/shard_map/ppermute | solution.py:787
  180.7 2.7 collective-permute-start.36
  183.7 12.5 %collective-permute-done.33.refs_0__0_.refs_8__2_ = f32[3,16,128]{2,1,0:T(8,128)S(1)} collective-permute-done((f32[3,16,128]{2,1,0:T(8,128)S(1)}, f32[3,16,128]{2,1,0:T(8,128)S(1)}, u32[]{:S(2)}, u32[]{:S(2)}) %collective-permute-start.33) | collective-permute-done | bytes 24608 | tf_op jit(solution)/shard_map/ppermute | solution.py:787
  199.8 11.5 %shard_map.540 = (f32[3,512,128]{2,1,0:T(8,128)S(1)}, f32[2,40,128]{2,1,0:T(8,128)S(1)}, f32[8,128]{1,0:T(8,128)S(1)}) custom-call(s32[3]{0:T(128)S(1)} %copy-done.30, bf16[2,512,192]{2,1,0:T(8,128)(2,1)S(1)} %copy-done.13, f32[3,512,128]{2,1,0:T(8,128)S(1)} %get-tuple-element.268.refs_2_, f32[16,192]{1,0:T(8,128)S(1)} %bitcast.79, f32[16,192]{1,0:T(8,128)S(1)} %bitcast.74, ...), custom_call_target="tpu_custom_call" | custom-call | flops 17250000896 | bytes 1 | tf_op jit(solution)/shard_map/pallas_call | solution.py:115
  217.5 10.6 %collective-permute-done.40 = bf16[192,768]{1,0:T(8,128)(2,1)S(1)} collective-permute-done((bf16[192,768]{1,0:T(8,128)(2,1)S(1)}, bf16[192,768]{1,0:T(8,128)(2,1)S(1)}, u32[]{:S(2)}, u32[]{:S(2)}) %collective-permute-start.40) | collective-permute-done | bytes 294944 | tf_op jit(solution)/shard_map/ppermute | solution.py:787
  228.5 3.2 %collective-permute-done.46 = bf16[192,768]{1,0:T(8,128)(2,1)S(1)} collective-permute-done((bf16[192,768]{1,0:T(8,128)(2,1)S(1)}, bf16[192,768]{1,0:T(8,128)(2,1)S(1)}, u32[]{:S(2)}, u32[]{:S(2)}) %collective-permute-start.46) | collective-permute-done | bytes 294944 | tf_op jit(solution)/shard_map/ppermute | solution.py:787
  231.8 3.1 %collective-permute-start.47 = (bf16[192,768]{1,0:T(8,128)(2,1)S(1)}, bf16[192,768]{1,0:T(8,128)(2,1)S(1)}, u32[]{:S(2)}, u32[]{:S(2)}) collective-permute-start(bf16[192,768]{1,0:T(8,128)(2,1)S(1)} %add_convert_fusion.9), channel_id=1, source_target_pairs={{0,16},{4,20},{8,24},{12,28},{16,0},{20,4},{24,8},{28,12},{1,17},{... | collective-permute-start | bytes 884744 | tf_op jit(solution)/shard_map/ppermute | solution.py:787
  236.6 13.0 %collective-permute-done.41 = bf16[192,768]{1,0:T(8,128)(2,1)S(1)} collective-permute-done((bf16[192,768]{1,0:T(8,128)(2,1)S(1)}, bf16[192,768]{1,0:T(8,128)(2,1)S(1)}, u32[]{:S(2)}, u32[]{:S(2)}) %collective-permute-start.41) | collective-permute-done | bytes 294944 | tf_op jit(solution)/shard_map/ppermute | solution.py:787
  249.7 3.0 collective-permute-done.47
  258.2 4.0 %collective-permute-done.48 = bf16[192,768]{1,0:T(8,128)(2,1)S(1)} collective-permute-done((bf16[192,768]{1,0:T(8,128)(2,1)S(1)}, bf16[192,768]{1,0:T(8,128)(2,1)S(1)}, u32[]{:S(2)}, u32[]{:S(2)}) %collective-permute-start.48) | collective-permute-done | bytes 294944 | tf_op jit(solution)/shard_map/ppermute | solution.py:787
  263.3 4.2 %collective-permute-done.53 = bf16[1440,128]{1,0:T(8,128)(2,1)S(1)} collective-permute-done((bf16[1440,128]{1,0:T(8,128)(2,1)S(1)}, bf16[1440,128]{1,0:T(8,128)(2,1)S(1)}, u32[]{:S(2)}, u32[]{:S(2)}) %collective-permute-start.53) | collective-permute-done | bytes 368672 | tf_op jit(solution)/shard_map/ppermute | solution.py:787
  275.6 3.3 %collective-permute-done.54 = bf16[1440,128]{1,0:T(8,128)(2,1)} collective-permute-done((bf16[1440,128]{1,0:T(8,128)(2,1)}, bf16[1440,128]{1,0:T(8,128)(2,1)}, u32[]{:S(2)}, u32[]{:S(2)}) %collective-permute-start.54) | collective-permute-done | bytes 368672 | tf_op jit(solution)/shard_map/ppermute | solution.py:787
  284.3 8.2 %collective-permute-done.56 = bf16[384,768]{1,0:T(8,128)(2,1)} collective-permute-done((bf16[384,768]{1,0:T(8,128)(2,1)S(1)}, bf16[384,768]{1,0:T(8,128)(2,1)}, u32[]{:S(2)}, u32[]{:S(2)}) %collective-permute-start.56) | collective-permute-done | bytes 589856 | tf_op jit(solution)/shard_map/ppermute | solution.py:787
  (356 shorter events, 103.0 us)
Async XLA Ops:
  4.7 17.1 %collective-permute-start.1 = (bf16[400,768]{1,0:T(8,128)(2,1)}, bf16[400,768]{1,0:T(8,128)(2,1)S(1)}, u32[]{:S(2)}, u32[]{:S(2)}) collective-permute-start(bf16[400,768]{1,0:T(8,128)(2,1)} %get-tuple-element.179.refs_4__0_), channel_id=1, source_target_pairs={{0,2},{1,3},{2,0},{3,1},{4,6},{5,7},{6,4},{7,5},{8,10},{9,11},{10,... | collective-permute-start | bytes 1843208 | tf_op jit(solution)/shard_map/ppermute | solution.py:787
  21.8 23.6 %collective-permute-start.11 = (bf16[400,768]{1,0:T(8,128)(2,1)S(1)}, bf16[400,768]{1,0:T(8,128)(2,1)S(1)}, u32[]{:S(2)}, u32[]{:S(2)}) collective-permute-start(bf16[400,768]{1,0:T(8,128)(2,1)S(1)} %collective-permute-done.1.refs_3__2__0_.refs_1__2__0_), channel_id=1, source_target_pairs={{0,4},{4,0},{8,12},{12,8},{16,20},{20,16},{24,28},{28,24},{1,5},{5... | collective-permute-start | bytes 1843208 | tf_op jit(solution)/shard_map/ppermute | solution.py:787
  23.5 19.9 %collective-permute-start.2 = (bf16[384,768]{1,0:T(8,128)(2,1)}, bf16[384,768]{1,0:T(8,128)(2,1)}, u32[]{:S(2)}, u32[]{:S(2)}) collective-permute-start(bf16[384,768]{1,0:T(8,128)(2,1)} %get-tuple-element.191), channel_id=1, source_target_pairs={{0,2},{1,3},{2,0},{3,1},{4,6},{5,7},{6,4},{7,5},{8,10},{9,11},{10,... | collective-permute-start | bytes 1769480 | tf_op jit(solution)/shard_map/ppermute | solution.py:787
  40.9 26.1 %collective-permute-start = (bf16[800,768]{1,0:T(8,128)(2,1)}, bf16[800,768]{1,0:T(8,128)(2,1)S(1)}, u32[]{:S(2)}, u32[]{:S(2)}) collective-permute-start(bf16[800,768]{1,0:T(8,128)(2,1)} %get-tuple-element.178.refs_3__0__0_.refs_1__0__0_), channel_id=1, source_target_pairs={{0,1},{1,0},{2,3},{3,2},{4,5},{5,4},{6,7},{7,6},{8,9},{9,8},{10,11... | collective-permute-start | bytes 3686408 | tf_op jit(solution)/shard_map/ppermute | solution.py:787
  43.4 15.5 %collective-permute-start.3 = (bf16[384,768]{1,0:T(8,128)(2,1)}, bf16[384,768]{1,0:T(8,128)(2,1)}, u32[]{:S(2)}, u32[]{:S(2)}) collective-permute-start(bf16[384,768]{1,0:T(8,128)(2,1)} %get-tuple-element.192), channel_id=1, source_target_pairs={{0,2},{1,3},{2,0},{3,1},{4,6},{5,7},{6,4},{7,5},{8,10},{9,11},{10,... | collective-permute-start | bytes 1769480 | tf_op jit(solution)/shard_map/ppermute | solution.py:787
  44.9 13.6 %collective-permute-start.4 = (bf16[384,768]{1,0:T(8,128)(2,1)}, bf16[384,768]{1,0:T(8,128)(2,1)S(1)}, u32[]{:S(2)}, u32[]{:S(2)}) collective-permute-start(bf16[384,768]{1,0:T(8,128)(2,1)} %collective-permute-done.2.refs_8__0_.refs_4__2__0_.refs_1__2__0_), channel_id=1, source_target_pairs={{0,4},{4,0},{8,12},{12,8},{16,20},{20,16},{24,28},{28,24},{1,5},{5... | collective-permute-start | bytes 1769480 | tf_op jit(solution)/shard_map/ppermute | solution.py:787
  70.5 18.3 %collective-permute-start.20 = (bf16[768,768]{1,0:T(8,128)(2,1)S(1)}, bf16[768,768]{1,0:T(8,128)(2,1)}, u32[]{:S(2)}, u32[]{:S(2)}) collective-permute-start(bf16[768,768]{1,0:T(8,128)(2,1)S(1)} %copy-done), channel_id=1, source_target_pairs={{0,1},{1,0},{2,3},{3,2},{4,5},{5,4},{6,7},{7,6},{8,9},{9,8},{10,11... | collective-permute-start | bytes 3538952 | tf_op jit(solution)/shard_map/ppermute | solution.py:787
  70.8 18.0 %collective-permute-start.21 = (bf16[384,768]{1,0:T(8,128)(2,1)}, bf16[384,768]{1,0:T(8,128)(2,1)S(1)}, u32[]{:S(2)}, u32[]{:S(2)}) collective-permute-start(bf16[384,768]{1,0:T(8,128)(2,1)} %collective-permute-done.3.refs_2__2__0_), channel_id=1, source_target_pairs={{0,4},{4,0},{8,12},{12,8},{16,20},{20,16},{24,28},{28,24},{1,5},{5... | collective-permute-start | bytes 1769480 | tf_op jit(solution)/shard_map/ppermute | solution.py:787
  72.3 16.6 %collective-permute-start.22 = (bf16[384,768]{1,0:T(8,128)(2,1)}, bf16[384,768]{1,0:T(8,128)(2,1)}, u32[]{:S(2)}, u32[]{:S(2)}) collective-permute-start(bf16[384,768]{1,0:T(8,128)(2,1)} %collective-permute-done.3.refs_2__2__0_), channel_id=1, source_target_pairs={{0,1},{1,0},{2,3},{3,2},{4,5},{5,4},{6,7},{7,6},{8,9},{9,8},{10,11... | collective-permute-start | bytes 1769480 | tf_op jit(solution)/shard_map/ppermute | solution.py:787
  117.7 32.9 %collective-permute-start.30 = (bf16[2,384,768]{2,1,0:T(8,128)(2,1)S(1)}, bf16[2,384,768]{2,1,0:T(8,128)(2,1)}, u32[]{:S(2)}, u32[]{:S(2)}) collective-permute-start(bf16[2,384,768]{2,1,0:T(8,128)(2,1)S(1)} %constant_dynamic-slice_fusion.5), channel_id=1, source_target_pairs={{0,4},{4,0},{8,12},{12,8},{16,20},{20,16},{24,28},{28,24},{1,5},{5... | collective-permute-start | bytes 3538952 | tf_op jit(solution)/shard_map/ppermute | solution.py:787
  132.0 21.6 %collective-permute-start.28 = (bf16[2,768,768]{2,1,0:T(8,128)(2,1)}, bf16[2,768,768]{2,1,0:T(8,128)(2,1)}, u32[]{:S(2)}, u32[]{:S(2)}) collective-permute-start(bf16[2,768,768]{2,1,0:T(8,128)(2,1)} %get-tuple-element.259), channel_id=1, source_target_pairs={{0,1},{1,0},{2,3},{3,2},{4,5},{5,4},{6,7},{7,6},{8,9},{9,8},{10,11... | collective-permute-start | bytes 7077896 | tf_op jit(solution)/shard_map/ppermute | solution.py:787
  153.7 18.0 %collective-permute-start.34 = (bf16[1,384,768]{2,1,0:T(8,128)(2,1)S(1)}, bf16[1,384,768]{2,1,0:T(8,128)(2,1)S(1)}, u32[]{:S(2)}, u32[]{:S(2)}) collective-permute-start(bf16[1,384,768]{2,1,0:T(8,128)(2,1)S(1)} %slice.261), channel_id=1, source_target_pairs={{0,2},{1,3},{2,0},{3,1},{4,6},{5,7},{6,4},{7,5},{8,10},{9,11},{10,... | collective-permute-start | bytes 1769480 | tf_op jit(solution)/shard_map/ppermute | solution.py:787
  165.7 31.4 %collective-permute-start.38 = (bf16[1,768,768]{2,1,0:T(8,128)(2,1)S(1)}, bf16[1,768,768]{2,1,0:T(8,128)(2,1)S(1)}, u32[]{:S(2)}, u32[]{:S(2)}) collective-permute-start(bf16[1,768,768]{2,1,0:T(8,128)(2,1)S(1)} %slice.263), channel_id=1, source_target_pairs={{0,2},{1,3},{2,0},{3,1},{4,6},{5,7},{6,4},{7,5},{8,10},{9,11},{10,... | collective-permute-start | bytes 3538952 | tf_op jit(solution)/shard_map/ppermute | solution.py:787
  167.1 30.3 %collective-permute-start.37 = (bf16[2,384,768]{2,1,0:T(8,128)(2,1)S(1)}, bf16[2,384,768]{2,1,0:T(8,128)(2,1)S(1)}, u32[]{:S(2)}, u32[]{:S(2)}) collective-permute-start(bf16[2,384,768]{2,1,0:T(8,128)(2,1)S(1)} %constant_dynamic-slice_fusion.4), channel_id=1, source_target_pairs={{0,4},{4,0},{8,12},{12,8},{16,20},{20,16},{24,28},{28,24},{1,5},{5... | collective-permute-start | bytes 3538952 | tf_op jit(solution)/shard_map/ppermute | solution.py:787
  180.7 15.6 %collective-permute-start.36 = (bf16[192,768]{1,0:T(8,128)(2,1)S(1)}, bf16[192,768]{1,0:T(8,128)(2,1)S(1)}, u32[]{:S(2)}, u32[]{:S(2)}) collective-permute-start(bf16[192,768]{1,0:T(8,128)(2,1)S(1)} %fusion.2), channel_id=1, source_target_pairs={{0,16},{4,20},{8,24},{12,28},{16,0},{20,4},{24,8},{28,12},{1,17},{... | collective-permute-start | bytes 884744 | tf_op jit(solution)/shard_map/ppermute | solution.py:787
  183.3 12.9 %collective-permute-start.33 = (f32[3,16,128]{2,1,0:T(8,128)S(1)}, f32[3,16,128]{2,1,0:T(8,128)S(1)}, u32[]{:S(2)}, u32[]{:S(2)}) collective-permute-start(f32[3,16,128]{2,1,0:T(8,128)S(1)} %add_select_fusion), channel_id=1, source_target_pairs={{0,16},{4,20},{8,24},{12,28},{16,0},{20,4},{24,8},{28,12},{1,17},{... | collective-permute-start | bytes 73736 | tf_op jit(solution)/shard_map/ppermute | solution.py:787
  196.3 16.8 %collective-permute-start.50 = (bf16[192,768]{1,0:T(8,128)(2,1)S(1)}, bf16[192,768]{1,0:T(8,128)(2,1)S(1)}, u32[]{:S(2)}, u32[]{:S(2)}) collective-permute-start(bf16[192,768]{1,0:T(8,128)(2,1)S(1)} %add_convert_fusion.11.refs_10__0_), channel_id=1, source_target_pairs={{0,8},{4,12},{8,0},{12,4},{16,24},{20,28},{24,16},{28,20},{1,9},{5... | collective-permute-start | bytes 884744 | tf_op jit(solution)/shard_map/ppermute | solution.py:787
  197.8 15.0 %collective-permute-start.39 = (bf16[1,384,768]{2,1,0:T(8,128)(2,1)S(1)}, bf16[1,384,768]{2,1,0:T(8,128)(2,1)S(1)}, u32[]{:S(2)}, u32[]{:S(2)}) collective-permute-start(bf16[1,384,768]{2,1,0:T(8,128)(2,1)S(1)} %slice.265), channel_id=1, source_target_pairs={{0,2},{1,3},{2,0},{3,1},{4,6},{5,7},{6,4},{7,5},{8,10},{9,11},{10,... | collective-permute-start | bytes 1769480 | tf_op jit(solution)/shard_map/ppermute | solution.py:787
  198.4 14.8 %collective-permute-start.45 = (bf16[384,768]{1,0:T(8,128)(2,1)S(1)}, bf16[384,768]{1,0:T(8,128)(2,1)S(1)}, u32[]{:S(2)}, u32[]{:S(2)}) collective-permute-start(bf16[384,768]{1,0:T(8,128)(2,1)S(1)} %dynamic-slice_bitcast_fusion), channel_id=1, source_target_pairs={{0,4},{4,0},{8,12},{12,8},{16,20},{20,16},{24,28},{28,24},{1,5},{5... | collective-permute-start | bytes 1769480 | tf_op jit(solution)/shard_map/ppermute | solution.py:787
  213.3 39.7 %collective-permute-start.58 = (bf16[384,768]{1,0:T(8,128)(2,1)S(1)}, bf16[384,768]{1,0:T(8,128)(2,1)S(1)}, u32[]{:S(2)}, u32[]{:S(2)}) collective-permute-start(bf16[384,768]{1,0:T(8,128)(2,1)S(1)} %maximum_select_fusion.5), channel_id=1, source_target_pairs={{0,4},{4,0},{8,12},{12,8},{16,20},{20,16},{24,28},{28,24},{1,5},{5... | collective-permute-start | bytes 1769480 | tf_op jit(solution)/shard_map/ppermute | solution.py:787
  215.0 13.2 %collective-permute-start.40 = (bf16[192,768]{1,0:T(8,128)(2,1)S(1)}, bf16[192,768]{1,0:T(8,128)(2,1)S(1)}, u32[]{:S(2)}, u32[]{:S(2)}) collective-permute-start(bf16[192,768]{1,0:T(8,128)(2,1)S(1)} %dynamic-slice_bitcast_fusion.1), channel_id=1, source_target_pairs={{0,8},{4,12},{8,0},{12,4},{16,24},{20,28},{24,16},{28,20},{1,9},{5... | collective-permute-start | bytes 884744 | tf_op jit(solution)/shard_map/ppermute | solution.py:787
  216.2 15.5 %collective-permute-start.46 = (bf16[192,768]{1,0:T(8,128)(2,1)S(1)}, bf16[192,768]{1,0:T(8,128)(2,1)S(1)}, u32[]{:S(2)}, u32[]{:S(2)}) collective-permute-start(bf16[192,768]{1,0:T(8,128)(2,1)S(1)} %constant_dynamic-slice_fusion.3), channel_id=1, source_target_pairs={{0,8},{4,12},{8,0},{12,4},{16,24},{20,28},{24,16},{28,20},{1,9},{5... | collective-permute-start | bytes 884744 | tf_op jit(solution)/shard_map/ppermute | solution.py:787
  217.4 17.4 %collective-permute-start.51 = (bf16[1280,128]{1,0:T(8,128)(2,1)S(1)}, bf16[1280,128]{1,0:T(8,128)(2,1)S(1)}, u32[]{:S(2)}, u32[]{:S(2)}) collective-permute-start(bf16[1280,128]{1,0:T(8,128)(2,1)S(1)} %pad_maximum_fusion.3), channel_id=1, source_target_pairs={{0,1},{1,0},{2,3},{3,2},{4,5},{5,4},{6,7},{7,6},{8,9},{9,8},{10,11... | collective-permute-start | bytes 983048 | tf_op jit(solution)/shard_map/ppermute | solution.py:787
  228.2 21.3 %collective-permute-start.41 = (bf16[192,768]{1,0:T(8,128)(2,1)S(1)}, bf16[192,768]{1,0:T(8,128)(2,1)S(1)}, u32[]{:S(2)}, u32[]{:S(2)}) collective-permute-start(bf16[192,768]{1,0:T(8,128)(2,1)S(1)} %fusion.1), channel_id=1, source_target_pairs={{0,16},{4,20},{8,24},{12,28},{16,0},{20,4},{24,8},{28,12},{1,17},{... | collective-permute-start | bytes 884744 | tf_op jit(solution)/shard_map/ppermute | solution.py:787
  231.8 21.0 %collective-permute-start.47 = (bf16[192,768]{1,0:T(8,128)(2,1)S(1)}, bf16[192,768]{1,0:T(8,128)(2,1)S(1)}, u32[]{:S(2)}, u32[]{:S(2)}) collective-permute-start(bf16[192,768]{1,0:T(8,128)(2,1)S(1)} %add_convert_fusion.9), channel_id=1, source_target_pairs={{0,16},{4,20},{8,24},{12,28},{16,0},{20,4},{24,8},{28,12},{1,17},{... | collective-permute-start | bytes 884744 | tf_op jit(solution)/shard_map/ppermute | solution.py:787
  235.0 21.2 %collective-permute-start.52 = (bf16[1280,128]{1,0:T(8,128)(2,1)S(1)}, bf16[1280,128]{1,0:T(8,128)(2,1)S(1)}, u32[]{:S(2)}, u32[]{:S(2)}) collective-permute-start(bf16[1280,128]{1,0:T(8,128)(2,1)S(1)} %pad_maximum_fusion.4), channel_id=1, source_target_pairs={{0,2},{1,3},{2,0},{3,1},{4,6},{5,7},{6,4},{7,5},{8,10},{9,11},{10,... | collective-permute-start | bytes 983048 | tf_op jit(solution)/shard_map/ppermute | solution.py:787
  249.6 12.8 %collective-permute-start.49 = (bf16[192,768]{1,0:T(8,128)(2,1)S(1)}, bf16[192,768]{1,0:T(8,128)(2,1)S(1)}, u32[]{:S(2)}, u32[]{:S(2)}) collective-permute-start(bf16[192,768]{1,0:T(8,128)(2,1)S(1)} %add_convert_fusion.10), channel_id=1, source_target_pairs={{0,8},{4,12},{8,0},{12,4},{16,24},{20,28},{24,16},{28,20},{1,9},{5... | collective-permute-start | bytes 884744 | tf_op jit(solution)/shard_map/ppermute | solution.py:787
  252.9 16.2 %collective-permute-start.42 = (bf16[256,384]{1,0:T(8,128)(2,1)S(1)}, bf16[256,384]{1,0:T(8,128)(2,1)S(1)}, u32[]{:S(2)}, u32[]{:S(2)}) collective-permute-start(bf16[256,384]{1,0:T(8,128)(2,1)S(1)} %get-tuple-element.293), channel_id=1, source_target_pairs={{0,1},{1,0},{2,3},{3,2},{4,5},{5,4},{6,7},{7,6},{8,9},{9,8},{10,11... | collective-permute-start | bytes 589832 | tf_op jit(solution)/shard_map/ppermute | solution.py:787
  253.0 18.4 %collective-permute-start.43 = (bf16[256,384]{1,0:T(8,128)(2,1)S(1)}, bf16[256,384]{1,0:T(8,128)(2,1)S(1)}, u32[]{:S(2)}, u32[]{:S(2)}) collective-permute-start(bf16[256,384]{1,0:T(8,128)(2,1)S(1)} %get-tuple-element.294), channel_id=1, source_target_pairs={{0,2},{1,3},{2,0},{3,1},{4,6},{5,7},{6,4},{7,5},{8,10},{9,11},{10,... | collective-permute-start | bytes 589832 | tf_op jit(solution)/shard_map/ppermute | solution.py:787
  262.4 18.1 %collective-permute-start.57 = (bf16[384,768]{1,0:T(8,128)(2,1)S(1)}, bf16[384,768]{1,0:T(8,128)(2,1)}, u32[]{:S(2)}, u32[]{:S(2)}) collective-permute-start(bf16[384,768]{1,0:T(8,128)(2,1)S(1)} %maximum_select_fusion.3.refs_4__0_), channel_id=1, source_target_pairs={{0,4},{4,0},{8,12},{12,8},{16,20},{20,16},{24,28},{28,24},{1,5},{5... | collective-permute-start | bytes 1769480 | tf_op jit(solution)/shard_map/ppermute | solution.py:787
  267.5 25.0 %collective-permute-start.56 = (bf16[384,768]{1,0:T(8,128)(2,1)S(1)}, bf16[384,768]{1,0:T(8,128)(2,1)}, u32[]{:S(2)}, u32[]{:S(2)}) collective-permute-start(bf16[384,768]{1,0:T(8,128)(2,1)S(1)} %maximum_select_fusion.4.refs_4__1_), channel_id=1, source_target_pairs={{0,4},{4,0},{8,12},{12,8},{16,20},{20,16},{24,28},{28,24},{1,5},{5... | collective-permute-start | bytes 1769480 | tf_op jit(solution)/shard_map/ppermute | solution.py:787
  280.0 17.1 %collective-permute-start.55 = (bf16[1440,128]{1,0:T(8,128)(2,1)S(1)}, bf16[1440,128]{1,0:T(8,128)(2,1)S(1)}, u32[]{:S(2)}, u32[]{:S(2)}) collective-permute-start(bf16[1440,128]{1,0:T(8,128)(2,1)S(1)} %pad_maximum_fusion.2), channel_id=1, source_target_pairs={{0,16},{4,20},{8,24},{12,28},{16,0},{20,4},{24,8},{28,12},{1,17},{... | collective-permute-start | bytes 1105928 | tf_op jit(solution)/shard_map/ppermute | solution.py:787
  (104 other events, 876.5 us)
